TPU v7x, 32 devices: a whole 2x2x4 slice. The times are simulated.
32 devices in a mesh: section: 4 (over x, core), dp: 8 (over z, y).
Axes of the slice: x: 2, y: 2, z: 4, core: 2. Of those that a mesh axis runs over, the one named last changes fastest.
Arguments:
- inputs: bfloat16 [4, 128, 64, 512], P(None, 'dp'), may hold values from -6 to 6
- cotangent: bfloat16 [4, 128, 64, 512], P(None, 'dp'), may hold values from -6 to 6
- segments: int32 [4, 128, 64], P(None, 'dp'), may hold values from 0 to 1, as said below
- observed: int32 [4, 128, 64], P(None, 'dp'), may hold values from 0 to 1, as said below
- q_weight: bfloat16 [2, 512, 384], P(None, 'dp'), may hold values from -0.0625 to 0.0625
- k_weight: bfloat16 [2, 512, 384], P(None, 'dp'), may hold values from -0.25 to 0.25
- v_weight: bfloat16 [2, 512, 384], P(None, 'dp'), may hold values from -0.25 to 0.25
- o_weight: bfloat16 [2, 384, 512], P(None, 'dp'), may hold values from -0.875 to 0.875
- gate_weight: bfloat16 [2, 512, 1024], P(None, 'dp'), may hold values from -0.25 to 0.25
- up_weight: bfloat16 [2, 512, 1024], P(None, 'dp'), may hold values from -0.25 to 0.25
- down_weight: bfloat16 [2, 1024, 512], P(None, 'dp'), may hold values from -0.25 to 0.25
- gains: bfloat16 [2, 2, 512], P(None, None, 'dp'), may hold values from 0.5 to 1.5
- position_table: bfloat16 [32, 6], replicated, may hold values from -4 to 4
Outputs:
- section_outputs: bfloat16 [4, 4, 128, 64, 512], P('section', None, 'dp')
- section_grads: bfloat16 [4, 4, 128, 64, 512], P('section', None, 'dp')
- q_grad: float32 [2, 512, 384], P(None, 'dp')
- k_grad: float32 [2, 512, 384], P(None, 'dp')
- v_grad: float32 [2, 512, 384], P(None, 'dp')
- o_grad: float32 [2, 384, 512], P(None, 'dp')
- gate_grad: float32 [2, 512, 1024], P(None, 'dp')
- up_grad: float32 [2, 512, 1024], P(None, 'dp')
- down_grad: float32 [2, 1024, 512], P(None, 'dp')
- gains_grad: float32 [2, 2, 512], P(None, None, 'dp')
- table_grad: float32 [32, 6], replicated
Inputs may be any that keep to these rules, and one draw needn't show every extreme that they name: `segments`: each row holds either one series of 64 patches, all numbered 0, or two series of 32 patches, numbered 0 then 1. Patches 0 and 32 of every row are observed.
All inputs are finite; a program needn't handle non-finite values.
Results may differ from a plain program's by a relative error of at most 0.03.
Values may be sent and summed in bfloat16 or wider, within the bound.
No kernel may reach another device: no remote copies, remote signals or barrier semaphores. Data moves between devices by JAX's collectives and lax.ppermute only.
A program may use at most 256 MiB of HBM per device.

v0:
```python
from functools import partial

import jax
import jax.numpy as jnp
from jax import lax
from jax.sharding import PartitionSpec as P

eps_norm = 1e-06
limits = (12, 16, 23, 32, 46, 64, 91)
masked = -1e30
highest = lax.Precision.HIGHEST


def shortened(value):

    def short(part):
        return part.astype(jnp.bfloat16) if part.dtype == jnp.float32 else part

    return jax.tree.map(short, value)


def shifted(value, axis, by):
    peers = lax.axis_size(axis)
    pairs = [(i, i + by) for i in range(peers) if 0 <= i + by < peers]
    return lax.ppermute(value, axis, pairs)


def bucket_onehot(seq_count, bucket_count):
    position = jnp.arange(seq_count, dtype=jnp.int32)
    offset = position[None, :] - position[:, None]
    distance = jnp.abs(offset)
    far_bucket = jnp.full(distance.shape, 8, jnp.int32)
    for threshold in limits:
        far_bucket = far_bucket + (distance >= threshold).astype(jnp.int32)
    bucket = jnp.where(distance < 8, distance, jnp.minimum(far_bucket, 15)) + 16 * (
        offset > 0
    ).astype(jnp.int32)
    return (bucket[:, :, None] == jnp.arange(bucket_count, dtype=jnp.int32)[None, None, :]).astype(
        jnp.float32
    )


def normalize(values):
    return values * lax.rsqrt(jnp.mean(values * values, axis=-1, keepdims=True) + eps_norm)


def normed_gain(values, gain_row):
    return normalize(values) * gain_row


def gated(gate_act, up_act):
    return jax.nn.gelu(gate_act, approximate=True) * up_act


def project(operand, matrix):
    return jnp.einsum("rsd,de->rse", operand, matrix, preferred_element_type=jnp.float32)


def project_back(operand, matrix):
    return jnp.einsum("rse,de->rsd", operand, matrix, preferred_element_type=jnp.float32)


def outer_sum(operand, other):
    return jnp.einsum("rsd,rse->de", operand, other, preferred_element_type=jnp.float32)


def split_heads(values, head_count):
    return values.reshape(values.shape[0], values.shape[1], head_count, -1)


def attention_scores(query_heads, key_heads, position_bias, allowed):
    scores = (
        jnp.einsum("rihd,rjhd->rhij", query_heads, key_heads, preferred_element_type=jnp.float32)
        + position_bias[None]
    )
    return jnp.where(allowed[:, None], scores, masked)


def store_slot(buffer, slot_index, new_value, active):
    previous = lax.dynamic_index_in_dim(buffer, slot_index, 0, keepdims=False)
    return lax.dynamic_update_index_in_dim(
        buffer, jnp.where(active, new_value, previous), slot_index, 0
    )


def pick_slot(buffer, slot_index):
    return lax.dynamic_index_in_dim(buffer, slot_index, 0, keepdims=False)


def attention_forward(stream_low, weights, position_bias, allowed):
    q_weight, k_weight, v_weight, o_weight, gain_row = weights
    row_count, seq_count, model_width = stream_low.shape
    head_count = position_bias.shape[0]
    stream = stream_low.astype(jnp.float32)
    attn_in = normed_gain(stream, gain_row).astype(jnp.bfloat16)
    query_low = project(attn_in, q_weight).astype(jnp.bfloat16)
    key_low = project(attn_in, k_weight).astype(jnp.bfloat16)
    value_low = project(attn_in, v_weight).astype(jnp.bfloat16)
    scores = attention_scores(
        split_heads(query_low, head_count), split_heads(key_low, head_count), position_bias, allowed
    )
    row_max = jnp.max(scores, axis=-1, keepdims=True)
    weights_raw = jnp.exp(scores - row_max)
    row_total = jnp.sum(weights_raw, axis=-1, keepdims=True)
    log_total = row_max + jnp.log(row_total)
    prob_low = (weights_raw / row_total).astype(jnp.bfloat16)
    attended = jnp.einsum(
        "rhij,rjhd->rihd",
        prob_low,
        split_heads(value_low, head_count),
        preferred_element_type=jnp.float32,
    )
    attended = attended.reshape(row_count, seq_count, -1).astype(jnp.bfloat16)
    layer_out = (stream + project(attended, o_weight)).astype(jnp.bfloat16)
    return (layer_out, (attn_in, query_low, key_low, value_low, log_total, attended))


def ffn_forward(stream_low, weights):
    gate_weight, up_weight, down_weight, gain_row = weights
    stream = stream_low.astype(jnp.float32)
    ffn_in = normed_gain(stream, gain_row).astype(jnp.bfloat16)
    gate_act = project(ffn_in, gate_weight)
    up_act = project(ffn_in, up_weight)
    hidden = gated(gate_act, up_act).astype(jnp.bfloat16)
    layer_out = (stream + project(hidden, down_weight)).astype(jnp.bfloat16)
    return (layer_out, (ffn_in, gate_act, up_act, hidden))


def attention_input_back(stream_low, saved_acts, grad_out, weights, position_bias, allowed):
    q_weight, k_weight, v_weight, o_weight, gain_row = weights
    attn_in, query_low, key_low, value_low, log_total, attended = saved_acts
    row_count, seq_count, model_width = grad_out.shape
    head_count = position_bias.shape[0]
    attended_grad = project_back(grad_out, o_weight).astype(jnp.bfloat16)
    query_heads = split_heads(query_low, head_count)
    key_heads = split_heads(key_low, head_count)
    value_heads = split_heads(value_low, head_count)
    scores = attention_scores(query_heads, key_heads, position_bias, allowed)
    prob_full = jnp.exp(scores - log_total)
    prob_low = prob_full.astype(jnp.bfloat16)
    grad_heads = split_heads(attended_grad, head_count)
    prob_grad = jnp.einsum(
        "rihd,rjhd->rhij", grad_heads, value_heads, preferred_element_type=jnp.float32
    )
    value_back = jnp.einsum(
        "rhij,rihd->rjhd", prob_low, grad_heads, preferred_element_type=jnp.float32
    )
    value_back = value_back.reshape(row_count, seq_count, -1).astype(jnp.bfloat16)
    score_grad = prob_full * (prob_grad - jnp.sum(prob_full * prob_grad, axis=-1, keepdims=True))
    score_grad = score_grad.astype(jnp.bfloat16)
    bias_grad = jnp.sum(score_grad.astype(jnp.float32), axis=0)
    query_back = jnp.einsum(
        "rhij,rjhd->rihd", score_grad, key_heads, preferred_element_type=jnp.float32
    )
    query_back = query_back.reshape(row_count, seq_count, -1).astype(jnp.bfloat16)
    key_back = jnp.einsum(
        "rhij,rihd->rjhd", score_grad, query_heads, preferred_element_type=jnp.float32
    )
    key_back = key_back.reshape(row_count, seq_count, -1).astype(jnp.bfloat16)
    attn_grad = (
        project_back(query_back, q_weight)
        + project_back(key_back, k_weight)
        + project_back(value_back, v_weight)
    )
    unused, pullback = jax.vjp(normed_gain, stream_low.astype(jnp.float32), gain_row)
    stream_grad, gain_term = pullback(attn_grad)
    input_grad = (stream_grad + grad_out.astype(jnp.float32)).astype(jnp.bfloat16)
    return (input_grad, (query_back, key_back, value_back), gain_term, bias_grad)


def ffn_input_back(stream_low, saved_acts, grad_out, weights):
    gate_weight, up_weight, down_weight, gain_row = weights
    ffn_in, gate_act, up_act, hidden = saved_acts
    hidden_grad = project_back(grad_out, down_weight)
    unused, pullback = jax.vjp(gated, gate_act, up_act)
    gate_back, up_back = pullback(hidden_grad)
    gate_back = gate_back.astype(jnp.bfloat16)
    up_back = up_back.astype(jnp.bfloat16)
    ffn_grad = project_back(gate_back, gate_weight) + project_back(up_back, up_weight)
    unused, pullback = jax.vjp(normed_gain, stream_low.astype(jnp.float32), gain_row)
    stream_grad, gain_term = pullback(ffn_grad)
    input_grad = (stream_grad + grad_out.astype(jnp.float32)).astype(jnp.bfloat16)
    return (input_grad, (gate_back, up_back), gain_term)


def attention_weight_terms(saved_acts, grad_out, back_parts):
    attn_in = saved_acts[0]
    attended = saved_acts[5]
    return (
        outer_sum(attn_in, back_parts[0]),
        outer_sum(attn_in, back_parts[1]),
        outer_sum(attn_in, back_parts[2]),
        outer_sum(attended, grad_out),
    )


def ffn_weight_terms(saved_acts, grad_out, back_parts):
    ffn_in = saved_acts[0]
    hidden = saved_acts[3]
    return (
        outer_sum(ffn_in, back_parts[3]),
        outer_sum(ffn_in, back_parts[4]),
        outer_sum(hidden, grad_out),
    )


def body(
    inputs,
    cotangent,
    segments,
    observed,
    q_weight,
    k_weight,
    v_weight,
    o_weight,
    gate_weight,
    up_weight,
    down_weight,
    gains,
    position_table,
):
    section_count = lax.axis_size("section")
    section_id = lax.axis_index("section")
    layer_id = section_id // 2
    branch_kind = section_id % 2
    micro_count, row_count, seq_count, model_width = inputs.shape
    layer_count = q_weight.shape[0]
    own_shards = tuple(
        (
            lax.dynamic_index_in_dim(matrix, layer_id, 0, keepdims=False)
            for matrix in (
                q_weight,
                k_weight,
                v_weight,
                o_weight,
                gate_weight,
                up_weight,
                down_weight,
                gains,
            )
        )
    )
    fetched = (
        lax.all_gather(own_shards[0], "dp", axis=0, tiled=True),
        lax.all_gather(own_shards[1], "dp", axis=0, tiled=True),
        lax.all_gather(own_shards[2], "dp", axis=0, tiled=True),
        lax.all_gather(own_shards[3], "dp", axis=0, tiled=True),
        lax.all_gather(own_shards[4], "dp", axis=0, tiled=True),
        lax.all_gather(own_shards[5], "dp", axis=0, tiled=True),
        lax.all_gather(own_shards[6], "dp", axis=0, tiled=True),
        lax.all_gather(own_shards[7], "dp", axis=1, tiled=True),
    )
    gain_pair = fetched[7].astype(jnp.float32)
    attention_weights = (fetched[0], fetched[1], fetched[2], fetched[3], gain_pair[0])
    ffn_weights = (fetched[4], fetched[5], fetched[6], gain_pair[1])
    bias_table = position_table.astype(jnp.float32)
    onehot = bucket_onehot(seq_count, bias_table.shape[0])
    position_bias = jnp.einsum("ijb,bh->hij", onehot, bias_table, precision=highest)
    head_count = bias_table.shape[1]
    inner_width = q_weight.shape[2]
    ffn_width = gate_weight.shape[2]
    allowed_all = (segments[:, :, :, None] == segments[:, :, None, :]) & (
        observed[:, :, None, :] == 1
    )
    tick_count = micro_count + section_count - 1
    layer_zero = jnp.zeros((row_count, seq_count, model_width), jnp.bfloat16)
    inner_zero = jnp.zeros((row_count, seq_count, inner_width), jnp.bfloat16)
    wide_zero = jnp.zeros((row_count, seq_count, ffn_width), jnp.bfloat16)
    wide_float = jnp.zeros((row_count, seq_count, ffn_width), jnp.float32)
    attn_blank = (
        layer_zero,
        inner_zero,
        inner_zero,
        inner_zero,
        jnp.zeros((row_count, head_count, seq_count, 1), jnp.float32),
        inner_zero,
    )
    ffn_blank = (layer_zero, wide_float, wide_float, wide_zero)
    back_blank = (inner_zero, inner_zero, inner_zero, wide_zero, wide_zero)
    zero_row = jnp.zeros((model_width,), jnp.float32)
    gain_zero = jnp.zeros((2, model_width), jnp.float32)
    bias_zero = jnp.zeros(position_bias.shape, jnp.float32)
    grad_zero = tuple((jnp.zeros(matrix.shape, jnp.float32) for matrix in fetched[:7]))

    def stacked(blank_set):
        return tuple(
            (
                jnp.zeros((micro_count,) + blank_part.shape, blank_part.dtype)
                for blank_part in blank_set
            )
        )

    def forward_tick(tick_index, loop_state):
        incoming, kept_in, kept_attn, kept_ffn, states_out = loop_state
        micro_index = tick_index - section_id
        active = (micro_index >= 0) & (micro_index < micro_count)
        slot_index = jnp.clip(micro_index, 0, micro_count - 1)
        first_micro = pick_slot(inputs, slot_index)
        layer_in = jnp.where(section_id == 0, first_micro, incoming)
        allowed = pick_slot(allowed_all, slot_index)

        def run_attention():
            layer_out, saved_acts = attention_forward(
                layer_in, attention_weights, position_bias, allowed
            )
            return (layer_out, saved_acts, ffn_blank)

        def run_ffn():
            layer_out, saved_acts = ffn_forward(layer_in, ffn_weights)
            return (layer_out, attn_blank, saved_acts)

        def run_spare():
            return (layer_zero, attn_blank, ffn_blank)

        choose = jnp.where(active, branch_kind, 2)
        layer_out, attn_saved, ffn_saved = lax.switch(choose, (run_attention, run_ffn, run_spare))
        kept_in = store_slot(kept_in, slot_index, layer_in, active)
        kept_attn = tuple(
            (
                store_slot(buffer, slot_index, new_value, active)
                for buffer, new_value in zip(kept_attn, attn_saved)
            )
        )
        kept_ffn = tuple(
            (
                store_slot(buffer, slot_index, new_value, active)
                for buffer, new_value in zip(kept_ffn, ffn_saved)
            )
        )
        states_out = store_slot(states_out, slot_index, layer_out, active)
        incoming = jax.tree.map(
            lambda part, own: part.astype(own.dtype),
            shifted(shortened(layer_out), "section", 1),
            layer_out,
        )
        return (incoming, kept_in, kept_attn, kept_ffn, states_out)

    start_state = (
        layer_zero,
        jnp.zeros(inputs.shape, jnp.bfloat16),
        stacked(attn_blank),
        stacked(ffn_blank),
        jnp.zeros(inputs.shape, jnp.bfloat16),
    )
    unused, kept_in, kept_attn, kept_ffn, states_out = lax.fori_loop(
        0, tick_count, forward_tick, start_state
    )

    def weight_terms(choose, attn_saved, ffn_saved, grad_out, back_parts):

        def attn_terms():
            return attention_weight_terms(attn_saved, grad_out, back_parts) + grad_zero[4:]

        def ffn_terms():
            return grad_zero[:4] + ffn_weight_terms(ffn_saved, grad_out, back_parts)

        def spare_terms():
            return grad_zero

        return lax.switch(choose, (attn_terms, ffn_terms, spare_terms))

    def accumulate(grad_sums, terms):
        return tuple((running + portion for running, portion in zip(grad_sums, terms)))

    def backward_tick(tick_index, loop_state, with_weights):
        incoming, grad_sums, side_totals, input_grads, stashed = loop_state
        micro_index = tick_index - (section_count - 1 - section_id)
        active = (micro_index >= 0) & (micro_index < micro_count)
        slot_index = jnp.clip(micro_index, 0, micro_count - 1)
        final_grad = pick_slot(cotangent, slot_index)
        grad_out = jnp.where(section_id == section_count - 1, final_grad, incoming)
        layer_in = pick_slot(kept_in, slot_index)
        attn_saved = tuple((pick_slot(buffer, slot_index) for buffer in kept_attn))
        ffn_saved = tuple((pick_slot(buffer, slot_index) for buffer in kept_ffn))
        allowed = pick_slot(allowed_all, slot_index)

        def back_attention():
            input_grad, back_parts, gain_term, bias_grad = attention_input_back(
                layer_in, attn_saved, grad_out, attention_weights, position_bias, allowed
            )
            return (
                input_grad,
                back_parts + (wide_zero, wide_zero),
                jnp.stack([gain_term, zero_row]),
                bias_grad,
            )

        def back_ffn():
            input_grad, back_parts, gain_term = ffn_input_back(
                layer_in, ffn_saved, grad_out, ffn_weights
            )
            return (
                input_grad,
                (inner_zero, inner_zero, inner_zero) + back_parts,
                jnp.stack([zero_row, gain_term]),
                bias_zero,
            )

        def back_spare():
            return (layer_zero, back_blank, gain_zero, bias_zero)

        choose = jnp.where(active, branch_kind, 2)
        input_grad, back_parts, gain_term, bias_grad = lax.switch(
            choose, (back_attention, back_ffn, back_spare)
        )
        side_totals = (side_totals[0] + gain_term, side_totals[1] + bias_grad)
        grad_sums = accumulate(
            grad_sums, weight_terms(choose, attn_saved, ffn_saved, grad_out, back_parts)
        )
        input_grads = store_slot(input_grads, slot_index, input_grad, active)
        incoming = jax.tree.map(
            lambda part, own: part.astype(own.dtype),
            shifted(shortened(input_grad), "section", -1),
            input_grad,
        )
        return (incoming, grad_sums, side_totals, input_grads, stashed)

    side_start = (gain_zero, bias_zero)
    grads_blank = jnp.zeros(inputs.shape, jnp.bfloat16)
    loop_out = lax.fori_loop(
        0,
        tick_count,
        partial(backward_tick, with_weights=True),
        (layer_zero, grad_zero, side_start, grads_blank, ()),
    )
    unused, grad_sums, side_totals, input_grads, stashed = loop_out
    grad_shares = (
        lax.psum_scatter(
            grad_sums[0].astype(jnp.bfloat16), "dp", scatter_dimension=0, tiled=True
        ).astype(jnp.float32),
        lax.psum_scatter(
            grad_sums[1].astype(jnp.bfloat16), "dp", scatter_dimension=0, tiled=True
        ).astype(jnp.float32),
        lax.psum_scatter(
            grad_sums[2].astype(jnp.bfloat16), "dp", scatter_dimension=0, tiled=True
        ).astype(jnp.float32),
        lax.psum_scatter(
            grad_sums[3].astype(jnp.bfloat16), "dp", scatter_dimension=0, tiled=True
        ).astype(jnp.float32),
        lax.psum_scatter(
            grad_sums[4].astype(jnp.bfloat16), "dp", scatter_dimension=0, tiled=True
        ).astype(jnp.float32),
        lax.psum_scatter(
            grad_sums[5].astype(jnp.bfloat16), "dp", scatter_dimension=0, tiled=True
        ).astype(jnp.float32),
        lax.psum_scatter(
            grad_sums[6].astype(jnp.bfloat16), "dp", scatter_dimension=0, tiled=True
        ).astype(jnp.float32),
    )
    placed = tuple(
        (
            lax.dynamic_update_index_in_dim(
                jnp.zeros((layer_count,) + grad_share.shape, jnp.float32), grad_share, layer_id, 0
            )
            for grad_share in grad_shares
        )
    )
    grad_full = (
        lax.psum(placed[0].astype(jnp.bfloat16), "section").astype(jnp.float32),
        lax.psum(placed[1].astype(jnp.bfloat16), "section").astype(jnp.float32),
        lax.psum(placed[2].astype(jnp.bfloat16), "section").astype(jnp.float32),
        lax.psum(placed[3].astype(jnp.bfloat16), "section").astype(jnp.float32),
        lax.psum(placed[4].astype(jnp.bfloat16), "section").astype(jnp.float32),
        lax.psum(placed[5].astype(jnp.bfloat16), "section").astype(jnp.float32),
        lax.psum(placed[6].astype(jnp.bfloat16), "section").astype(jnp.float32),
    )
    gains_placed = lax.dynamic_update_index_in_dim(
        jnp.zeros((layer_count, 2, model_width), jnp.float32), side_totals[0], layer_id, 0
    )
    table_local = jnp.einsum("ijb,hij->bh", onehot, side_totals[1], precision=highest)
    table_grad, gains_all = lax.psum((table_local, gains_placed), ("section", "dp"))
    shard_width = gains.shape[2]
    gains_grad = lax.dynamic_slice_in_dim(
        gains_all, lax.axis_index("dp") * shard_width, shard_width, 2
    )
    return (
        states_out[None],
        input_grads[None],
        grad_full[0],
        grad_full[1],
        grad_full[2],
        grad_full[3],
        grad_full[4],
        grad_full[5],
        grad_full[6],
        gains_grad,
        table_grad,
    )


def solution(mesh):
    placed = (
        P(None, "dp", None, None),
        P(None, "dp", None, None),
        P(None, "dp", None),
        P(None, "dp", None),
        P(None, "dp", None),
        P(None, "dp", None),
        P(None, "dp", None),
        P(None, "dp", None),
        P(None, "dp", None),
        P(None, "dp", None),
        P(None, "dp", None),
        P(None, None, "dp"),
        P(),
    )
    return jax.shard_map(
        body,
        mesh=mesh,
        in_specs=placed,
        out_specs=(
            P("section", None, "dp", None, None),
            P("section", None, "dp", None, None),
            P(None, "dp", None),
            P(None, "dp", None),
            P(None, "dp", None),
            P(None, "dp", None),
            P(None, "dp", None),
            P(None, "dp", None),
            P(None, "dp", None),
            P(None, None, "dp"),
            P(),
        ),
        check_vma=False,
    )
```

profile of v0, /device:TPU:0, one launch (start us, length us, event | category | flops | bytes accessed | tf_op | source)
XLA Modules:
  0.0 2024.8 jit_solution(6079038215074248245)
XLA Ops:
  13.1 33.2 %all-gather = bf16[1,2,512]{1,0,2:T(2,128)(2,1)S(1)} all-gather(bf16[1,2,64]{1,0,2:T(2,128)(2,1)S(1)} %copy.175), channel_id=2, replica_groups=mesh['section'=4,'dp'=8] {'dp'}, dimensions={2}, use_global_device_ids=true | all-gather | bytes 2304 | tf_op jit(solution)/shard_map/all_gather | solution.py:251
  50.5 33.5 %all-gather.1 = bf16[1,512,384]{2,1,0:T(8,128)(2,1)} all-gather(bf16[1,64,384]{2,1,0:T(8,128)(2,1)S(1)} %constant_dynamic-slice_fusion.29), channel_id=3, replica_groups=mesh['section'=4,'dp'=8] {'dp'}, dimensions={1}, use_global_device_ids=true | all-gather | bytes 442368 | tf_op jit(solution)/shard_map/all_gather | solution.py:246
  84.0 33.5 %all-gather.2 = bf16[1,512,384]{2,1,0:T(8,128)(2,1)} all-gather(bf16[1,64,384]{2,1,0:T(8,128)(2,1)S(1)} %constant_dynamic-slice_fusion.28), channel_id=4, replica_groups=mesh['section'=4,'dp'=8] {'dp'}, dimensions={1}, use_global_device_ids=true | all-gather | bytes 442368 | tf_op jit(solution)/shard_map/all_gather | solution.py:244
  117.5 33.9 %all-gather.3 = bf16[1,512,384]{2,1,0:T(8,128)(2,1)} all-gather(bf16[1,64,384]{2,1,0:T(8,128)(2,1)S(1)} %constant_dynamic-slice_fusion.27), channel_id=5, replica_groups=mesh['section'=4,'dp'=8] {'dp'}, dimensions={1}, use_global_device_ids=true | all-gather | bytes 442368 | tf_op jit(solution)/shard_map/all_gather | solution.py:245
  151.4 33.0 %all-gather.4 = bf16[1,384,512]{2,1,0:T(8,128)(2,1)} all-gather(bf16[1,48,512]{2,1,0:T(8,128)(2,1)S(1)} %constant_dynamic-slice_fusion.26), channel_id=6, replica_groups=mesh['section'=4,'dp'=8] {'dp'}, dimensions={1}, use_global_device_ids=true | all-gather | bytes 442368 | tf_op jit(solution)/shard_map/all_gather | solution.py:247
  184.4 8.0 broadcast.280
  192.4 8.0 broadcast.280.clone
  225.5 725.9 %while.75 = (s32[]{:T(128)}, bf16[16,64,512]{2,1,0:T(8,128)(2,1)}, bf16[4,16,64,512]{3,2,1,0:T(8,128)(2,1)}, bf16[4,16,64,512]{3,2,1,0:T(8,128)(2,1)}, bf16[4,16...) while((s32[]{:T(128)}, bf16[16,64,512]{2,1,0:T(8,128)(2,1)}, ...), condition=%wide.region_8.9_spmd.clone, body=%wide.region_0.8_spmd.clone.sunk | while | flops 3244301312 | bytes 207014352 | solution.py:345
  246.5 39.1 %conditional.9 = (bf16[16,64,512]{2,1,0:T(8,128)(2,1)}, bf16[16,64,512]{2,1,0:T(8,128)(2,1)}, f32[16,6,64,1]{2,1,0,3:T(8,128)S(1)}, bf16[16,64,384]{1,2,0:T(8,12...) conditional(s32[]{:T(128)} %clamp.22, ...), branch_computations={%region_1.4_spmd, %region_5.6_spmd, %region_7.7_spmd} | conditional | flops 3236955136 | bytes 56898780 | solution.py:316
  342.8 4.9 constant_dynamic-slice_fusion.54
  347.7 10.4 bitcast_dynamic-update-slice_fusion.20
  362.2 39.1 %conditional.9 = (bf16[16,64,512]{2,1,0:T(8,128)(2,1)}, bf16[16,64,512]{2,1,0:T(8,128)(2,1)}, f32[16,6,64,1]{2,1,0,3:T(8,128)S(1)}, bf16[16,64,384]{1,2,0:T(8,12...) conditional(s32[]{:T(128)} %clamp.22, ...), branch_computations={%region_1.4_spmd, %region_5.6_spmd, %region_7.7_spmd} | conditional | flops 3236955136 | bytes 56898780 | solution.py:316
  463.4 10.6 bitcast_dynamic-update-slice_fusion.20
  478.1 39.1 %conditional.9 = (bf16[16,64,512]{2,1,0:T(8,128)(2,1)}, bf16[16,64,512]{2,1,0:T(8,128)(2,1)}, f32[16,6,64,1]{2,1,0,3:T(8,128)S(1)}, bf16[16,64,384]{1,2,0:T(8,12...) conditional(s32[]{:T(128)} %clamp.22, ...), branch_computations={%region_1.4_spmd, %region_5.6_spmd, %region_7.7_spmd} | conditional | flops 3236955136 | bytes 56898780 | solution.py:316
  579.3 10.4 bitcast_dynamic-update-slice_fusion.20
  593.9 39.1 %conditional.9 = (bf16[16,64,512]{2,1,0:T(8,128)(2,1)}, bf16[16,64,512]{2,1,0:T(8,128)(2,1)}, f32[16,6,64,1]{2,1,0,3:T(8,128)S(1)}, bf16[16,64,384]{1,2,0:T(8,12...) conditional(s32[]{:T(128)} %clamp.22, ...), branch_computations={%region_1.4_spmd, %region_5.6_spmd, %region_7.7_spmd} | conditional | flops 3236955136 | bytes 56898780 | solution.py:316
  695.1 10.5 bitcast_dynamic-update-slice_fusion.20
  709.7 14.9 conditional.9
  779.5 8.0 bitcast_dynamic-update-slice_fusion.20
  791.7 14.9 conditional.9
  861.5 8.0 bitcast_dynamic-update-slice_fusion.20
  873.6 14.9 conditional.9
  943.4 8.0 bitcast_dynamic-update-slice_fusion.20
  955.0 557.4 %while.76 = (s32[]{:T(128)}, bf16[16,64,512]{2,1,0:T(8,128)(2,1)}, f32[512,384]{1,0:T(8,128)}, f32[512,384]{1,0:T(8,128)}, f32[512,384]{1,0:T(8,128)}, /*index=5...) while((s32[]{:T(128)}, bf16[16,64,512]{2,1,0:T(8,128)(2,1)}, ...), condition=%wide.region_24.25_spmd.clone, body=%wide.region_9.24_spmd.clone.sunk | while | flops 6483926528 | bytes 295360896 | solution.py:420
  982.8 7.5 conditional.10
  1013.0 7.5 conditional.10
  1043.8 7.5 conditional.10
  1068.6 57.4 %collective-permute-done.1 = bf16[16,64,512]{2,1,0:T(8,128)(2,1)} collective-permute-done((bf16[16,64,512]{2,1,0:T(8,128)(2,1)S(1)}, bf16[16,64,512]{2,1,0:T(8,128)(2,1)}, u32[]{:S(2)}, u32[]{:S(2)}) %collective-permute-start.1) | collective-permute-done | bytes 1048608 | tf_op jit(solution)/shard_map/while/body/eval_jaxpr/ppermute | solution.py:25
  1130.0 64.3 %conditional.10 = (bf16[16,64,512]{2,1,0:T(8,128)(2,1)S(1)}, bf16[16,64,384]{2,1,0:T(8,128)(2,1)}, bf16[16,64,384]{2,1,0:T(8,128)(2,1)}, bf16[16,64,384]{1,2,0:T...) conditional(s32[]{:T(128)} %clamp.23, ...), branch_computations={%region_10.15_spmd, %region_16.19_spmd, %region_20.20_spmd} | conditional | flops 3256882688 | bytes 101981472 | solution.py:403
  1153.9 5.0 multiply_reduce_fusion
  1198.5 8.9 conditional.11
  1226.0 64.3 %conditional.10 = (bf16[16,64,512]{2,1,0:T(8,128)(2,1)S(1)}, bf16[16,64,384]{2,1,0:T(8,128)(2,1)}, bf16[16,64,384]{2,1,0:T(8,128)(2,1)}, bf16[16,64,384]{1,2,0:T...) conditional(s32[]{:T(128)} %clamp.23, ...), branch_computations={%region_10.15_spmd, %region_16.19_spmd, %region_20.20_spmd} | conditional | flops 3256882688 | bytes 101981472 | solution.py:403
  1250.0 5.0 multiply_reduce_fusion
  1294.6 8.9 conditional.11
  1322.1 64.3 %conditional.10 = (bf16[16,64,512]{2,1,0:T(8,128)(2,1)S(1)}, bf16[16,64,384]{2,1,0:T(8,128)(2,1)}, bf16[16,64,384]{2,1,0:T(8,128)(2,1)}, bf16[16,64,384]{1,2,0:T...) conditional(s32[]{:T(128)} %clamp.23, ...), branch_computations={%region_10.15_spmd, %region_16.19_spmd, %region_20.20_spmd} | conditional | flops 3256882688 | bytes 101981472 | solution.py:403
  1346.0 5.0 multiply_reduce_fusion
  1390.6 8.9 conditional.11
  1418.1 64.3 %conditional.10 = (bf16[16,64,512]{2,1,0:T(8,128)(2,1)S(1)}, bf16[16,64,384]{2,1,0:T(8,128)(2,1)}, bf16[16,64,384]{2,1,0:T(8,128)(2,1)}, bf16[16,64,384]{1,2,0:T...) conditional(s32[]{:T(128)} %clamp.23, ...), branch_computations={%region_10.15_spmd, %region_16.19_spmd, %region_20.20_spmd} | conditional | flops 3256882688 | bytes 101981472 | solution.py:403
  1442.0 5.0 multiply_reduce_fusion
  1486.6 8.9 conditional.11
  1525.1 50.8 %reduce-scatter.14.cloned.1.call-done = bf16[48,512]{1,0:T(8,128)(2,1)} async-done(((bf16[384,512]{1,0:T(8,128)(2,1)}), bf16[48,512]{1,0:T(8,128)(2,1)}) %reduce-scatter.14.cloned.1.call-update) | async-done | bytes 49168 | tf_op jit(solution)/shard_map/reduce_scatter | solution.py:437
  1576.7 63.3 %reduce-scatter.12.cloned.1.call-done = bf16[64,384]{1,0:T(8,128)(2,1)} async-done(((bf16[512,384]{1,0:T(8,128)(2,1)}), bf16[64,384]{1,0:T(8,128)(2,1)}) %reduce-scatter.12.cloned.1.call-update) | async-done | bytes 49168 | tf_op jit(solution)/shard_map/reduce_scatter | solution.py:434
  1640.9 63.3 %reduce-scatter.10.cloned.1.call-done = bf16[64,384]{1,0:T(8,128)(2,1)} async-done(((bf16[512,384]{1,0:T(8,128)(2,1)}), bf16[64,384]{1,0:T(8,128)(2,1)}) %reduce-scatter.10.cloned.1.call-update) | async-done | bytes 49168 | tf_op jit(solution)/shard_map/reduce_scatter | solution.py:431
  1705.0 63.4 %reduce-scatter.8.cloned.1.call-done = bf16[64,384]{1,0:T(8,128)(2,1)} async-done(((bf16[512,384]{1,0:T(8,128)(2,1)}), bf16[64,384]{1,0:T(8,128)(2,1)}) %reduce-scatter.8.cloned.1.call-update) | async-done | bytes 49168 | tf_op jit(solution)/shard_map/reduce_scatter | solution.py:428
  1769.3 65.0 %reduce-scatter.20.cloned.1.call-done = bf16[128,512]{1,0:T(8,128)(2,1)} async-done(((bf16[1024,512]{1,0:T(8,128)(2,1)}), bf16[128,512]{1,0:T(8,128)(2,1)}) %reduce-scatter.20.cloned.1.call-update) | async-done | bytes 131088 | tf_op jit(solution)/shard_map/reduce_scatter | solution.py:446
  1835.3 65.3 %reduce-scatter.18.cloned.1.call-done = bf16[64,1024]{1,0:T(8,128)(2,1)} async-done(((bf16[512,1024]{1,0:T(8,128)(2,1)}), bf16[64,1024]{1,0:T(8,128)(2,1)}) %reduce-scatter.18.cloned.1.call-update) | async-done | bytes 131088 | tf_op jit(solution)/shard_map/reduce_scatter | solution.py:443
  1901.5 64.7 %reduce-scatter.16.cloned.1.call-done = bf16[64,1024]{1,0:T(8,128)(2,1)} async-done(((bf16[512,1024]{1,0:T(8,128)(2,1)}), bf16[64,1024]{1,0:T(8,128)(2,1)}) %reduce-scatter.16.cloned.1.call-update) | async-done | bytes 131088 | tf_op jit(solution)/shard_map/reduce_scatter | solution.py:440
  1968.8 40.4 %all-reduce.2 = (f32[2,2,512]{2,1,0:T(2,128)S(1)}, f32[32,6]{0,1:T(8,128)}) all-reduce(f32[2,2,512]{2,1,0:T(2,128)S(1)} %constant_dynamic-update-slice_fusion.4, f32[32,6]{0,1:T(8,128)S(1)} %convolution_bitcast_fusion.7), channel_id=1, replica_groups=mesh['section'=4,'dp'=8] {'section','dp'}, use_global_device_ids=true, to_apply=%region_39.40 | all-reduce | flops 2240 | bytes 17920 | tf_op jit(solution)/shard_map/psum | solution.py:471
  (1293 shorter events, 1157.9 us)
Async XLA Ops:
  7.2 40.0 %copy-start.70 = (bf16[32,6]{0,1:T(8,128)(2,1)S(1)}, bf16[32,6]{0,1:T(8,128)(2,1)}, u32[]{:S(2)}) copy-start(bf16[32,6]{0,1:T(8,128)(2,1)} %param.38) | copy-start | bytes 1156
  7.2 40.4 %copy-start.66 = (bf16[2,64,384]{2,1,0:T(8,128)(2,1)S(1)}, bf16[2,64,384]{2,1,0:T(8,128)(2,1)}, u32[]{:S(2)}) copy-start(bf16[2,64,384]{2,1,0:T(8,128)(2,1)} %param.32) | copy-start | bytes 294916
  7.2 40.4 %copy-start.67 = (bf16[2,64,384]{2,1,0:T(8,128)(2,1)S(1)}, bf16[2,64,384]{2,1,0:T(8,128)(2,1)}, u32[]{:S(2)}) copy-start(bf16[2,64,384]{2,1,0:T(8,128)(2,1)} %param.30) | copy-start | bytes 294916
  7.2 40.4 %copy-start.68 = (bf16[2,64,384]{2,1,0:T(8,128)(2,1)S(1)}, bf16[2,64,384]{2,1,0:T(8,128)(2,1)}, u32[]{:S(2)}) copy-start(bf16[2,64,384]{2,1,0:T(8,128)(2,1)} %param.31) | copy-start | bytes 294916
  7.2 40.5 %copy-start.69 = (bf16[2,48,512]{2,1,0:T(8,128)(2,1)S(1)}, bf16[2,48,512]{2,1,0:T(8,128)(2,1)}, u32[]{:S(2)}) copy-start(bf16[2,48,512]{2,1,0:T(8,128)(2,1)} %param.33) | copy-start | bytes 294916
  7.2 177.1 %all-gather.12.cloned.1.call-start = ((), (), s32[]{:S(2)}) async-start(), calls=%async_computation.14 | async-start | bytes 1179648 | tf_op jit(solution)/shard_map/all_gather | solution.py:248
  8.8 175.6 %all-gather.14.cloned.1.call-start = ((), (), s32[]{:S(2)}) async-start(), calls=%async_computation.15 | async-start | bytes 1179648 | tf_op jit(solution)/shard_map/all_gather | solution.py:249
  10.5 174.0 %all-gather.16.cloned.1.call-start = ((), (), s32[]{:S(2)}) async-start(), calls=%async_computation.16 | async-start | bytes 1179648 | tf_op jit(solution)/shard_map/all_gather | solution.py:250
  12.1 1563.8 %reduce-scatter.14.cloned.1.call-start = ((), (), s32[]{:S(2)}) async-start(), calls=%async_computation.10 | async-start | bytes 442368 | tf_op jit(solution)/shard_map/reduce_scatter | solution.py:437
  13.1 171.3 %copy-start.65 = (s32[4,16,64]{2,1,0:T(8,128)S(1)}, s32[4,16,64]{2,1,0:T(8,128)}, u32[]{:S(2)}) copy-start(s32[4,16,64]{2,1,0:T(8,128)} %param.29) | copy-start | bytes 49156
  285.7 72.4 %collective-permute-start = (bf16[16,64,512]{2,1,0:T(8,128)(2,1)}, bf16[16,64,512]{2,1,0:T(8,128)(2,1)}, u32[]{:S(2)}, u32[]{:S(2)}) collective-permute-start(bf16[16,64,512]{2,1,0:T(8,128)(2,1)} %get-tuple-element.3112), channel_id=1, source_target_pairs={{0,8},{8,16},{16,24},{1,9},{9,17},{17,25},{2,10},{10,18},{18,26},{... | collective-permute-start | bytes 3145736 | tf_op jit(solution)/shard_map/while/body/eval_jaxpr/ppermute | solution.py:25
  370.0 5.7 copy-start.22
  401.3 72.6 %collective-permute-start = (bf16[16,64,512]{2,1,0:T(8,128)(2,1)}, bf16[16,64,512]{2,1,0:T(8,128)(2,1)}, u32[]{:S(2)}, u32[]{:S(2)}) collective-permute-start(bf16[16,64,512]{2,1,0:T(8,128)(2,1)} %get-tuple-element.3112), channel_id=1, source_target_pairs={{0,8},{8,16},{16,24},{1,9},{9,17},{17,25},{2,10},{10,18},{18,26},{... | collective-permute-start | bytes 3145736 | tf_op jit(solution)/shard_map/while/body/eval_jaxpr/ppermute | solution.py:25
  486.0 5.7 copy-start.22
  517.3 72.5 %collective-permute-start = (bf16[16,64,512]{2,1,0:T(8,128)(2,1)}, bf16[16,64,512]{2,1,0:T(8,128)(2,1)}, u32[]{:S(2)}, u32[]{:S(2)}) collective-permute-start(bf16[16,64,512]{2,1,0:T(8,128)(2,1)} %get-tuple-element.3112), channel_id=1, source_target_pairs={{0,8},{8,16},{16,24},{1,9},{9,17},{17,25},{2,10},{10,18},{18,26},{... | collective-permute-start | bytes 3145736 | tf_op jit(solution)/shard_map/while/body/eval_jaxpr/ppermute | solution.py:25
  633.0 72.6 %collective-permute-start = (bf16[16,64,512]{2,1,0:T(8,128)(2,1)}, bf16[16,64,512]{2,1,0:T(8,128)(2,1)}, u32[]{:S(2)}, u32[]{:S(2)}) collective-permute-start(bf16[16,64,512]{2,1,0:T(8,128)(2,1)} %get-tuple-element.3112), channel_id=1, source_target_pairs={{0,8},{8,16},{16,24},{1,9},{9,17},{17,25},{2,10},{10,18},{18,26},{... | collective-permute-start | bytes 3145736 | tf_op jit(solution)/shard_map/while/body/eval_jaxpr/ppermute | solution.py:25
  724.6 62.9 %collective-permute-start = (bf16[16,64,512]{2,1,0:T(8,128)(2,1)}, bf16[16,64,512]{2,1,0:T(8,128)(2,1)}, u32[]{:S(2)}, u32[]{:S(2)}) collective-permute-start(bf16[16,64,512]{2,1,0:T(8,128)(2,1)} %get-tuple-element.3112), channel_id=1, source_target_pairs={{0,8},{8,16},{16,24},{1,9},{9,17},{17,25},{2,10},{10,18},{18,26},{... | collective-permute-start | bytes 3145736 | tf_op jit(solution)/shard_map/while/body/eval_jaxpr/ppermute | solution.py:25
  806.5 62.9 %collective-permute-start = (bf16[16,64,512]{2,1,0:T(8,128)(2,1)}, bf16[16,64,512]{2,1,0:T(8,128)(2,1)}, u32[]{:S(2)}, u32[]{:S(2)}) collective-permute-start(bf16[16,64,512]{2,1,0:T(8,128)(2,1)} %get-tuple-element.3112), channel_id=1, source_target_pairs={{0,8},{8,16},{16,24},{1,9},{9,17},{17,25},{2,10},{10,18},{18,26},{... | collective-permute-start | bytes 3145736 | tf_op jit(solution)/shard_map/while/body/eval_jaxpr/ppermute | solution.py:25
  888.5 62.9 %collective-permute-start = (bf16[16,64,512]{2,1,0:T(8,128)(2,1)}, bf16[16,64,512]{2,1,0:T(8,128)(2,1)}, u32[]{:S(2)}, u32[]{:S(2)}) collective-permute-start(bf16[16,64,512]{2,1,0:T(8,128)(2,1)} %get-tuple-element.3112), channel_id=1, source_target_pairs={{0,8},{8,16},{16,24},{1,9},{9,17},{17,25},{2,10},{10,18},{18,26},{... | collective-permute-start | bytes 3145736 | tf_op jit(solution)/shard_map/while/body/eval_jaxpr/ppermute | solution.py:25
  990.2 16.9 collective-permute-start.1
  1020.5 17.3 collective-permute-start.1
  1051.3 74.8 %collective-permute-start.1 = (bf16[16,64,512]{2,1,0:T(8,128)(2,1)S(1)}, bf16[16,64,512]{2,1,0:T(8,128)(2,1)}, u32[]{:S(2)}, u32[]{:S(2)}) collective-permute-start(bf16[16,64,512]{2,1,0:T(8,128)(2,1)S(1)} %get-tuple-element.3171), channel_id=1, source_target_pairs={{8,0},{16,8},{24,16},{9,1},{17,9},{25,17},{10,2},{18,10},{26,18},{... | collective-permute-start | bytes 3145736 | tf_op jit(solution)/shard_map/while/body/eval_jaxpr/ppermute | solution.py:25
  1068.6 57.5 %copy-start.27 = (f32[512,1024]{1,0:T(8,128)}, f32[512,1024]{1,0:T(8,128)S(1)}, u32[]{:S(2)}) copy-start(f32[512,1024]{1,0:T(8,128)S(1)} %get-tuple-element.3467) | copy-start | bytes 6291460 | tf_op jit(solution)/shard_map/while
  1068.6 57.5 %copy-start.30 = (f32[512,1024]{1,0:T(8,128)}, f32[512,1024]{1,0:T(8,128)S(1)}, u32[]{:S(2)}) copy-start(f32[512,1024]{1,0:T(8,128)S(1)} %get-tuple-element.3468) | copy-start | bytes 6291460 | tf_op jit(solution)/shard_map/while
  1194.3 27.7 %collective-permute-start.1 = (bf16[16,64,512]{2,1,0:T(8,128)(2,1)S(1)}, bf16[16,64,512]{2,1,0:T(8,128)(2,1)}, u32[]{:S(2)}, u32[]{:S(2)}) collective-permute-start(bf16[16,64,512]{2,1,0:T(8,128)(2,1)S(1)} %get-tuple-element.3171), channel_id=1, source_target_pairs={{8,0},{16,8},{24,16},{9,1},{17,9},{25,17},{10,2},{18,10},{26,18},{... | collective-permute-start | bytes 3145736 | tf_op jit(solution)/shard_map/while/body/eval_jaxpr/ppermute | solution.py:25
  1290.3 27.7 %collective-permute-start.1 = (bf16[16,64,512]{2,1,0:T(8,128)(2,1)S(1)}, bf16[16,64,512]{2,1,0:T(8,128)(2,1)}, u32[]{:S(2)}, u32[]{:S(2)}) collective-permute-start(bf16[16,64,512]{2,1,0:T(8,128)(2,1)S(1)} %get-tuple-element.3171), channel_id=1, source_target_pairs={{8,0},{16,8},{24,16},{9,1},{17,9},{25,17},{10,2},{18,10},{26,18},{... | collective-permute-start | bytes 3145736 | tf_op jit(solution)/shard_map/while/body/eval_jaxpr/ppermute | solution.py:25
  1386.4 27.7 %collective-permute-start.1 = (bf16[16,64,512]{2,1,0:T(8,128)(2,1)S(1)}, bf16[16,64,512]{2,1,0:T(8,128)(2,1)}, u32[]{:S(2)}, u32[]{:S(2)}) collective-permute-start(bf16[16,64,512]{2,1,0:T(8,128)(2,1)S(1)} %get-tuple-element.3171), channel_id=1, source_target_pairs={{8,0},{16,8},{24,16},{9,1},{17,9},{25,17},{10,2},{18,10},{26,18},{... | collective-permute-start | bytes 3145736 | tf_op jit(solution)/shard_map/while/body/eval_jaxpr/ppermute | solution.py:25
  1482.4 25.2 %collective-permute-start.1 = (bf16[16,64,512]{2,1,0:T(8,128)(2,1)S(1)}, bf16[16,64,512]{2,1,0:T(8,128)(2,1)}, u32[]{:S(2)}, u32[]{:S(2)}) collective-permute-start(bf16[16,64,512]{2,1,0:T(8,128)(2,1)S(1)} %get-tuple-element.3171), channel_id=1, source_target_pairs={{8,0},{16,8},{24,16},{9,1},{17,9},{25,17},{10,2},{18,10},{26,18},{... | collective-permute-start | bytes 3145736 | tf_op jit(solution)/shard_map/while/body/eval_jaxpr/ppermute | solution.py:25
  1512.5 6.3 copy-start.36
  1514.5 125.5 %reduce-scatter.12.cloned.1.call-start = ((), (), s32[]{:S(2)}) async-start(), calls=%async_computation.9 | async-start | bytes 442368 | tf_op jit(solution)/shard_map/reduce_scatter | solution.py:434
  1516.7 187.5 %reduce-scatter.10.cloned.1.call-start = ((), (), s32[]{:S(2)}) async-start(), calls=%async_computation.8 | async-start | bytes 442368 | tf_op jit(solution)/shard_map/reduce_scatter | solution.py:431
  1518.7 249.8 %reduce-scatter.8.cloned.1.call-start = ((), (), s32[]{:S(2)}) async-start(), calls=%async_computation.7 | async-start | bytes 442368 | tf_op jit(solution)/shard_map/reduce_scatter | solution.py:428
  1519.6 314.8 %reduce-scatter.20.cloned.1.call-start = ((), (), s32[]{:S(2)}) async-start(), calls=%async_computation.13 | async-start | bytes 1179648 | tf_op jit(solution)/shard_map/reduce_scatter | solution.py:446
  1520.8 379.8 %reduce-scatter.18.cloned.1.call-start = ((), (), s32[]{:S(2)}) async-start(), calls=%async_computation.12 | async-start | bytes 1179648 | tf_op jit(solution)/shard_map/reduce_scatter | solution.py:443
  1523.8 442.5 %reduce-scatter.16.cloned.1.call-start = ((), (), s32[]{:S(2)}) async-start(), calls=%async_computation.11 | async-start | bytes 1179648 | tf_op jit(solution)/shard_map/reduce_scatter | solution.py:440
  1525.0 442.9 %copy-start.49 = (f32[6,64,64]{1,2,0:T(8,128)S(1)}, f32[6,64,64]{1,2,0:T(8,128)}, u32[]{:S(2)}) copy-start(f32[6,64,64]{1,2,0:T(8,128)} %get-tuple-element.1821) | copy-start | bytes 294916
  1525.1 484.8 %all-reduce.6.cloned.1.call-start = ((), (), s32[]{:S(2)}) async-start(), calls=%async_computation.17 | async-start | bytes 2359296 | tf_op jit(solution)/shard_map/psum | solution.py:459
  1576.7 390.5 %copy-start.54 = (bf16[2,48,512]{2,1,0:T(8,128)(2,1)}, bf16[2,48,512]{2,1,0:T(8,128)(2,1)S(1)}, u32[]{:S(2)}) copy-start(bf16[2,48,512]{2,1,0:T(8,128)(2,1)S(1)} %convert_dynamic-update-slice_fusion.3) | copy-start | bytes 294916
  1640.9 326.4 %copy-start.55 = (bf16[2,64,384]{2,1,0:T(8,128)(2,1)}, bf16[2,64,384]{2,1,0:T(8,128)(2,1)S(1)}, u32[]{:S(2)}) copy-start(bf16[2,64,384]{2,1,0:T(8,128)(2,1)S(1)} %convert_dynamic-update-slice_fusion.4) | copy-start | bytes 294916
  1640.9 327.2 %copy-start.60 = (s32[64,64]{1,0:T(8,128)S(1)}, s32[64,64]{1,0:T(8,128)}, u32[]{:S(2)}) copy-start(s32[64,64]{1,0:T(8,128)} %copy-done.59) | copy-start | bytes 49156
  1705.0 262.2 %copy-start.56 = (bf16[2,64,384]{2,1,0:T(8,128)(2,1)}, bf16[2,64,384]{2,1,0:T(8,128)(2,1)S(1)}, u32[]{:S(2)}) copy-start(bf16[2,64,384]{2,1,0:T(8,128)(2,1)S(1)} %convert_dynamic-update-slice_fusion.5) | copy-start | bytes 294916
  1769.3 198.0 %copy-start.57 = (bf16[2,64,384]{2,1,0:T(8,128)(2,1)}, bf16[2,64,384]{2,1,0:T(8,128)(2,1)S(1)}, u32[]{:S(2)}) copy-start(bf16[2,64,384]{2,1,0:T(8,128)(2,1)S(1)} %convert_dynamic-update-slice_fusion.6) | copy-start | bytes 294916
  1835.3 132.0 %copy-start.50 = (bf16[2,128,512]{2,1,0:T(8,128)(2,1)}, bf16[2,128,512]{2,1,0:T(8,128)(2,1)S(1)}, u32[]{:S(2)}) copy-start(bf16[2,128,512]{2,1,0:T(8,128)(2,1)S(1)} %convert_dynamic-update-slice_fusion) | copy-start | bytes 786436
  1901.5 65.8 %copy-start.51 = (bf16[2,64,1024]{2,1,0:T(8,128)(2,1)}, bf16[2,64,1024]{2,1,0:T(8,128)(2,1)S(1)}, u32[]{:S(2)}) copy-start(bf16[2,64,1024]{2,1,0:T(8,128)(2,1)S(1)} %convert_dynamic-update-slice_fusion.1) | copy-start | bytes 786436
  1967.9 50.2 %copy-start.1 = (bf16[2,64,1024]{2,1,0:T(8,128)(2,1)S(1)}, bf16[2,64,1024]{2,1,0:T(8,128)(2,1)}, u32[]{:S(2)}) copy-start(bf16[2,64,1024]{2,1,0:T(8,128)(2,1)} %param.34) | copy-start | bytes 786436
  2009.9 6.1 copy-start.63
  2009.9 6.8 copy-start.62
  2009.9 7.5 copy-start.61
  (255 other events, 730.5 us)
Sparse Core Ops, SparseCore 0:
  10.8 43.6 all-gather.11
  57.2 41.6 all-gather.13
  101.6 40.5 all-gather.15
  1514.6 61.2 reduce-scatter.13
  1579.6 60.3 reduce-scatter.11
  1643.7 60.4 reduce-scatter.9
  1708.0 60.3 reduce-scatter.7
  1771.9 62.4 reduce-scatter.19
  1838.1 62.3 reduce-scatter.17
  1903.8 62.3 reduce-scatter.15
  1970.5 38.3 all-reduce.5
where the time goes:
time: 2040 us; the launch traced here: 2020 us
  local copies, waits for them, and re-layouts  690 us (34%)
  waiting for transfers between devices  501 us (25%)
  other arithmetic  335 us (16%)
  blocking collectives  207 us (10%)
  matrix products  203 us (10%)
  loops' own time  47.6 us (2%)
  starting transfers between devices  25.2 us (1%)
    dynamic_slice x119, local copies, waits for them, and re-layouts, store_slot(): previous = lax.dynamic_index_in_dim(buffer, slot_index, 0, keepdims=False)  215 us
    dynamic_update_slice x49, other arithmetic, store_slot(): lax.dynamic_update_index_in_dim(buffer, jnp.where(active, new_value, prev...  156 us
    dynamic_update_slice x42, local copies, waits for them, and re-layouts, store_slot(): lax.dynamic_update_index_in_dim(buffer, jnp.where(active, new_value, prev...  83 us
    reshape x28, local copies, waits for them, and re-layouts, split_heads(): return values.reshape(values.shape[0], values.shape[1], head_count, -1)  69.7 us
    reduce_scatter x1, waiting for transfers between devices, body(): lax.psum_scatter(grad_sums[5].astype(jnp.bfloat16), 'dp', scatter_dimensi...  65.3 us
    ppermute x14, waiting for transfers between devices, shifted(): return lax.ppermute(value, axis, pairs)  65.2 us
    reduce_scatter x1, waiting for transfers between devices, body(): lax.psum_scatter(grad_sums[6].astype(jnp.bfloat16), 'dp', scatter_dimensi...  65 us
    reduce_scatter x1, waiting for transfers between devices, body(): lax.psum_scatter(grad_sums[4].astype(jnp.bfloat16), 'dp', scatter_dimensi...  64.7 us
  transfers between devices with their start and end apart: 25, of which 11 were waited for; matrix products, arithmetic and copies ran while one was open for 29% of the time, Pallas kernels for 0%

commit v1 on v0

v1 whole, which is shorter than its diff:
```python
import jax
import jax.numpy as jnp
from jax import lax
from jax.experimental import pallas as pl
from jax.experimental.pallas import tpu as pltpu
from jax.sharding import PartitionSpec as P

eps_norm = 1e-06
limits = (12, 16, 23, 32, 46, 64, 91)
masked = -1e30
bf = jnp.bfloat16
f32 = jnp.float32
vmem_limit = 60 * 1024 * 1024


def dot_nn(a, b):
    return lax.dot_general(a, b, (((1,), (0,)), ((), ())), preferred_element_type=f32)


def dot_nt(a, b):
    return lax.dot_general(a, b, (((1,), (1,)), ((), ())), preferred_element_type=f32)


def dot_tn(a, b):
    return lax.dot_general(a, b, (((0,), (0,)), ((), ())), preferred_element_type=f32)


def row_scale(x):
    return lax.rsqrt(jnp.mean(x * x, axis=-1, keepdims=True) + eps_norm)


def pair_parts(values):
    lane = lax.broadcasted_iota(jnp.int32, values.shape, 1)
    zero = jnp.zeros_like(values)
    return jnp.concatenate(
        [jnp.where(lane < 64, values, zero), jnp.where(lane < 64, zero, values)], axis=0
    )


def pair_pick(values):
    half = values.shape[0] // 2
    lane = lax.broadcasted_iota(jnp.int32, (half, values.shape[1]), 1)
    return jnp.where(lane < 64, values[:half], values[half:])


def pair_max(values):
    lane = lax.broadcasted_iota(jnp.int32, values.shape, 1)
    low = jnp.max(jnp.where(lane < 64, values, -jnp.inf), axis=-1, keepdims=True)
    high = jnp.max(jnp.where(lane < 64, -jnp.inf, values), axis=-1, keepdims=True)
    return jnp.where(lane < 64, low, high)


def pair_sum(values):
    lane = lax.broadcasted_iota(jnp.int32, values.shape, 1)
    low = jnp.sum(jnp.where(lane < 64, values, 0.0), axis=-1, keepdims=True)
    high = jnp.sum(jnp.where(lane < 64, 0.0, values), axis=-1, keepdims=True)
    return jnp.where(lane < 64, low, high)


def attn_fwd_kernel(x_ref, mask_ref, bias_ref, gain_ref, wq_ref, wk_ref, wv_ref, wo_ref,
                    out_ref, q_ref, k_ref, v_ref, p_ref, att_ref):
    x = x_ref[...].astype(f32)
    a = (x * row_scale(x) * gain_ref[...]).astype(bf)
    q = dot_nn(a, wq_ref[...]).astype(bf)
    k = dot_nn(a, wk_ref[...]).astype(bf)
    v = dot_nn(a, wv_ref[...]).astype(bf)
    q_ref[...] = q
    k_ref[...] = k
    v_ref[...] = v
    rows = x.shape[0] // 64
    units = [(r, h) for r in range(rows) for h in range(3)]
    at = lambda arr, r, h: arr[r * 64:r * 64 + 64, h * 128:h * 128 + 128]
    scores = [dot_nt(at(k, r, h), pair_parts(at(q, r, h))) for r, h in units]
    probs = []
    for (r, h), s in zip(units, scores):
        s = s + (bias_ref[:, h * 128:h * 128 + 128] + mask_ref[r])
        e = jnp.exp(s - jnp.max(s, axis=0, keepdims=True))
        p = (e * (1.0 / jnp.sum(e, axis=0, keepdims=True))).astype(bf)
        p_ref[r * 64:r * 64 + 64, h * 128:h * 128 + 128] = p
        probs.append(p)
    full_att = [dot_tn(p, at(v, r, h)) for (r, h), p in zip(units, probs)]
    att = {unit: pair_pick(part).astype(bf) for unit, part in zip(units, full_att)}
    att = jnp.concatenate([jnp.concatenate([att[r, h] for h in range(3)], axis=1) for r in range(rows)], axis=0)
    att_ref[...] = att
    out_ref[...] = (x + dot_nn(att, wo_ref[...])).astype(bf)


def attn_bwd_kernel(x_ref, q_ref, k_ref, v_ref, p_ref, att_ref, g_ref, gain_ref,
                    wq_ref, wk_ref, wv_ref, wo_ref,
                    gin_ref, dwq_ref, dwk_ref, dwv_ref, dwo_ref, dgain_ref, dbias_ref,
                    a_s, dq_s, dk_s, dv_s, att_s, g_s, dgain_s, dbias_s):
    step = pl.program_id(0)
    last = pl.num_programs(0) - 1
    block = x_ref.shape[0]

    @pl.when(step == 0)
    def _():
        dgain_s[...] = jnp.zeros_like(dgain_s)
        dbias_s[...] = jnp.zeros_like(dbias_s)

    here = pl.ds(pl.multiple_of(step * block, block), block)
    g_low = g_ref[...]
    da = dot_nt(g_low, wo_ref[...]).astype(bf)
    att_s[here, :] = att_ref[...]
    g_s[here, :] = g_low
    rows = block // 64
    units = [(r, h) for r in range(rows) for h in range(3)]
    at = lambda arr, r, h: arr[r * 64:r * 64 + 64, h * 128:h * 128 + 128]
    db = [None] * 3
    da_bds = [pair_parts(at(da, r, h)) for r, h in units]
    dps = [dot_nt(at(v_ref, r, h), da_bd) for (r, h), da_bd in zip(units, da_bds)]
    dv_u = {(r, h): dot_nn(at(p_ref, r, h), da_bd).astype(bf) for (r, h), da_bd in zip(units, da_bds)}
    dss = []
    for (r, h), dp in zip(units, dps):
        pf = at(p_ref, r, h).astype(f32)
        ds = pf * (dp - jnp.sum(pf * dp, axis=0, keepdims=True))
        db[h] = ds if db[h] is None else db[h] + ds
        dss.append(ds.astype(bf))
    dk_u = {(r, h): dot_nn(ds, pair_parts(at(q_ref, r, h))).astype(bf) for (r, h), ds in zip(units, dss)}
    full_dq = [dot_tn(ds, at(k_ref, r, h)) for (r, h), ds in zip(units, dss)]
    dq_u = {unit: pair_pick(part).astype(bf) for unit, part in zip(units, full_dq)}
    join = lambda u: jnp.concatenate([jnp.concatenate([u[r, h] for h in range(3)], axis=1) for r in range(rows)], axis=0)
    dq, dk, dv = join(dq_u), join(dk_u), join(dv_u)
    dq_s[here, :] = dq
    dk_s[here, :] = dk
    dv_s[here, :] = dv
    for h in range(3):
        dbias_s[:, h * 128:h * 128 + 128] += db[h]
    gx = dot_nt(dq, wq_ref[...]) + dot_nt(dk, wk_ref[...]) + dot_nt(dv, wv_ref[...])
    x = x_ref[...].astype(f32)
    r_ = row_scale(x)
    n = x * r_
    a_s[here, :] = (n * gain_ref[...]).astype(bf)
    dgain_s[...] += jnp.sum(gx * n, axis=0, keepdims=True)
    e = gx * gain_ref[...]
    dx = r_ * (e - n * jnp.mean(e * n, axis=-1, keepdims=True))
    gin_ref[...] = (g_low.astype(f32) + dx).astype(bf)

    @pl.when(step == last)
    def _():
        dwq_ref[...] = dot_tn(a_s[...], dq_s[...]).astype(bf)
        dwk_ref[...] = dot_tn(a_s[...], dk_s[...]).astype(bf)
        dwv_ref[...] = dot_tn(a_s[...], dv_s[...]).astype(bf)
        dwo_ref[...] = dot_tn(att_s[...], g_s[...]).astype(bf)
        dgain_ref[...] = dgain_s[...]
        dbias_ref[...] = dbias_s[...]


def gelu_parts(u):
    c = 0.7978845608028654
    u2 = u * u
    t = jnp.tanh(u * (c + (c * 0.044715) * u2))
    half = 0.5 + 0.5 * t
    act = u * half
    slope = half + (0.5 * u) * (1.0 - t * t) * (c + (3.0 * c * 0.044715) * u2)
    return act, slope


def gelu(u):
    c = 0.7978845608028654
    t = jnp.tanh(u * (c + (c * 0.044715) * (u * u)))
    return u * (0.5 + 0.5 * t)


def ffn_fwd_kernel(x_ref, gain_ref, wg_ref, wu_ref, wd_ref, out_ref, gate_ref, up_ref):
    x = x_ref[...].astype(f32)
    a = (x * row_scale(x) * gain_ref[...]).astype(bf)
    gate = dot_nn(a, wg_ref[...])
    up = dot_nn(a, wu_ref[...])
    gate_ref[...] = gate.astype(bf)
    up_ref[...] = up.astype(bf)
    hidden = (gelu(gate) * up).astype(bf)
    out_ref[...] = (x + dot_nn(hidden, wd_ref[...])).astype(bf)


def ffn_bwd_kernel(x_ref, gate_ref, up_ref, g_ref, gain_ref, wg_ref, wu_ref, wd_ref,
                   gin_ref, dwg_ref, dwu_ref, dwd_ref, dgain_ref,
                   a_s, gb_s, ub_s, hid_s, g_s, dgain_s):
    step = pl.program_id(0)
    last = pl.num_programs(0) - 1
    block = x_ref.shape[0]

    @pl.when(step == 0)
    def _():
        dgain_s[...] = jnp.zeros_like(dgain_s)

    here = pl.ds(pl.multiple_of(step * block, block), block)
    g_low = g_ref[...]
    g_s[here, :] = g_low
    hg = dot_nt(g_low, wd_ref[...])
    gate = gate_ref[...].astype(f32)
    up = up_ref[...].astype(f32)
    act, slope = gelu_parts(gate)
    hid_s[here, :] = (act * up).astype(bf)
    gb = (hg * up * slope).astype(bf)
    ub = (hg * act).astype(bf)
    gb_s[here, :] = gb
    ub_s[here, :] = ub
    gx = dot_nt(gb, wg_ref[...]) + dot_nt(ub, wu_ref[...])
    x = x_ref[...].astype(f32)
    r_ = row_scale(x)
    n = x * r_
    a_s[here, :] = (n * gain_ref[...]).astype(bf)
    dgain_s[...] += jnp.sum(gx * n, axis=0, keepdims=True)
    e = gx * gain_ref[...]
    dx = r_ * (e - n * jnp.mean(e * n, axis=-1, keepdims=True))
    gin_ref[...] = (g_low.astype(f32) + dx).astype(bf)

    @pl.when(step == last)
    def _():
        dwg_ref[...] = dot_tn(a_s[...], gb_s[...]).astype(bf)
        dwu_ref[...] = dot_tn(a_s[...], ub_s[...]).astype(bf)
        dwd_ref[...] = dot_tn(hid_s[...], g_s[...]).astype(bf)
        dgain_ref[...] = dgain_s[...]


def tok(block, width):
    return pl.BlockSpec((block, width), lambda i: (i, 0))


def full(shape):
    zero = (0,) * len(shape)
    return pl.BlockSpec(shape, lambda i: zero)


def sds(shape, dtype):
    return jax.ShapeDtypeStruct(shape, dtype)


def call(kernel, grid, in_specs, out_specs, out_shape, scratch, flops, byts, name):
    return pl.pallas_call(
        kernel, grid=(grid,), in_specs=in_specs, out_specs=out_specs, out_shape=out_shape,
        scratch_shapes=scratch, name=name,
        compiler_params=pltpu.CompilerParams(vmem_limit_bytes=vmem_limit),
        cost_estimate=pl.CostEstimate(flops=flops, bytes_accessed=byts, transcendentals=0),
    )


def attn_fwd(x, mask, bias, gain, wq, wk, wv, wo, block=256):
    t, d = x.shape
    inner = wq.shape[1]
    return call(attn_fwd_kernel, t // block,
        [tok(block, d), pl.BlockSpec((block // 64, 64, 128), lambda i: (i, 0, 0)), full(bias.shape),
         full((1, d)), full(wq.shape), full(wk.shape), full(wv.shape), full(wo.shape)],
        [tok(block, d)] + [tok(block, inner)] * 5,
        [sds((t, d), bf)] + [sds((t, inner), bf)] * 5, [],
        2 * t * d * inner * 4, 4 * t * d, "attn_fwd")(x, mask, bias, gain, wq, wk, wv, wo)


def attn_bwd(x, q, k, v, p, att, g, gain, wq, wk, wv, wo, block=256):
    t, d = x.shape
    inner = wq.shape[1]
    return call(attn_bwd_kernel, t // block,
        [tok(block, d)] + [tok(block, inner)] * 5 + [tok(block, d), full((1, d)),
         full(wq.shape), full(wk.shape), full(wv.shape), full(wo.shape)],
        [tok(block, d), full(wq.shape), full(wk.shape), full(wv.shape), full(wo.shape),
         full((1, d)), full((64, inner))],
        [sds((t, d), bf), sds(wq.shape, bf), sds(wk.shape, bf), sds(wv.shape, bf), sds(wo.shape, bf),
         sds((1, d), f32), sds((64, inner), f32)],
        [pltpu.VMEM((t, d), bf)] + [pltpu.VMEM((t, inner), bf)] * 4 + [pltpu.VMEM((t, d), bf),
         pltpu.VMEM((1, d), f32), pltpu.VMEM((64, inner), f32)],
        2 * t * d * inner * 8, 12 * t * d, "attn_bwd")(x, q, k, v, p, att, g, gain, wq, wk, wv, wo)


def ffn_fwd(x, gain, wg, wu, wd, block=256):
    t, d = x.shape
    ff = wg.shape[1]
    return call(ffn_fwd_kernel, t // block,
        [tok(block, d), full((1, d)), full(wg.shape), full(wu.shape), full(wd.shape)],
        [tok(block, d), tok(block, ff), tok(block, ff)],
        [sds((t, d), bf), sds((t, ff), bf), sds((t, ff), bf)], [],
        2 * t * d * ff * 3, 4 * t * d, "ffn_fwd")(x, gain, wg, wu, wd)


def ffn_bwd(x, gate, up, g, gain, wg, wu, wd, block=256):
    t, d = x.shape
    ff = wg.shape[1]
    return call(ffn_bwd_kernel, t // block,
        [tok(block, d), tok(block, ff), tok(block, ff), tok(block, d), full((1, d)),
         full(wg.shape), full(wu.shape), full(wd.shape)],
        [tok(block, d), full(wg.shape), full(wu.shape), full(wd.shape), full((1, d))],
        [sds((t, d), bf), sds(wg.shape, bf), sds(wu.shape, bf), sds(wd.shape, bf), sds((1, d), f32)],
        [pltpu.VMEM((t, d), bf)] + [pltpu.VMEM((t, ff), bf)] * 3 + [pltpu.VMEM((t, d), bf),
         pltpu.VMEM((1, d), f32)],
        2 * t * d * ff * 6, 12 * t * d, "ffn_bwd")(x, gate, up, g, gain, wg, wu, wd)


def z_shift(values, by):
    half = lax.axis_size("dp") // 2
    pairs = [(z * 2 + y, ((z + by) % half) * 2 + y) for z in range(half) for y in range(2)]
    return lax.ppermute(values, "dp", pairs)


def swapped(values, axis, bit):
    return lax.ppermute(values, axis, [(i, i ^ bit) for i in range(lax.axis_size(axis))])


def after(values, *others):
    return lax.optimization_barrier((values,) + others)[0]


def by_core(core, arrays):
    return jnp.where(core == 0, arrays[0], arrays[1])


def half_rows(core, matrix):
    half = matrix.shape[0] // 2
    return lax.dynamic_slice_in_dim(matrix, core * half, half, 0)


def fold_rows(matrix, unit):
    return jnp.concatenate(
        [matrix[at:at + unit] for at in range(0, matrix.shape[0], unit)], axis=1
    )


def gather_part(piece, place):
    z, y, core = place
    half = lax.axis_size("dp") // 2
    got = [piece] + [z_shift(piece, by) for by in range(1, half)]
    column = jnp.stack([lax.select_n((z - at) % half, *got) for at in range(half)])
    other = swapped(column, "dp", 1)
    both = jnp.stack([by_core(y, (column, other)), by_core(y, (other, column))], axis=1)
    peer = swapped(both, "section", 1)
    whole = jnp.stack([by_core(core, (both, peer)), by_core(core, (peer, both))], axis=2)
    return whole, got[-1]


def reduce_part(packed, place):
    z, y, core = place
    half = lax.axis_size("dp") // 2

    def added(*terms):
        total = terms[0].astype(f32)
        for term in terms[1:]:
            total = total + term.astype(f32)
        return total.astype(bf)

    def exchanged(values, index, axis):
        keep = lax.dynamic_index_in_dim(values, index, 0, keepdims=False)
        give = lax.dynamic_index_in_dim(values, 1 - index, 0, keepdims=False)
        return added(keep, swapped(give, axis, 1))

    chip = exchanged(packed, core, "section")
    column = exchanged(chip, y, "dp")
    terms = [lax.dynamic_index_in_dim(column, z, 0, keepdims=False)]
    for by in range(1, half):
        terms.append(
            z_shift(lax.dynamic_index_in_dim(column, (z + by) % half, 0, keepdims=False), by)
        )
    mine = added(*terms)
    return added(mine, swapped(mine, "section", 2))


def split_last(values, widths):
    parts, at = [], 0
    for width in widths:
        parts.append(values[..., at:at + width])
        at += width
    return parts


def pack_rows(grad, half, unit):
    rows, width = grad.shape
    tiles = rows // (4 * half * unit)
    split = grad.reshape(half, 2, 2, tiles, unit, width)
    return split.transpose(2, 1, 0, 4, 3, 5).reshape(2, 2, half, unit, tiles * width)


def pack_columns(grad, half, unit):
    rows, width = grad.shape
    tiles = rows // (2 * half * unit)
    split = grad.reshape(half, 2, tiles, unit, 2, width // 2)
    return split.transpose(4, 1, 0, 3, 2, 5).reshape(2, 2, half, unit, tiles * (width // 2))


def open_rows(packed, width):
    half, _, _, unit, n = packed.shape
    split = packed.reshape(half, 2, 2, unit, n // width, width)
    return split.transpose(0, 1, 2, 4, 3, 5).reshape(-1, width)


def open_columns(packed, width):
    half, _, _, unit, n = packed.shape
    tiles = n // (width // 2)
    split = packed.reshape(half, 2, 2, unit, tiles, width // 2)
    return split.transpose(0, 1, 4, 3, 2, 5).reshape(-1, width)


def bucket_onehot(seq_count, bucket_count):
    position = jnp.arange(seq_count, dtype=jnp.int32)
    offset = position[None, :] - position[:, None]
    distance = jnp.abs(offset)
    far_bucket = jnp.full(distance.shape, 8, jnp.int32)
    for threshold in limits:
        far_bucket = far_bucket + (distance >= threshold).astype(jnp.int32)
    bucket = jnp.where(distance < 8, distance, jnp.minimum(far_bucket, 15)) + 16 * (
        offset > 0
    ).astype(jnp.int32)
    return (bucket[:, :, None] == jnp.arange(bucket_count, dtype=jnp.int32)[None, None, :]).astype(f32)


def body(inputs, cotangent, segments, observed, q_weight, k_weight, v_weight, o_weight,
         gate_weight, up_weight, down_weight, gains, position_table):
    section = lax.axis_index("section")
    core = section % 2
    chip = section // 2
    dp = lax.axis_index("dp")
    half = lax.axis_size("dp") // 2
    place = (dp // 2, dp % 2, core)
    micro_count, row_count, seq_count, width = inputs.shape
    layers = q_weight.shape[0]
    inner, wide = q_weight.shape[2], gate_weight.shape[2]
    unit = q_weight.shape[1] // 4
    heads = position_table.shape[1]
    tokens = row_count * seq_count

    attn_n, ffn_n = 8 * inner + 0, 6 * wide
    attn_widths = (2 * inner,) * 3 + (3 * (width // 2),)
    ffn_widths = (2 * wide, 2 * wide, 4 * width)

    weights = []
    previous = None
    for layer in range(layers):
        o_half = lax.dynamic_slice_in_dim(o_weight[layer], core * (width // 2), width // 2, 1)
        piece = jnp.concatenate(
            [fold_rows(half_rows(core, w[layer]), unit) for w in (q_weight, k_weight, v_weight)]
            + [fold_rows(o_half, unit)], axis=1)
        if previous is not None:
            piece = after(piece, previous)
        whole, previous = gather_part(piece, place)
        parts = split_last(whole, attn_widths)
        attn = tuple(open_rows(part, inner) for part in parts[:3]) + (open_columns(parts[3], width),)
        piece = jnp.concatenate(
            [fold_rows(half_rows(core, w[layer]), unit) for w in (gate_weight, up_weight, down_weight)],
            axis=1)
        piece = after(piece, previous)
        whole, previous = gather_part(piece, place)
        parts = split_last(whole, ffn_widths)
        ffn = (open_rows(parts[0], wide), open_rows(parts[1], wide), open_rows(parts[2], width))
        weights.append((attn, ffn))

    gains_all = lax.all_gather(gains, "dp", axis=2, tiled=True).astype(f32)

    x = lax.dynamic_index_in_dim(inputs, section, 0, keepdims=False).reshape(tokens, width)
    grad = lax.dynamic_index_in_dim(cotangent, section, 0, keepdims=False).reshape(tokens, width)
    seg = lax.dynamic_index_in_dim(segments, section, 0, keepdims=False)
    obs = lax.dynamic_index_in_dim(observed, section, 0, keepdims=False)
    allowed = (seg[:, :, None] == seg[:, None, :]) & (obs[:, :, None] == 1)
    mask = jnp.where(allowed, 0.0, masked).astype(f32)
    mask = jnp.concatenate([mask, mask], axis=2)
    onehot = bucket_onehot(seq_count, position_table.shape[0])
    bias = jnp.einsum("ijb,bh->jhi", onehot, position_table.astype(f32), precision=lax.Precision.HIGHEST)
    bias = bias.reshape(seq_count, heads * seq_count)

    states, kept = [x], []
    for layer in range(layers):
        attn, ffn = weights[layer]
        out, *saved = attn_fwd(states[-1], mask, bias, gains_all[layer, 0][None], *attn, block=512)
        states.append(out)
        kept.append(saved)
        out, *saved = ffn_fwd(states[-1], gains_all[layer, 1][None], *ffn, block=512)
        states.append(out)
        kept.append(saved)
    outs = states[1:]

    grads = [None] * 4
    reduced = [None] * 4
    gain_terms = [None] * 4
    bias_terms = []
    for layer in reversed(range(layers)):
        attn, ffn = weights[layer]
        s = 2 * layer + 1
        grad, dg, du, dd, gain_terms[s] = ffn_bwd(
            states[s], *kept[s], grad, gains_all[layer, 1][None], *ffn, block=512)
        grads[s] = grad
        packed = jnp.concatenate([pack_rows(t, half, unit) for t in (dg, du, dd)], axis=-1)
        reduced[s] = reduce_part(packed, place)
        s = 2 * layer
        grad, dq, dk, dv, do, gain_terms[s], bias_term = attn_bwd(
            states[s], *kept[s], grad, gains_all[layer, 0][None], *attn, block=512)
        grads[s] = grad
        bias_terms.append(bias_term)
        packed = jnp.concatenate(
            [pack_rows(t, half, unit) for t in (dq, dk, dv)] + [pack_columns(do, half, unit)], axis=-1)
        reduced[s] = reduce_part(packed, place)

    def across(value, s):
        pairs = [(0, 2), (1, 3)] if s >= 2 else [(2, 0), (3, 1)]
        return lax.ppermute(value, "section", pairs)

    def placed(values, received):
        own = lax.select_n(section, *values)
        far = lax.select_n(section, *received)
        swap = lambda arrays: lax.select_n(section, arrays[1], arrays[0], arrays[3], arrays[2])
        near = swapped(jnp.stack([swap(values), swap(received)]), "section", 1)
        pool = (own, near[0], far, near[1])
        full = jnp.stack([lax.select_n(section ^ m, *pool) for m in range(micro_count)])
        return full.reshape(1, micro_count, row_count, seq_count, width)

    section_outputs = placed(outs, [across(outs[s], s) for s in range(4)])
    section_grads = placed(grads, [across(grads[s], s) for s in range(4)])

    both = [jnp.stack([by_core(core, (r, p)), by_core(core, (p, r))])
            for r, p in ((r, swapped(r, "section", 1)) for r in reduced)]

    def rows_out(part, columns):
        split = part.reshape(2, unit, part.shape[2] // columns, columns)
        return split.transpose(0, 2, 1, 3).reshape(-1, columns).astype(f32)

    def columns_out(part, columns):
        tiles = part.shape[2] // (columns // 2)
        split = part.reshape(2, unit, tiles, columns // 2)
        return split.transpose(2, 1, 0, 3).reshape(-1, columns).astype(f32)

    attn_parts = [split_last(both[s], attn_widths) for s in (0, 2)]
    ffn_parts = [split_last(both[s], ffn_widths) for s in (1, 3)]
    q_grad, k_grad, v_grad = (jnp.stack([rows_out(p[i], inner) for p in attn_parts]) for i in range(3))
    o_grad = jnp.stack([columns_out(p[3], width) for p in attn_parts])
    gate_grad, up_grad = (jnp.stack([rows_out(p[i], wide) for p in ffn_parts]) for i in range(2))
    down_grad = jnp.stack([rows_out(p[2], width) for p in ffn_parts])

    bias_sum = (bias_terms[0] + bias_terms[1]).reshape(seq_count, heads, seq_count)
    table = jnp.einsum("ijb,jhi->bh", onehot, bias_sum, precision=lax.Precision.HIGHEST)
    gain_flat = jnp.concatenate([t.reshape(-1) for t in gain_terms])
    small = jnp.concatenate([gain_flat, table.reshape(-1)])
    pad = -small.shape[0] % 1024
    small = jnp.pad(small, (0, pad)).reshape(-1, 128)
    bit = 1
    while bit < lax.axis_size("dp"):
        small = small + swapped(small, "dp", bit)
        bit *= 2
    small = small + swapped(small, "section", 1)
    small = small + swapped(small, "section", 2)
    small = small.reshape(-1)
    shard = gains.shape[2]
    gains_grad = lax.dynamic_slice_in_dim(
        small[:gain_flat.shape[0]].reshape(layers, 2, width), dp * shard, shard, 2)
    table_grad = small[gain_flat.shape[0]:gain_flat.shape[0] + table.size].reshape(table.shape)
    return (section_outputs, section_grads, q_grad, k_grad, v_grad, o_grad, gate_grad, up_grad,
            down_grad, gains_grad, table_grad)


def solution(mesh):
    rows4 = P(None, "dp", None, None)
    rows3 = P(None, "dp", None)
    staged = P("section", None, "dp", None, None)
    return jax.shard_map(
        body,
        mesh=mesh,
        in_specs=(rows4, rows4) + (rows3,) * 9 + (P(None, None, "dp"), P()),
        out_specs=(staged, staged) + (rows3,) * 7 + (P(None, None, "dp"), P()),
        check_vma=False,
    )
```

time: 2040 us -> 589 us (0.29)
  local copies, waits for them, and re-layouts: 690 us -> 152 us
  waiting for transfers between devices: 501 us -> 158 us
  other arithmetic: 335 us -> 58.9 us
  matrix products: 203 us -> 0.9 us
  blocking collectives: 207 us -> 31.1 us
  Pallas kernels: 0 us -> 92 us
  starting transfers between devices: 25.2 us -> 88.1 us
  loops' own time: 47.6 us -> 0 us
    reduce_scatter x7 -> x0, waiting for transfers between devices: 436 us -> none  [the longest x1 65.3 us: body(): lax.psum_scatter(grad_sums[5].astype(jnp.bfloat16), 'dp', scatter_dimensi...]
    dynamic_slice x152 -> x3, local copies, waits for them, and re-layouts: 239 us -> 5.32 us  [the longest x1 2.35 us: body(): lax.dynamic_index_in_dim(cotangent, section, 0, keepdims=False)]
    dot_general x78 -> x2, matrix products: 203 us -> 0.9 us  [the longest x1 0.63 us: body(): jnp.einsum('ijb,jhi->bh', onehot, bias_sum, precision=lax.Precision.HIGHEST)]
    dynamic_update_slice x56 -> x0, other arithmetic: 162 us -> none  [the longest x49 156 us: store_slot(): lax.dynamic_update_index_in_dim(buffer, jnp.where(active, new_value, prev...]
    all_gather x5 -> x1, blocking collectives: 167 us -> 31.1 us  [body(): gains_all = lax.all_gather(gains, 'dp', axis=2, tiled=True).astype(f32)]
    broadcast_in_dim x98 -> x0, local copies, waits for them, and re-layouts: 120 us -> none  [the longest x14 35.9 us: body(): wide_float = jnp.zeros((row_count, seq_count, ffn_width), jnp.float32)]
    ppermute x14 -> x63, waiting for transfers between devices: 65.2 us -> 158 us  [the longest x8 74.3 us: across(): return lax.ppermute(value, 'section', pairs)]
    pallas_call x0 -> x8, Pallas kernels: none -> 92 us  [the longest x2 40.6 us: ffn_bwd(): call(ffn_bwd_kernel, t // block, [tok(block, d), tok(block, ff), tok(bloc...]
  transfers between devices with their start and end apart: 25 -> 63, of which waited for: 11 -> 25; matrix products, arithmetic and copies ran while one was open for 29% -> 33% of each run, Pallas kernels for 0% -> 16%
where the time goes in v1:
time: 589 us; the launch traced here: 584 us
  waiting for transfers between devices  158 us (27%)
  local copies, waits for them, and re-layouts  152 us (26%)
  Pallas kernels  92 us (16%)
  starting transfers between devices  88.1 us (15%)
  other arithmetic  58.9 us (10%)
  blocking collectives  31.1 us (5%)
    ppermute x8, waiting for transfers between devices, across(): return lax.ppermute(value, 'section', pairs)  74.3 us
    ppermute x31, waiting for transfers between devices, swapped(): lax.ppermute(values, axis, [(i, i ^ bit) for i in range(lax.axis_size(axi...  46.4 us
    ppermute x24, starting transfers between devices, z_shift(): return lax.ppermute(values, 'dp', pairs)  40.9 us
    pallas_call x2, Pallas kernels, ffn_bwd(): call(ffn_bwd_kernel, t // block, [tok(block, d), tok(block, ff), tok(bloc...  40.6 us
    ppermute x24, waiting for transfers between devices, z_shift(): return lax.ppermute(values, 'dp', pairs)  37.1 us
    all_gather x1, blocking collectives, body(): gains_all = lax.all_gather(gains, 'dp', axis=2, tiled=True).astype(f32)  31.1 us
    reshape x24, local copies, waits for them, and re-layouts, open_rows(): split = packed.reshape(half, 2, 2, unit, n // width, width)  31.1 us
    ppermute x31, starting transfers between devices, swapped(): lax.ppermute(values, axis, [(i, i ^ bit) for i in range(lax.axis_size(axi...  30.8 us
  transfers between devices with their start and end apart: 63, of which 25 were waited for; matrix products, arithmetic and copies ran while one was open for 33% of the time, Pallas kernels for 16%

profile of v1, /device:TPU:0, one launch (start us, length us, event | category | flops | bytes accessed | tf_op | source)
XLA Modules:
  0.0 583.7 jit_solution(464635509955636316)
XLA Ops:
  4.3 5.1 collective-permute-start.2
  15.7 31.1 %all_gather.3 = bf16[2,2,512]{1,0,2:T(2,128)(2,1)S(1)} all-gather(bf16[2,2,64]{1,0,2:T(2,128)(2,1)S(1)} %copy.172), channel_id=1, replica_groups=mesh['section'=4,'dp'=8] {'dp'}, dimensions={2}, use_global_device_ids=true | all-gather | bytes 4608 | tf_op jit(solution)/shard_map/all_gather | solution.py:443
  46.9 6.8 %slice_reduce_fusion = (f32[512]{0:T(512)}, f32[512]{0:T(512)}, f32[512]{0:T(512)}, f32[512]{0:T(512)}) fusion(f32[2,2,512]{1,0,2:T(2,128)S(1)} %convert_element_type.520), kind=kLoop, calls=%fused_computation.145 | loop fusion | bytes 16384 | tf_op jit(solution)/shard_map/slice | solution.py:462
  59.5 2.9 collective-permute-start.3
  62.3 4.6 collective-permute-done.7
  67.5 2.7 collective-permute-start.10
  70.2 3.0 collective-permute-start.11
  73.1 7.0 %collective-permute-done.6 = bf16[16,6144]{1,0:T(8,128)(2,1)S(1)} collective-permute-done((bf16[16,6144]{1,0:T(8,128)(2,1)S(1)}, bf16[16,6144]{1,0:T(8,128)(2,1)S(1)}, u32[]{:S(2)}, u32[]{:S(2)}) %collective-permute-start.6) | collective-permute-done | bytes 196640 | tf_op jit(solution)/shard_map/ppermute | solution.py:291
  80.4 3.5 collective-permute-start.8
  84.4 3.6 collective-permute-start.17
  88.2 3.0 collective-permute-start.13
  91.6 3.2 collective-permute-done.16
  97.0 6.7 %collective-permute-done.13 = bf16[4,16,3072]{2,1,0:T(8,128)(2,1)S(1)} collective-permute-done((bf16[4,16,3072]{2,1,0:T(8,128)(2,1)S(1)}, bf16[4,16,3072]{2,1,0:T(8,128)(2,1)S(1)}, u32[]{:S(2)}, u32[]{:S(2)}) %collective-permute-start.13) | collective-permute-done | bytes 393248 | tf_op jit(solution)/shard_map/ppermute | solution.py:295
  115.2 6.9 %attn_fwd.2 = (bf16[1024,512]{1,0:T(8,128)(2,1)}, bf16[1024,384]{1,0:T(8,128)(2,1)}, bf16[1024,384]{1,0:T(8,128)(2,1)}, bf16[1024,384]{1,0:T(8,128)(2,1)}, bf16[...) custom-call(bf16[1024,512]{1,0:T(8,128)(2,1)} %bitcast.579, f32[16,64,128]{2,1,0:T(8,128)} %pad_maximum_fusion.12.mask_ref, ...), custom_call_target="tpu_custom_call" | custom-call | flops 1610612736 | bytes 2097152 | tf_op jit(solution)/shard_map/attn_fwd/pallas_call | solution.py:242
  157.8 6.7 %ffn_fwd.2 = (bf16[1024,512]{1,0:T(8,128)(2,1)}, bf16[1024,1024]{1,0:T(8,128)(2,1)}, bf16[1024,1024]{1,0:T(8,128)(2,1)}) custom-call(bf16[1024,512]{1,0:T(8,128)(2,1)} %get-tuple-element.56.x_ref, f32[1,512]{1,0:T(1,128)} %bitcast.651, bf16[512,1024]{1,0:T(8,128)(2,1)} %bitcast.585, bf16[512,1024]{1,0:T(8,128)(2,1)} %bitcast.587, bf16[1024,512]{1,0:T(8,128)(2,1)} %bitcast.589), custom_call_target="tpu_custom_call" | custom-call | flops 3221225472 | bytes 2097152 | tf_op jit(solution)/shard_map/ffn_fwd/pallas_call | solution.py:268
  164.5 6.8 %attn_fwd.3 = (bf16[1024,512]{1,0:T(8,128)(2,1)}, bf16[1024,384]{1,0:T(8,128)(2,1)}, bf16[1024,384]{1,0:T(8,128)(2,1)}, bf16[1024,384]{1,0:T(8,128)(2,1)}, bf16[...) custom-call(bf16[1024,512]{1,0:T(8,128)(2,1)} %get-tuple-element.58.x_ref, f32[16,64,128]{2,1,0:T(8,128)} %pad_maximum_fusion.12.mask_ref, ...), custom_call_target="tpu_custom_call" | custom-call | flops 1610612736 | bytes 2097152 | tf_op jit(solution)/shard_map/attn_fwd/pallas_call | solution.py:242
  181.4 6.7 %ffn_fwd.3 = (bf16[1024,512]{1,0:T(8,128)(2,1)}, bf16[1024,1024]{1,0:T(8,128)(2,1)}, bf16[1024,1024]{1,0:T(8,128)(2,1)}) custom-call(bf16[1024,512]{1,0:T(8,128)(2,1)} %get-tuple-element.60.x_ref, f32[1,512]{1,0:T(1,128)} %bitcast.655, bf16[512,1024]{1,0:T(8,128)(2,1)} %bitcast.594, bf16[512,1024]{1,0:T(8,128)(2,1)} %bitcast.596, bf16[1024,512]{1,0:T(8,128)(2,1)} %bitcast.598), custom_call_target="tpu_custom_call" | custom-call | flops 3221225472 | bytes 2097152 | tf_op jit(solution)/shard_map/ffn_fwd/pallas_call | solution.py:268
  188.1 25.8 %ffn_bwd.2 = (bf16[1024,512]{1,0:T(8,128)(2,1)}, bf16[512,1024]{1,0:T(8,128)(2,1)}, bf16[512,1024]{1,0:T(8,128)(2,1)}, bf16[1024,512]{1,0:T(8,128)(2,1)}, f32[1,512]{1,0:T(1,128)}) custom-call(bf16[1024,512]{1,0:T(8,128)(2,1)} %get-tuple-element.60.x_ref, bf16[1024,1024]{1,0:T(8,128)(2,1)} %get-tuple-element.75.gate_ref, ...), custom_call_target="tpu_custom_call" | custom-call | flops 6442450944 | bytes 6291456 | tf_op jit(solution)/shard_map/ffn_bwd/pallas_call | solution.py:278
  213.9 11.9 %attn_bwd.2 = (bf16[1024,512]{1,0:T(8,128)(2,1)}, bf16[512,384]{1,0:T(8,128)(2,1)}, bf16[512,384]{1,0:T(8,128)(2,1)}, bf16[512,384]{1,0:T(8,128)(2,1)}, bf16[384...) custom-call(bf16[1024,512]{1,0:T(8,128)(2,1)} %get-tuple-element.58.x_ref, ...), custom_call_target="tpu_custom_call" | custom-call | flops 3221225472 | bytes 6291456 | tf_op jit(solution)/shard_map/attn_bwd/pallas_call | solution.py:253
  225.8 14.9 %ffn_bwd.3 = (bf16[1024,512]{1,0:T(8,128)(2,1)}, bf16[512,1024]{1,0:T(8,128)(2,1)}, bf16[512,1024]{1,0:T(8,128)(2,1)}, bf16[1024,512]{1,0:T(8,128)(2,1)}, f32[1,512]{1,0:T(1,128)}) custom-call(bf16[1024,512]{1,0:T(8,128)(2,1)} %get-tuple-element.56.x_ref, bf16[1024,1024]{1,0:T(8,128)(2,1)} %get-tuple-element.68.gate_ref, ...), custom_call_target="tpu_custom_call" | custom-call | flops 6442450944 | bytes 6291456 | tf_op jit(solution)/shard_map/ffn_bwd/pallas_call | solution.py:278
  242.0 12.3 %attn_bwd.3 = (bf16[1024,512]{1,0:T(8,128)(2,1)}, bf16[512,384]{1,0:T(8,128)(2,1)}, bf16[512,384]{1,0:T(8,128)(2,1)}, bf16[512,384]{1,0:T(8,128)(2,1)}, bf16[384...) custom-call(bf16[1024,512]{1,0:T(8,128)(2,1)} %bitcast.580, bf16[1024,384]{1,0:T(8,128)(2,1)} %get-tuple-element.63.q_ref, ...), custom_call_target="tpu_custom_call" | custom-call | flops 3221225472 | bytes 6291456 | tf_op jit(solution)/shard_map/attn_bwd/pallas_call | solution.py:253
  263.2 2.6 reshape.651
  265.8 3.1 copy.241
  271.5 3.3 copy.240
  274.8 2.8 reshape.655
  282.0 2.6 reshape.657
  284.6 3.1 copy.238
  287.7 2.6 reshape.659
  330.1 5.8 collective-permute-start.62
  339.5 3.6 collective-permute-start.28
  350.6 16.2 %collective-permute-done.28 = bf16[1024,512]{1,0:T(8,128)(2,1)S(1)} collective-permute-done((bf16[1024,512]{1,0:T(8,128)(2,1)}, bf16[1024,512]{1,0:T(8,128)(2,1)S(1)}, u32[]{:S(2)}, u32[]{:S(2)}) %collective-permute-start.28) | collective-permute-done | bytes 1048608 | tf_op jit(solution)/shard_map/ppermute | solution.py:490
  366.8 4.5 collective-permute-start.22
  371.5 17.7 %collective-permute-done.27 = bf16[1024,512]{1,0:T(8,128)(2,1)S(1)} collective-permute-done((bf16[1024,512]{1,0:T(8,128)(2,1)S(1)}, bf16[1024,512]{1,0:T(8,128)(2,1)S(1)}, u32[]{:S(2)}, u32[]{:S(2)}) %collective-permute-start.27) | collective-permute-done | bytes 1048608 | tf_op jit(solution)/shard_map/ppermute | solution.py:490
  391.4 20.3 %collective-permute-done.23 = bf16[1024,512]{1,0:T(8,128)(2,1)S(1)} collective-permute-done((bf16[1024,512]{1,0:T(8,128)(2,1)S(1)}, bf16[1024,512]{1,0:T(8,128)(2,1)S(1)}, u32[]{:S(2)}, u32[]{:S(2)}) %collective-permute-start.23) | collective-permute-done | bytes 1048608 | tf_op jit(solution)/shard_map/ppermute | solution.py:490
  413.7 20.0 %collective-permute-done.22 = bf16[1024,512]{1,0:T(8,128)(2,1)S(1)} collective-permute-done((bf16[1024,512]{1,0:T(8,128)(2,1)S(1)}, bf16[1024,512]{1,0:T(8,128)(2,1)S(1)}, u32[]{:S(2)}, u32[]{:S(2)}) %collective-permute-start.22) | collective-permute-done | bytes 1048608 | tf_op jit(solution)/shard_map/ppermute | solution.py:490
  439.6 2.6 collective-permute-start.33
  445.5 4.1 collective-permute-done.33
  449.5 3.8 collective-permute-start.41
  453.5 4.7 collective-permute-done.40
  494.3 16.4 %collective-permute-done.45 = bf16[4,16,6144]{2,1,0:T(8,128)(2,1)S(1)} collective-permute-done((bf16[4,16,6144]{2,1,0:T(8,128)(2,1)S(1)}, bf16[4,16,6144]{2,1,0:T(8,128)(2,1)S(1)}, u32[]{:S(2)}, u32[]{:S(2)}) %collective-permute-start.45) | collective-permute-done | bytes 786464 | tf_op jit(solution)/shard_map/ppermute | solution.py:295
  512.4 3.2 collective-permute-start.47
  515.6 11.2 %collective-permute-done.52 = bf16[4,16,6144]{2,1,0:T(8,128)(2,1)S(1)} collective-permute-done((bf16[4,16,6144]{2,1,0:T(8,128)(2,1)S(1)}, bf16[4,16,6144]{2,1,0:T(8,128)(2,1)S(1)}, u32[]{:S(2)}, u32[]{:S(2)}) %collective-permute-start.52) | collective-permute-done | bytes 786464 | tf_op jit(solution)/shard_map/ppermute | solution.py:295
  526.8 3.9 collective-permute-start.48
  531.7 4.5 collective-permute-done.48
  536.1 4.3 collective-permute-start.55
  542.6 5.3 collective-permute-done.54
  549.9 3.8 collective-permute-done.56
  569.9 3.0 select_select_fusion.3
  (469 shorter events, 226.7 us)
Async XLA Ops:
  4.3 53.0 %collective-permute-start.2 = (bf16[16,3072]{1,0:T(8,128)(2,1)S(1)}, bf16[16,3072]{1,0:T(8,128)(2,1)S(1)}, u32[]{:S(2)}, u32[]{:S(2)}) collective-permute-start(bf16[16,3072]{1,0:T(8,128)(2,1)S(1)} %constant_dynamic-update-slice_fusion), channel_id=1, source_target_pairs={{0,6},{1,7},{2,0},{3,1},{4,2},{5,3},{6,4},{7,5},{8,14},{9,15},{10,... | collective-permute-start | bytes 294920 | tf_op jit(solution)/shard_map/ppermute | solution.py:291
  9.4 49.9 %collective-permute-start = (bf16[16,3072]{1,0:T(8,128)(2,1)S(1)}, bf16[16,3072]{1,0:T(8,128)(2,1)S(1)}, u32[]{:S(2)}, u32[]{:S(2)}) collective-permute-start(bf16[16,3072]{1,0:T(8,128)(2,1)S(1)} %constant_dynamic-update-slice_fusion), channel_id=1, source_target_pairs={{0,2},{1,3},{2,4},{3,5},{4,6},{5,7},{6,0},{7,1},{8,10},{9,11},{10,... | collective-permute-start | bytes 294920 | tf_op jit(solution)/shard_map/ppermute | solution.py:291
  9.4 49.9 %collective-permute-start.1 = (bf16[16,3072]{1,0:T(8,128)(2,1)S(1)}, bf16[16,3072]{1,0:T(8,128)(2,1)S(1)}, u32[]{:S(2)}, u32[]{:S(2)}) collective-permute-start(bf16[16,3072]{1,0:T(8,128)(2,1)S(1)} %constant_dynamic-update-slice_fusion), channel_id=1, source_target_pairs={{0,4},{1,5},{2,6},{3,7},{4,0},{5,1},{6,2},{7,3},{8,12},{9,13},{10,... | collective-permute-start | bytes 294920 | tf_op jit(solution)/shard_map/ppermute | solution.py:291
  57.3 9.6 %collective-permute-start.7 = (bf16[16,6144]{1,0:T(8,128)(2,1)S(1)}, bf16[16,6144]{1,0:T(8,128)(2,1)S(1)}, u32[]{:S(2)}, u32[]{:S(2)}) collective-permute-start(bf16[16,6144]{1,0:T(8,128)(2,1)S(1)} %constant_dynamic-update-slice_fusion.9), channel_id=1, source_target_pairs={{0,6},{1,7},{2,0},{3,1},{4,2},{5,3},{6,4},{7,5},{8,14},{9,15},{10,... | collective-permute-start | bytes 589832 | tf_op jit(solution)/shard_map/ppermute | solution.py:291
  57.9 12.3 %collective-permute-start.5 = (bf16[16,6144]{1,0:T(8,128)(2,1)S(1)}, bf16[16,6144]{1,0:T(8,128)(2,1)S(1)}, u32[]{:S(2)}, u32[]{:S(2)}) collective-permute-start(bf16[16,6144]{1,0:T(8,128)(2,1)S(1)} %constant_dynamic-update-slice_fusion.9), channel_id=1, source_target_pairs={{0,2},{1,3},{2,4},{3,5},{4,6},{5,7},{6,0},{7,1},{8,10},{9,11},{10,... | collective-permute-start | bytes 589832 | tf_op jit(solution)/shard_map/ppermute | solution.py:291
  59.3 20.9 %collective-permute-start.6 = (bf16[16,6144]{1,0:T(8,128)(2,1)S(1)}, bf16[16,6144]{1,0:T(8,128)(2,1)S(1)}, u32[]{:S(2)}, u32[]{:S(2)}) collective-permute-start(bf16[16,6144]{1,0:T(8,128)(2,1)S(1)} %constant_dynamic-update-slice_fusion.9), channel_id=1, source_target_pairs={{0,4},{1,5},{2,6},{3,7},{4,0},{5,1},{6,2},{7,3},{8,12},{9,13},{10,... | collective-permute-start | bytes 589832 | tf_op jit(solution)/shard_map/ppermute | solution.py:291
  59.5 28.7 %collective-permute-start.3 = (bf16[4,16,3072]{2,1,0:T(8,128)(2,1)S(1)}, bf16[4,16,3072]{2,1,0:T(8,128)(2,1)S(1)}, u32[]{:S(2)}, u32[]{:S(2)}) collective-permute-start(bf16[4,16,3072]{2,1,0:T(8,128)(2,1)S(1)} %pad_maximum_fusion.15), channel_id=1, source_target_pairs={{0,1},{1,0},{2,3},{3,2},{4,5},{5,4},{6,7},{7,6},{8,9},{9,8},{10,11... | collective-permute-start | bytes 1179656 | tf_op jit(solution)/shard_map/ppermute | solution.py:295
  66.9 17.0 %collective-permute-start.12 = (bf16[16,3072]{1,0:T(8,128)(2,1)S(1)}, bf16[16,3072]{1,0:T(8,128)(2,1)S(1)}, u32[]{:S(2)}, u32[]{:S(2)}) collective-permute-start(bf16[16,3072]{1,0:T(8,128)(2,1)S(1)} %constant_dynamic-update-slice_fusion.17), channel_id=1, source_target_pairs={{0,6},{1,7},{2,0},{3,1},{4,2},{5,3},{6,4},{7,5},{8,14},{9,15},{10,... | collective-permute-start | bytes 294920 | tf_op jit(solution)/shard_map/ppermute | solution.py:291
  67.5 16.4 %collective-permute-start.10 = (bf16[16,3072]{1,0:T(8,128)(2,1)S(1)}, bf16[16,3072]{1,0:T(8,128)(2,1)S(1)}, u32[]{:S(2)}, u32[]{:S(2)}) collective-permute-start(bf16[16,3072]{1,0:T(8,128)(2,1)S(1)} %constant_dynamic-update-slice_fusion.17), channel_id=1, source_target_pairs={{0,2},{1,3},{2,4},{3,5},{4,6},{5,7},{6,0},{7,1},{8,10},{9,11},{10,... | collective-permute-start | bytes 294920 | tf_op jit(solution)/shard_map/ppermute | solution.py:291
  70.2 14.2 %collective-permute-start.11 = (bf16[16,3072]{1,0:T(8,128)(2,1)S(1)}, bf16[16,3072]{1,0:T(8,128)(2,1)S(1)}, u32[]{:S(2)}, u32[]{:S(2)}) collective-permute-start(bf16[16,3072]{1,0:T(8,128)(2,1)S(1)} %constant_dynamic-update-slice_fusion.17), channel_id=1, source_target_pairs={{0,4},{1,5},{2,6},{3,7},{4,0},{5,1},{6,2},{7,3},{8,12},{9,13},{10,... | collective-permute-start | bytes 294920 | tf_op jit(solution)/shard_map/ppermute | solution.py:291
  80.4 24.6 %collective-permute-start.8 = (bf16[4,16,6144]{2,1,0:T(8,128)(2,1)S(1)}, bf16[4,16,6144]{2,1,0:T(8,128)(2,1)S(1)}, u32[]{:S(2)}, u32[]{:S(2)}) collective-permute-start(bf16[4,16,6144]{2,1,0:T(8,128)(2,1)S(1)} %pad_maximum_fusion.9), channel_id=1, source_target_pairs={{0,1},{1,0},{2,3},{3,2},{4,5},{5,4},{6,7},{7,6},{8,9},{9,8},{10,11... | collective-permute-start | bytes 2359304 | tf_op jit(solution)/shard_map/ppermute | solution.py:295
  83.9 10.8 %collective-permute-start.16 = (bf16[16,6144]{1,0:T(8,128)(2,1)S(1)}, bf16[16,6144]{1,0:T(8,128)(2,1)S(1)}, u32[]{:S(2)}, u32[]{:S(2)}) collective-permute-start(bf16[16,6144]{1,0:T(8,128)(2,1)S(1)} %constant_dynamic-update-slice_fusion.26), channel_id=1, source_target_pairs={{0,4},{1,5},{2,6},{3,7},{4,0},{5,1},{6,2},{7,3},{8,12},{9,13},{10,... | collective-permute-start | bytes 589832 | tf_op jit(solution)/shard_map/ppermute | solution.py:291
  84.4 10.4 %collective-permute-start.17 = (bf16[16,6144]{1,0:T(8,128)(2,1)S(1)}, bf16[16,6144]{1,0:T(8,128)(2,1)S(1)}, u32[]{:S(2)}, u32[]{:S(2)}) collective-permute-start(bf16[16,6144]{1,0:T(8,128)(2,1)S(1)} %constant_dynamic-update-slice_fusion.26), channel_id=1, source_target_pairs={{0,6},{1,7},{2,0},{3,1},{4,2},{5,3},{6,4},{7,5},{8,14},{9,15},{10,... | collective-permute-start | bytes 589832 | tf_op jit(solution)/shard_map/ppermute | solution.py:291
  88.2 15.6 %collective-permute-start.13 = (bf16[4,16,3072]{2,1,0:T(8,128)(2,1)S(1)}, bf16[4,16,3072]{2,1,0:T(8,128)(2,1)S(1)}, u32[]{:S(2)}, u32[]{:S(2)}) collective-permute-start(bf16[4,16,3072]{2,1,0:T(8,128)(2,1)S(1)} %pad_maximum_fusion.16), channel_id=1, source_target_pairs={{0,1},{1,0},{2,3},{3,2},{4,5},{5,4},{6,7},{7,6},{8,9},{9,8},{10,11... | collective-permute-start | bytes 1179656 | tf_op jit(solution)/shard_map/ppermute | solution.py:295
  91.6 15.3 %collective-permute-start.4 = (bf16[4,2,16,3072]{3,2,0,1:T(8,128)(2,1)S(1)}, bf16[4,2,16,3072]{3,2,0,1:T(8,128)(2,1)S(1)}, u32[]{:S(2)}, u32[]{:S(2)}) collective-permute-start(bf16[4,2,16,3072]{3,2,0,1:T(8,128)(2,1)S(1)} %pad_maximum_fusion.8), channel_id=1, source_target_pairs={{0,8},{8,0},{16,24},{24,16},{1,9},{9,1},{17,25},{25,17},{2,10},{10... | collective-permute-start | bytes 2359304 | tf_op jit(solution)/shard_map/ppermute | solution.py:295
  96.0 27.4 %collective-permute-start.18 = (bf16[4,16,6144]{2,1,0:T(8,128)(2,1)}, bf16[4,16,6144]{2,1,0:T(8,128)(2,1)}, u32[]{:S(2)}, u32[]{:S(2)}) collective-permute-start(bf16[4,16,6144]{2,1,0:T(8,128)(2,1)} %pad_maximum_fusion.11), channel_id=1, source_target_pairs={{0,1},{1,0},{2,3},{3,2},{4,5},{5,4},{6,7},{7,6},{8,9},{9,8},{10,11... | collective-permute-start | bytes 2359304 | tf_op jit(solution)/shard_map/ppermute | solution.py:295
  104.9 21.2 %collective-permute-start.14 = (bf16[4,2,16,3072]{3,2,0,1:T(8,128)(2,1)}, bf16[4,2,16,3072]{3,2,0,1:T(8,128)(2,1)}, u32[]{:S(2)}, u32[]{:S(2)}) collective-permute-start(bf16[4,2,16,3072]{3,2,0,1:T(8,128)(2,1)} %pad_maximum_fusion.10), channel_id=1, source_target_pairs={{0,8},{8,0},{16,24},{24,16},{1,9},{9,1},{17,25},{25,17},{2,10},{10... | collective-permute-start | bytes 2359304 | tf_op jit(solution)/shard_map/ppermute | solution.py:295
  106.5 38.6 %collective-permute-start.9 = (bf16[4,2,16,6144]{3,2,0,1:T(8,128)(2,1)}, bf16[4,2,16,6144]{3,2,0,1:T(8,128)(2,1)}, u32[]{:S(2)}, u32[]{:S(2)}) collective-permute-start(bf16[4,2,16,6144]{3,2,0,1:T(8,128)(2,1)} %pad_maximum_fusion.4), channel_id=1, source_target_pairs={{0,8},{8,0},{16,24},{24,16},{1,9},{9,1},{17,25},{25,17},{2,10},{10... | collective-permute-start | bytes 4718600 | tf_op jit(solution)/shard_map/ppermute | solution.py:295
  122.1 269.1 %collective-permute-start.21 = (bf16[1024,512]{1,0:T(8,128)(2,1)}, bf16[1024,512]{1,0:T(8,128)(2,1)}, u32[]{:S(2)}, u32[]{:S(2)}) collective-permute-start(bf16[1024,512]{1,0:T(8,128)(2,1)} %get-tuple-element.56.x_ref), channel_id=1, source_target_pairs={{16,0},{24,8},{17,1},{25,9},{18,2},{26,10},{19,3},{27,11},{20,4},{... | collective-permute-start | bytes 3145736 | tf_op jit(solution)/shard_map/ppermute | solution.py:490
  126.1 45.2 %collective-permute-start.19 = (bf16[4,2,16,6144]{3,2,0,1:T(8,128)(2,1)}, bf16[4,2,16,6144]{3,2,0,1:T(8,128)(2,1)}, u32[]{:S(2)}, u32[]{:S(2)}) collective-permute-start(bf16[4,2,16,6144]{3,2,0,1:T(8,128)(2,1)} %pad_maximum_fusion.5), channel_id=1, source_target_pairs={{0,8},{8,0},{16,24},{24,16},{1,9},{9,1},{17,25},{25,17},{2,10},{10... | collective-permute-start | bytes 4718600 | tf_op jit(solution)/shard_map/ppermute | solution.py:295
  240.7 108.6 %collective-permute-start.25 = (bf16[1024,512]{1,0:T(8,128)(2,1)}, bf16[1024,512]{1,0:T(8,128)(2,1)}, u32[]{:S(2)}, u32[]{:S(2)}) collective-permute-start(bf16[1024,512]{1,0:T(8,128)(2,1)} %get-tuple-element.79.g_ref), channel_id=1, source_target_pairs={{16,0},{24,8},{17,1},{25,9},{18,2},{26,10},{19,3},{27,11},{20,4},{... | collective-permute-start | bytes 3145736 | tf_op jit(solution)/shard_map/ppermute | solution.py:490
  256.6 57.4 %collective-permute-start.58 = (f32[24,128]{1,0:T(8,128)S(1)}, f32[24,128]{1,0:T(8,128)S(1)}, u32[]{:S(2)}, u32[]{:S(2)}) collective-permute-start(f32[24,128]{1,0:T(8,128)S(1)} %pad_bitcast_fusion), channel_id=1, source_target_pairs={{0,1},{1,0},{2,3},{3,2},{4,5},{5,4},{6,7},{7,6},{8,9},{9,8},{10,11... | collective-permute-start | bytes 36872 | tf_op jit(solution)/shard_map/ppermute | solution.py:295
  304.5 35.0 %collective-permute-start.30 = (bf16[2,4,16,3072]{3,2,1,0:T(8,128)(2,1)}, bf16[2,4,16,3072]{3,2,1,0:T(8,128)(2,1)}, u32[]{:S(2)}, u32[]{:S(2)}) collective-permute-start(bf16[2,4,16,3072]{3,2,1,0:T(8,128)(2,1)} %dynamic-slice_bitcast_fusion.5), channel_id=1, source_target_pairs={{0,8},{8,0},{16,24},{24,16},{1,9},{9,1},{17,25},{25,17},{2,10},{10... | collective-permute-start | bytes 2359304 | tf_op jit(solution)/shard_map/ppermute | solution.py:295
  306.0 41.8 %collective-permute-start.26 = (bf16[1024,512]{1,0:T(8,128)(2,1)}, bf16[1024,512]{1,0:T(8,128)(2,1)}, u32[]{:S(2)}, u32[]{:S(2)}) collective-permute-start(bf16[1024,512]{1,0:T(8,128)(2,1)} %get-tuple-element.80), channel_id=1, source_target_pairs={{16,0},{24,8},{17,1},{25,9},{18,2},{26,10},{19,3},{27,11},{20,4},{... | collective-permute-start | bytes 3145736 | tf_op jit(solution)/shard_map/ppermute | solution.py:490
  319.9 8.0 %collective-permute-start.60 = (f32[24,128]{1,0:T(8,128)S(1)}, f32[24,128]{1,0:T(8,128)S(1)}, u32[]{:S(2)}, u32[]{:S(2)}) collective-permute-start(f32[24,128]{1,0:T(8,128)S(1)} %fusion.91), channel_id=1, source_target_pairs={{0,4},{1,5},{2,6},{3,7},{4,0},{5,1},{6,2},{7,3},{8,12},{9,13},{10,... | collective-permute-start | bytes 36872 | tf_op jit(solution)/shard_map/ppermute | solution.py:295
  339.5 27.3 %collective-permute-start.28 = (bf16[1024,512]{1,0:T(8,128)(2,1)}, bf16[1024,512]{1,0:T(8,128)(2,1)S(1)}, u32[]{:S(2)}, u32[]{:S(2)}) collective-permute-start(bf16[1024,512]{1,0:T(8,128)(2,1)} %get-tuple-element.78.g_ref), channel_id=1, source_target_pairs={{0,16},{8,24},{1,17},{9,25},{2,18},{10,26},{3,19},{11,27},{4,20},{... | collective-permute-start | bytes 3145736 | tf_op jit(solution)/shard_map/ppermute | solution.py:490
  344.8 44.4 %collective-permute-start.27 = (bf16[1024,512]{1,0:T(8,128)(2,1)S(1)}, bf16[1024,512]{1,0:T(8,128)(2,1)S(1)}, u32[]{:S(2)}, u32[]{:S(2)}) collective-permute-start(bf16[1024,512]{1,0:T(8,128)(2,1)S(1)} %copy-done.20), channel_id=1, source_target_pairs={{0,16},{8,24},{1,17},{9,25},{2,18},{10,26},{3,19},{11,27},{4,20},{... | collective-permute-start | bytes 3145736 | tf_op jit(solution)/shard_map/ppermute | solution.py:490
  347.9 63.8 %collective-permute-start.23 = (bf16[1024,512]{1,0:T(8,128)(2,1)S(1)}, bf16[1024,512]{1,0:T(8,128)(2,1)S(1)}, u32[]{:S(2)}, u32[]{:S(2)}) collective-permute-start(bf16[1024,512]{1,0:T(8,128)(2,1)S(1)} %copy-done.14), channel_id=1, source_target_pairs={{0,16},{8,24},{1,17},{9,25},{2,18},{10,26},{3,19},{11,27},{4,20},{... | collective-permute-start | bytes 3145736 | tf_op jit(solution)/shard_map/ppermute | solution.py:490
  349.3 64.1 %collective-permute-start.20 = (bf16[1024,512]{1,0:T(8,128)(2,1)S(1)}, bf16[1024,512]{1,0:T(8,128)(2,1)S(1)}, u32[]{:S(2)}, u32[]{:S(2)}) collective-permute-start(bf16[1024,512]{1,0:T(8,128)(2,1)S(1)} %copy-done.11), channel_id=1, source_target_pairs={{16,0},{24,8},{17,1},{25,9},{18,2},{26,10},{19,3},{27,11},{20,4},{... | collective-permute-start | bytes 3145736 | tf_op jit(solution)/shard_map/ppermute | solution.py:490
  366.8 66.9 %collective-permute-start.22 = (bf16[1024,512]{1,0:T(8,128)(2,1)S(1)}, bf16[1024,512]{1,0:T(8,128)(2,1)S(1)}, u32[]{:S(2)}, u32[]{:S(2)}) collective-permute-start(bf16[1024,512]{1,0:T(8,128)(2,1)S(1)} %copy-done.17), channel_id=1, source_target_pairs={{0,16},{8,24},{1,17},{9,25},{2,18},{10,26},{3,19},{11,27},{4,20},{... | collective-permute-start | bytes 3145736 | tf_op jit(solution)/shard_map/ppermute | solution.py:490
  389.2 98.7 %collective-permute-start.44 = (bf16[2,4,16,6144]{3,2,1,0:T(8,128)(2,1)}, bf16[2,4,16,6144]{3,2,1,0:T(8,128)(2,1)}, u32[]{:S(2)}, u32[]{:S(2)}) collective-permute-start(bf16[2,4,16,6144]{3,2,1,0:T(8,128)(2,1)} %dynamic-slice_bitcast_fusion.1), channel_id=1, source_target_pairs={{0,8},{8,0},{16,24},{24,16},{1,9},{9,1},{17,25},{25,17},{2,10},{10... | collective-permute-start | bytes 4718600 | tf_op jit(solution)/shard_map/ppermute | solution.py:295
  391.2 100.9 %collective-permute-start.51 = (bf16[2,4,16,6144]{3,2,1,0:T(8,128)(2,1)}, bf16[2,4,16,6144]{3,2,1,0:T(8,128)(2,1)}, u32[]{:S(2)}, u32[]{:S(2)}) collective-permute-start(bf16[2,4,16,6144]{3,2,1,0:T(8,128)(2,1)} %dynamic-slice_bitcast_fusion), channel_id=1, source_target_pairs={{0,8},{8,0},{16,24},{24,16},{1,9},{9,1},{17,25},{25,17},{2,10},{10... | collective-permute-start | bytes 4718600 | tf_op jit(solution)/shard_map/ppermute | solution.py:295
  411.7 26.1 %collective-permute-start.31 = (bf16[4,16,3072]{2,1,0:T(8,128)(2,1)S(1)}, bf16[4,16,3072]{2,1,0:T(8,128)(2,1)S(1)}, u32[]{:S(2)}, u32[]{:S(2)}) collective-permute-start(bf16[4,16,3072]{2,1,0:T(8,128)(2,1)S(1)} %dynamic-slice_bitcast_fusion.7), channel_id=1, source_target_pairs={{0,1},{1,0},{2,3},{3,2},{4,5},{5,4},{6,7},{7,6},{8,9},{9,8},{10,11... | collective-permute-start | bytes 1179656 | tf_op jit(solution)/shard_map/ppermute | solution.py:295
  413.4 28.9 %collective-permute-start.38 = (bf16[4,16,3072]{2,1,0:T(8,128)(2,1)S(1)}, bf16[4,16,3072]{2,1,0:T(8,128)(2,1)S(1)}, u32[]{:S(2)}, u32[]{:S(2)}) collective-permute-start(bf16[4,16,3072]{2,1,0:T(8,128)(2,1)S(1)} %dynamic-slice_bitcast_fusion.6), channel_id=1, source_target_pairs={{0,1},{1,0},{2,3},{3,2},{4,5},{5,4},{6,7},{7,6},{8,9},{9,8},{10,11... | collective-permute-start | bytes 1179656 | tf_op jit(solution)/shard_map/ppermute | solution.py:295
  439.6 9.9 %collective-permute-start.33 = (bf16[16,3072]{1,0:T(8,128)(2,1)S(1)}, bf16[16,3072]{1,0:T(8,128)(2,1)S(1)}, u32[]{:S(2)}, u32[]{:S(2)}) collective-permute-start(bf16[16,3072]{1,0:T(8,128)(2,1)S(1)} %get-tuple-element.217), channel_id=1, source_target_pairs={{0,4},{1,5},{2,6},{3,7},{4,0},{5,1},{6,2},{7,3},{8,12},{9,13},{10,... | collective-permute-start | bytes 294920 | tf_op jit(solution)/shard_map/ppermute | solution.py:291
  449.5 8.7 %collective-permute-start.40 = (bf16[16,3072]{1,0:T(8,128)(2,1)S(1)}, bf16[16,3072]{1,0:T(8,128)(2,1)S(1)}, u32[]{:S(2)}, u32[]{:S(2)}) collective-permute-start(bf16[16,3072]{1,0:T(8,128)(2,1)S(1)} %get-tuple-element.220), channel_id=1, source_target_pairs={{0,4},{1,5},{2,6},{3,7},{4,0},{5,1},{6,2},{7,3},{8,12},{9,13},{10,... | collective-permute-start | bytes 294920 | tf_op jit(solution)/shard_map/ppermute | solution.py:291
  449.5 9.6 %collective-permute-start.41 = (bf16[16,3072]{1,0:T(8,128)(2,1)S(1)}, bf16[16,3072]{1,0:T(8,128)(2,1)S(1)}, u32[]{:S(2)}, u32[]{:S(2)}) collective-permute-start(bf16[16,3072]{1,0:T(8,128)(2,1)S(1)} %get-tuple-element.219), channel_id=1, source_target_pairs={{0,6},{1,7},{2,0},{3,1},{4,2},{5,3},{6,4},{7,5},{8,14},{9,15},{10,... | collective-permute-start | bytes 294920 | tf_op jit(solution)/shard_map/ppermute | solution.py:291
  453.4 116.5 %collective-permute-start.29 = (bf16[2,1024,512]{2,1,0:T(8,128)(2,1)}, bf16[2,1024,512]{2,1,0:T(8,128)(2,1)}, u32[]{:S(2)}, u32[]{:S(2)}) collective-permute-start(bf16[2,1024,512]{2,1,0:T(8,128)(2,1)} %pad_maximum_fusion.3), channel_id=1, source_target_pairs={{0,8},{8,0},{16,24},{24,16},{1,9},{9,1},{17,25},{25,17},{2,10},{10... | collective-permute-start | bytes 6291464 | tf_op jit(solution)/shard_map/ppermute | solution.py:295
  458.2 119.1 %collective-permute-start.24 = (bf16[2,1024,512]{2,1,0:T(8,128)(2,1)}, bf16[2,1024,512]{2,1,0:T(8,128)(2,1)S(1)}, u32[]{:S(2)}, u32[]{:S(2)}) collective-permute-start(bf16[2,1024,512]{2,1,0:T(8,128)(2,1)} %pad_maximum_fusion.2), channel_id=1, source_target_pairs={{0,8},{8,0},{16,24},{24,16},{1,9},{9,1},{17,25},{25,17},{2,10},{10... | collective-permute-start | bytes 6291464 | tf_op jit(solution)/shard_map/ppermute | solution.py:295
  490.3 20.4 %collective-permute-start.45 = (bf16[4,16,6144]{2,1,0:T(8,128)(2,1)S(1)}, bf16[4,16,6144]{2,1,0:T(8,128)(2,1)S(1)}, u32[]{:S(2)}, u32[]{:S(2)}) collective-permute-start(bf16[4,16,6144]{2,1,0:T(8,128)(2,1)S(1)} %dynamic-slice_bitcast_fusion.3), channel_id=1, source_target_pairs={{0,1},{1,0},{2,3},{3,2},{4,5},{5,4},{6,7},{7,6},{8,9},{9,8},{10,11... | collective-permute-start | bytes 2359304 | tf_op jit(solution)/shard_map/ppermute | solution.py:295
  494.0 32.9 %collective-permute-start.52 = (bf16[4,16,6144]{2,1,0:T(8,128)(2,1)S(1)}, bf16[4,16,6144]{2,1,0:T(8,128)(2,1)S(1)}, u32[]{:S(2)}, u32[]{:S(2)}) collective-permute-start(bf16[4,16,6144]{2,1,0:T(8,128)(2,1)S(1)} %dynamic-slice_bitcast_fusion.2), channel_id=1, source_target_pairs={{0,1},{1,0},{2,3},{3,2},{4,5},{5,4},{6,7},{7,6},{8,9},{9,8},{10,11... | collective-permute-start | bytes 2359304 | tf_op jit(solution)/shard_map/ppermute | solution.py:295
  511.0 20.0 %collective-permute-start.46 = (bf16[16,6144]{1,0:T(8,128)(2,1)S(1)}, bf16[16,6144]{1,0:T(8,128)(2,1)S(1)}, u32[]{:S(2)}, u32[]{:S(2)}) collective-permute-start(bf16[16,6144]{1,0:T(8,128)(2,1)S(1)} %get-tuple-element.187), channel_id=1, source_target_pairs={{0,2},{1,3},{2,4},{3,5},{4,6},{5,7},{6,0},{7,1},{8,10},{9,11},{10,... | collective-permute-start | bytes 589832 | tf_op jit(solution)/shard_map/ppermute | solution.py:291
  512.4 18.7 %collective-permute-start.47 = (bf16[16,6144]{1,0:T(8,128)(2,1)S(1)}, bf16[16,6144]{1,0:T(8,128)(2,1)S(1)}, u32[]{:S(2)}, u32[]{:S(2)}) collective-permute-start(bf16[16,6144]{1,0:T(8,128)(2,1)S(1)} %get-tuple-element.189), channel_id=1, source_target_pairs={{0,4},{1,5},{2,6},{3,7},{4,0},{5,1},{6,2},{7,3},{8,12},{9,13},{10,... | collective-permute-start | bytes 589832 | tf_op jit(solution)/shard_map/ppermute | solution.py:291
  526.8 9.3 %collective-permute-start.48 = (bf16[16,6144]{1,0:T(8,128)(2,1)S(1)}, bf16[16,6144]{1,0:T(8,128)(2,1)S(1)}, u32[]{:S(2)}, u32[]{:S(2)}) collective-permute-start(bf16[16,6144]{1,0:T(8,128)(2,1)S(1)} %get-tuple-element.188), channel_id=1, source_target_pairs={{0,6},{1,7},{2,0},{3,1},{4,2},{5,3},{6,4},{7,5},{8,14},{9,15},{10,... | collective-permute-start | bytes 589832 | tf_op jit(solution)/shard_map/ppermute | solution.py:291
  531.0 9.8 %collective-permute-start.53 = (bf16[16,6144]{1,0:T(8,128)(2,1)S(1)}, bf16[16,6144]{1,0:T(8,128)(2,1)S(1)}, u32[]{:S(2)}, u32[]{:S(2)}) collective-permute-start(bf16[16,6144]{1,0:T(8,128)(2,1)S(1)} %get-tuple-element.190), channel_id=1, source_target_pairs={{0,2},{1,3},{2,4},{3,5},{4,6},{5,7},{6,0},{7,1},{8,10},{9,11},{10,... | collective-permute-start | bytes 589832 | tf_op jit(solution)/shard_map/ppermute | solution.py:291
  531.1 16.8 %collective-permute-start.54 = (bf16[16,6144]{1,0:T(8,128)(2,1)S(1)}, bf16[16,6144]{1,0:T(8,128)(2,1)S(1)}, u32[]{:S(2)}, u32[]{:S(2)}) collective-permute-start(bf16[16,6144]{1,0:T(8,128)(2,1)S(1)} %get-tuple-element.192), channel_id=1, source_target_pairs={{0,4},{1,5},{2,6},{3,7},{4,0},{5,1},{6,2},{7,3},{8,12},{9,13},{10,... | collective-permute-start | bytes 589832 | tf_op jit(solution)/shard_map/ppermute | solution.py:291
  536.1 11.7 %collective-permute-start.55 = (bf16[16,6144]{1,0:T(8,128)(2,1)S(1)}, bf16[16,6144]{1,0:T(8,128)(2,1)S(1)}, u32[]{:S(2)}, u32[]{:S(2)}) collective-permute-start(bf16[16,6144]{1,0:T(8,128)(2,1)S(1)} %get-tuple-element.191), channel_id=1, source_target_pairs={{0,6},{1,7},{2,0},{3,1},{4,2},{5,3},{6,4},{7,5},{8,14},{9,15},{10,... | collective-permute-start | bytes 589832 | tf_op jit(solution)/shard_map/ppermute | solution.py:291
  540.9 8.9 %collective-permute-start.49 = (bf16[16,6144]{1,0:T(8,128)(2,1)S(1)}, bf16[16,6144]{1,0:T(8,128)(2,1)S(1)}, u32[]{:S(2)}, u32[]{:S(2)}) collective-permute-start(bf16[16,6144]{1,0:T(8,128)(2,1)S(1)} %fusion.25), channel_id=1, source_target_pairs={{0,16},{8,24},{16,0},{24,8},{1,17},{9,25},{17,1},{25,9},{2,18},{10... | collective-permute-start | bytes 589832 | tf_op jit(solution)/shard_map/ppermute | solution.py:295
  (76 other events, 424.7 us)

commit v2 on v1

v2 whole, which is shorter than its diff:
```python
import jax
import jax.numpy as jnp
from jax import lax
from jax.experimental import pallas as pl
from jax.experimental.pallas import tpu as pltpu
from jax.sharding import PartitionSpec as P

eps_norm = 1e-06
limits = (12, 16, 23, 32, 46, 64, 91)
masked = -1e30
bf = jnp.bfloat16
f32 = jnp.float32
vmem_limit = 60 * 1024 * 1024


def dot_nn(a, b):
    return lax.dot_general(a, b, (((1,), (0,)), ((), ())), preferred_element_type=f32)


def dot_nt(a, b):
    return lax.dot_general(a, b, (((1,), (1,)), ((), ())), preferred_element_type=f32)


def dot_tn(a, b):
    return lax.dot_general(a, b, (((0,), (0,)), ((), ())), preferred_element_type=f32)


def row_scale(x):
    return lax.rsqrt(jnp.mean(x * x, axis=-1, keepdims=True) + eps_norm)


def pair_parts(values):
    lane = lax.broadcasted_iota(jnp.int32, values.shape, 1)
    zero = jnp.zeros_like(values)
    return jnp.concatenate(
        [jnp.where(lane < 64, values, zero), jnp.where(lane < 64, zero, values)], axis=0
    )


def pair_pick(values):
    half = values.shape[0] // 2
    lane = lax.broadcasted_iota(jnp.int32, (half, values.shape[1]), 1)
    return jnp.where(lane < 64, values[:half], values[half:])


blocks = 16
block_rows = 32


def order_of(ids, z, other_y, other_core):
    return (z * 2 + (ids[1] ^ other_y)) * 2 + (ids[2] ^ other_core)


def open_attn(ids, parts, wqkv, wo):
    for at, ref in enumerate(parts):
        other_y, other_core = at % 2, at // 2
        for z in range(4):
            place = order_of(ids, z, other_y, other_core)
            wqkv[pl.ds(pl.multiple_of(place * 32, 32), 32), :] = ref[z, :, :1152]
            shard = z * 2 + (ids[1] ^ other_y)
            core = ids[2] ^ other_core
            for i in range(3):
                rows = pl.ds(pl.multiple_of(shard * 48 + i * 16, 16), 16)
                for j in range(2):
                    columns = pl.ds(pl.multiple_of(core * 256 + j * 128, 128), 128)
                    wo[rows, columns] = ref[z, j * 16:j * 16 + 16, 1152 + i * 128:1280 + i * 128]


def open_ffn(ids, parts, wgu, wd):
    for at, ref in enumerate(parts):
        other_y, other_core = at % 2, at // 2
        for z in range(4):
            place = order_of(ids, z, other_y, other_core)
            wgu[pl.ds(pl.multiple_of(place * 32, 32), 32), :] = ref[z, :, :2048]
            for i in range(2):
                wd[pl.ds(pl.multiple_of(place * 64 + i * 32, 32), 32), :] = (
                    ref[z, :, 2048 + i * 512:2560 + i * 512])


def hand_out(ids, packed, keep_ref, give_ref):
    for other_core, ref in enumerate((keep_ref, give_ref)):
        for other_y in range(2):
            for by in range(4):
                place = order_of(ids, (ids[0] + by) & 3, other_y, other_core)
                ref[other_y, by] = packed[pl.ds(pl.multiple_of(place * 32, 32), 32), :]


def attn_fwd_kernel(ids, x_ref, mask_ref, bias_ref, gain_ref, w0, w1, w2, w3,
                    out_ref, q_ref, k_ref, v_ref, p_ref, att_ref, wqkv, wo):
    @pl.when(pl.program_id(0) == 0)
    def _():
        open_attn(ids, (w0, w1, w2, w3), wqkv, wo)

    x = x_ref[...].astype(f32)
    a = (x * row_scale(x) * gain_ref[...]).astype(bf)
    q = dot_nn(a, wqkv[:, :384]).astype(bf)
    k = dot_nn(a, wqkv[:, 384:768]).astype(bf)
    v = dot_nn(a, wqkv[:, 768:]).astype(bf)
    q_ref[...] = q
    k_ref[...] = k
    v_ref[...] = v
    rows = x.shape[0] // 64
    units = [(r, h) for r in range(rows) for h in range(3)]
    at = lambda arr, r, h: arr[r * 64:r * 64 + 64, h * 128:h * 128 + 128]
    scores = [dot_nt(at(k, r, h), pair_parts(at(q, r, h))) for r, h in units]
    probs = []
    for (r, h), s in zip(units, scores):
        s = s + (bias_ref[:, h * 128:h * 128 + 128] + mask_ref[r])
        e = jnp.exp(s - jnp.max(s, axis=0, keepdims=True))
        p = (e * (1.0 / jnp.sum(e, axis=0, keepdims=True))).astype(bf)
        p_ref[r * 64:r * 64 + 64, h * 128:h * 128 + 128] = p
        probs.append(p)
    full_att = [dot_tn(p, at(v, r, h)) for (r, h), p in zip(units, probs)]
    att = {unit: pair_pick(part).astype(bf) for unit, part in zip(units, full_att)}
    att = jnp.concatenate(
        [jnp.concatenate([att[r, h] for h in range(3)], axis=1) for r in range(rows)], axis=0)
    att_ref[...] = att
    out_ref[...] = (x + dot_nn(att, wo[...])).astype(bf)


def norm_back(x_ref, gain_ref, gx, g_low, a_ref, dgain):
    x = x_ref[...].astype(f32)
    scale = row_scale(x)
    n = x * scale
    a_ref[...] = (n * gain_ref[...]).astype(bf)
    dgain[...] += jnp.sum(gx * n, axis=0, keepdims=True)
    e = gx * gain_ref[...]
    dx = scale * (e - n * jnp.mean(e * n, axis=-1, keepdims=True))
    return (g_low.astype(f32) + dx).astype(bf)


def bucket_of(key, query):
    offset = key - query
    distance = jnp.abs(offset)
    far = jnp.full(distance.shape, 8, jnp.int32)
    for threshold in limits:
        far = far + (distance >= threshold).astype(jnp.int32)
    near = jnp.where(distance < 8, distance, jnp.minimum(far, 15))
    return near + 16 * (offset > 0).astype(jnp.int32)


def table_terms(bias_grad):
    key = lax.broadcasted_iota(jnp.int32, (64, 128), 0)
    query = lax.broadcasted_iota(jnp.int32, (64, 128), 1) & 63
    bucket = bucket_of(key, query)
    pieces = [bias_grad[:, h * 128:h * 128 + 128] for h in range(3)]
    sums = [[], [], []]
    for b in range(32):
        hit = bucket == b
        for h in range(3):
            sums[h].append(jnp.sum(jnp.where(hit, pieces[h], 0.0), axis=0, keepdims=True))
    lane = lax.broadcasted_iota(jnp.int32, (32, 128), 1)
    table = jnp.zeros((32, 128), f32)
    for h in range(3):
        part = jnp.concatenate(sums[h], axis=0)
        low = jnp.sum(jnp.where(lane < 64, part, 0.0), axis=1, keepdims=True)
        high = jnp.sum(jnp.where(lane < 64, 0.0, part), axis=1, keepdims=True)
        table = jnp.where(lane == 2 * h, low, jnp.where(lane == 2 * h + 1, high, table))
    return table


def attn_bwd_kernel(ids, x_ref, q_ref, k_ref, v_ref, p_ref, att_ref, g_ref, gain_ref, w0, w1, w2, w3,
                    gains_in, bias_in, gin_ref, keep_ref, give_ref, dgain_ref, dbias_ref,
                    wqkv, wo, a_s, dqkv_s, att_s, g_s, dgain_s, dbias_s, packed):
    step = pl.program_id(0)
    last = pl.num_programs(0) - 1
    block = x_ref.shape[0]
    with_small = keep_ref.shape[3] > 1536

    @pl.when(step == 0)
    def _():
        open_attn(ids, (w0, w1, w2, w3), wqkv, wo)
        dgain_s[...] = jnp.zeros_like(dgain_s)
        dbias_s[...] = bias_in[...]

    here = pl.ds(pl.multiple_of(step * block, block), block)
    g_low = g_ref[...]
    da = dot_nt(g_low, wo[...]).astype(bf)
    att_s[here, :] = att_ref[...]
    g_s[here, :] = g_low
    rows = block // 64
    units = [(r, h) for r in range(rows) for h in range(3)]
    at = lambda arr, r, h: arr[r * 64:r * 64 + 64, h * 128:h * 128 + 128]
    db = [None] * 3
    da_bds = [pair_parts(at(da, r, h)) for r, h in units]
    dps = [dot_nt(at(v_ref, r, h), da_bd) for (r, h), da_bd in zip(units, da_bds)]
    dv_u = {(r, h): dot_nn(at(p_ref, r, h), da_bd).astype(bf) for (r, h), da_bd in zip(units, da_bds)}
    dss = []
    for (r, h), dp in zip(units, dps):
        pf = at(p_ref, r, h).astype(f32)
        ds = pf * (dp - jnp.sum(pf * dp, axis=0, keepdims=True))
        db[h] = ds if db[h] is None else db[h] + ds
        dss.append(ds.astype(bf))
    dk_u = {(r, h): dot_nn(ds, pair_parts(at(q_ref, r, h))).astype(bf) for (r, h), ds in zip(units, dss)}
    full_dq = [dot_tn(ds, at(k_ref, r, h)) for (r, h), ds in zip(units, dss)]
    dq_u = {unit: pair_pick(part).astype(bf) for unit, part in zip(units, full_dq)}
    dqkv = jnp.concatenate(
        [jnp.concatenate([u[r, h] for u in (dq_u, dk_u, dv_u) for h in range(3)], axis=1)
         for r in range(rows)], axis=0)
    dqkv_s[here, :] = dqkv
    for h in range(3):
        dbias_s[:, h * 128:h * 128 + 128] += db[h]
    gx = dot_nt(dqkv, wqkv[...])
    gin_ref[...] = norm_back(x_ref, gain_ref, gx, g_low, a_s.at[here, :], dgain_s)

    @pl.when(step == last)
    def _():
        for h in range(3):
            columns = slice(h * 384, h * 384 + 384)
            packed[:, columns] = dot_tn(a_s[...], dqkv_s[:, columns]).astype(bf)
        dwo = dot_tn(att_s[...], g_s[...]).astype(bf)
        for shard in range(8):
            for core in range(2):
                for i in range(3):
                    for j in range(2):
                        packed[(shard * 2 + core) * 32 + j * 16:(shard * 2 + core) * 32 + j * 16 + 16,
                               1152 + i * 128:1280 + i * 128] = (
                            dwo[shard * 48 + i * 16:shard * 48 + i * 16 + 16,
                                core * 256 + j * 128:core * 256 + j * 128 + 128])
        dgain_ref[...] = dgain_s[...]
        dbias_ref[...] = dbias_s[...]
        if with_small:
            table = table_terms(dbias_s[...]).astype(bf)
            terms = jnp.concatenate([dgain_s[...], gains_in[...]], axis=0)
            row = lax.broadcasted_iota(jnp.int32, (32, 128), 0)
            for shard in range(8):
                spot = slice(shard * 64, shard * 64 + 64)
                first = jnp.concatenate([terms[0:1, spot], terms[1:2, spot]], axis=1)
                second = jnp.concatenate([terms[2:3, spot], terms[3:4, spot]], axis=1)
                small = jnp.where(row == 0, first, jnp.where(row == 1, second, 0.0)).astype(bf)
                packed[shard * 64:shard * 64 + 32, 1536:1664] = small
                packed[shard * 64 + 32:shard * 64 + 64, 1536:1664] = table
        hand_out(ids, packed, keep_ref, give_ref)


def gelu_parts(u):
    c = 0.7978845608028654
    u2 = u * u
    t = jnp.tanh(u * (c + (c * 0.044715) * u2))
    half = 0.5 + 0.5 * t
    act = u * half
    slope = half + (0.5 * u) * (1.0 - t * t) * (c + (3.0 * c * 0.044715) * u2)
    return act, slope


def gelu(u):
    c = 0.7978845608028654
    t = jnp.tanh(u * (c + (c * 0.044715) * (u * u)))
    return u * (0.5 + 0.5 * t)


def ffn_fwd_kernel(ids, x_ref, gain_ref, w0, w1, w2, w3, out_ref, gate_ref, up_ref, wgu, wd):
    @pl.when(pl.program_id(0) == 0)
    def _():
        open_ffn(ids, (w0, w1, w2, w3), wgu, wd)

    x = x_ref[...].astype(f32)
    a = (x * row_scale(x) * gain_ref[...]).astype(bf)
    gate = dot_nn(a, wgu[:, :1024])
    up = dot_nn(a, wgu[:, 1024:])
    gate_ref[...] = gate.astype(bf)
    up_ref[...] = up.astype(bf)
    hidden = (gelu(gate) * up).astype(bf)
    out_ref[...] = (x + dot_nn(hidden, wd[...])).astype(bf)


def ffn_bwd_kernel(ids, x_ref, gate_ref, up_ref, g_ref, gain_ref, w0, w1, w2, w3,
                   gin_ref, keep_ref, give_ref, dgain_ref,
                   wgu, wd, a_s, gub_s, hid_s, g_s, dgain_s, packed):
    step = pl.program_id(0)
    last = pl.num_programs(0) - 1
    block = x_ref.shape[0]

    @pl.when(step == 0)
    def _():
        open_ffn(ids, (w0, w1, w2, w3), wgu, wd)
        dgain_s[...] = jnp.zeros_like(dgain_s)

    here = pl.ds(pl.multiple_of(step * block, block), block)
    g_low = g_ref[...]
    g_s[here, :] = g_low
    hg = dot_nt(g_low, wd[...])
    gate = gate_ref[...].astype(f32)
    up = up_ref[...].astype(f32)
    act, slope = gelu_parts(gate)
    hid_s[here, :] = (act * up).astype(bf)
    gb = (hg * up * slope).astype(bf)
    ub = (hg * act).astype(bf)
    gub_s[here, :1024] = gb
    gub_s[here, 1024:] = ub
    gx = dot_nt(gb, wgu[:, :1024]) + dot_nt(ub, wgu[:, 1024:])
    gin_ref[...] = norm_back(x_ref, gain_ref, gx, g_low, a_s.at[here, :], dgain_s)

    @pl.when(step == last)
    def _():
        for h in range(4):
            columns = slice(h * 512, h * 512 + 512)
            packed[:, columns] = dot_tn(a_s[...], gub_s[:, columns]).astype(bf)
        for h in range(2):
            dwd = dot_tn(hid_s[:, h * 512:h * 512 + 512], g_s[...]).astype(bf)
            for at in range(8):
                for i in range(2):
                    packed[(h * 8 + at) * 32:(h * 8 + at) * 32 + 32, 2048 + i * 512:2560 + i * 512] = (
                        dwd[at * 64 + i * 32:at * 64 + i * 32 + 32])
        dgain_ref[...] = dgain_s[...]
        hand_out(ids, packed, keep_ref, give_ref)


def tok(block, width):
    return pl.BlockSpec((block, width), lambda i, ids: (i, 0))


def full(shape):
    zero = (0,) * len(shape)
    return pl.BlockSpec(shape, lambda i, ids: zero)


def sds(shape, dtype):
    return jax.ShapeDtypeStruct(shape, dtype)


def call(kernel, grid, in_specs, out_specs, out_shape, scratch, micros, name):
    return pl.pallas_call(
        kernel,
        grid_spec=pltpu.PrefetchScalarGridSpec(
            num_scalar_prefetch=1, grid=(grid,), in_specs=in_specs, out_specs=out_specs,
            scratch_shapes=scratch),
        out_shape=out_shape, name=name,
        compiler_params=pltpu.CompilerParams(vmem_limit_bytes=vmem_limit),
        cost_estimate=pl.CostEstimate(flops=int(micros * 1.1e9), bytes_accessed=0, transcendentals=0),
    )


token_block = 512


def attn_fwd(ids, x, mask, bias, gain, parts):
    t, d = x.shape
    block = token_block
    return call(
        attn_fwd_kernel, t // block,
        [tok(block, d), pl.BlockSpec((block // 64, 64, 128), lambda i, ids: (i, 0, 0)), full(bias.shape),
         full((1, d))] + [full(parts[0].shape)] * 4,
        [tok(block, d)] + [tok(block, 384)] * 5,
        [sds((t, d), bf)] + [sds((t, 384), bf)] * 5,
        [pltpu.VMEM((512, 1152), bf), pltpu.VMEM((384, 512), bf)],
        7, "attn_fwd")(ids, x, mask, bias, gain, *parts)


def attn_bwd(ids, x, q, k, v, p, att, g, gain, parts, gains_in, bias_in, with_small):
    t, d = x.shape
    block = token_block
    n = 1664 if with_small else 1536
    packed = (2, 4, 32, n)
    return call(
        attn_bwd_kernel, t // block,
        [tok(block, d)] + [tok(block, 384)] * 5 + [tok(block, d), full((1, d))]
        + [full(parts[0].shape)] * 4 + [full(gains_in.shape), full(bias_in.shape)],
        [tok(block, d), full(packed), full(packed), full((1, d)), full((64, 384))],
        [sds((t, d), bf), sds(packed, bf), sds(packed, bf), sds((1, d), f32), sds((64, 384), f32)],
        [pltpu.VMEM((512, 1152), bf), pltpu.VMEM((384, 512), bf), pltpu.VMEM((t, d), bf),
         pltpu.VMEM((t, 1152), bf), pltpu.VMEM((t, 384), bf), pltpu.VMEM((t, d), bf),
         pltpu.VMEM((1, d), f32), pltpu.VMEM((64, 384), f32), pltpu.VMEM((512, n), bf)],
        12, "attn_bwd")(ids, x, q, k, v, p, att, g, gain, *parts, gains_in, bias_in)


def ffn_fwd(ids, x, gain, parts):
    t, d = x.shape
    block = token_block
    return call(
        ffn_fwd_kernel, t // block,
        [tok(block, d), full((1, d))] + [full(parts[0].shape)] * 4,
        [tok(block, d), tok(block, 1024), tok(block, 1024)],
        [sds((t, d), bf), sds((t, 1024), bf), sds((t, 1024), bf)],
        [pltpu.VMEM((512, 2048), bf), pltpu.VMEM((1024, 512), bf)],
        7, "ffn_fwd")(ids, x, gain, *parts)


def ffn_bwd(ids, x, gate, up, g, gain, parts):
    t, d = x.shape
    block = token_block
    packed = (2, 4, 32, 3072)
    return call(
        ffn_bwd_kernel, t // block,
        [tok(block, d), tok(block, 1024), tok(block, 1024), tok(block, d), full((1, d))]
        + [full(parts[0].shape)] * 4,
        [tok(block, d), full(packed), full(packed), full((1, d))],
        [sds((t, d), bf), sds(packed, bf), sds(packed, bf), sds((1, d), f32)],
        [pltpu.VMEM((512, 2048), bf), pltpu.VMEM((1024, 512), bf), pltpu.VMEM((t, d), bf),
         pltpu.VMEM((t, 2048), bf), pltpu.VMEM((t, 1024), bf), pltpu.VMEM((t, d), bf),
         pltpu.VMEM((1, d), f32), pltpu.VMEM((512, 3072), bf)],
        15, "ffn_bwd")(ids, x, gate, up, g, gain, *parts)


def pack_kernel(ids, q, k, v, o, gate, up, down, a0, f0, a1, f1):
    core = ids[2]
    rows = pl.ds(pl.multiple_of(core * 32, 32), 32)
    for layer, a_ref, f_ref in ((0, a0, f0), (1, a1, f1)):
        for at, w in enumerate((q, k, v)):
            a_ref[:, at * 384:at * 384 + 384] = w[layer, rows, :]
        for i in range(3):
            for j in range(2):
                columns = pl.ds(pl.multiple_of(core * 256 + j * 128, 128), 128)
                a_ref[j * 16:j * 16 + 16, 1152 + i * 128:1280 + i * 128] = (
                    o[layer, i * 16:i * 16 + 16, columns])
        f_ref[:, :1024] = gate[layer, rows, :]
        f_ref[:, 1024:2048] = up[layer, rows, :]
        for i in range(2):
            f_ref[:, 2048 + i * 512:2560 + i * 512] = (
                down[layer, pl.ds(pl.multiple_of(core * 64 + i * 32, 32), 32), :])


def pack_weights(ids, *weights):
    return call(
        pack_kernel, 1, [full(w.shape) for w in weights],
        [full((32, 1536)), full((32, 3072))] * 2,
        [sds((32, 1536), bf), sds((32, 3072), bf)] * 2, [], 2, "pack_weights")(ids, *weights)


def unpack_kernel(ids, *refs):
    sums, outs = refs[:16], refs[16:]
    q, k, v, o, gate, up, down, gains, table = outs
    first = ids[2] == 0
    for s in range(4):
        own, near, far, cross = (ref[...].astype(f32) for ref in sums[s * 4:s * 4 + 4])
        mine, peer = own + far, near + cross
        halves = (jnp.where(first, mine, peer), jnp.where(first, peer, mine))
        layer = s // 2
        for core in range(2):
            part = halves[core]
            rows = slice(core * 32, core * 32 + 32)
            if s % 2 == 0:
                for at, w in enumerate((q, k, v)):
                    w[layer, rows, :] = part[:, at * 384:at * 384 + 384]
                for i in range(3):
                    for j in range(2):
                        o[layer, i * 16:i * 16 + 16, core * 256 + j * 128:core * 256 + j * 128 + 128] = (
                            part[j * 16:j * 16 + 16, 1152 + i * 128:1280 + i * 128])
            else:
                gate[layer, rows, :] = part[:, :1024]
                up[layer, rows, :] = part[:, 1024:2048]
                for i in range(2):
                    down[layer, core * 64 + i * 32:core * 64 + i * 32 + 32, :] = (
                        part[:, 2048 + i * 512:2560 + i * 512])
        if s == 0:
            for l in range(2):
                for n in range(2):
                    gains[l, n:n + 1, :] = halves[0][l:l + 1, 1536 + n * 64:1600 + n * 64]
            table[...] = halves[1][:, 1536:1542]


def unpack_grads(ids, sums, shapes):
    flat = [array for part in sums for array in part]
    return call(
        unpack_kernel, 1, [full(array.shape) for array in flat], [full(shape) for shape in shapes],
        [sds(shape, f32) for shape in shapes], [], 3, "unpack_grads")(ids, *flat)


def place_kernel(ids, own0, own1, own2, own3, near, far, cross, out, sems):
    section = ids[3]
    def copy(ref, slot, sem):
        return pltpu.make_async_copy(ref, out.at[slot], sems.at[sem])
    for at, ref in enumerate((own0, own1, own2, own3)):
        @pl.when(section == at)
        def _(ref=ref):
            copy(ref, section, 0).start()
    copy(near, section ^ 1, 1).start()
    copy(far, section ^ 2, 2).start()
    copy(cross, section ^ 3, 3).start()
    copy(near, section, 0).wait()
    copy(near, section ^ 1, 1).wait()
    copy(far, section ^ 2, 2).wait()
    copy(cross, section ^ 3, 3).wait()


def place(ids, own, others):
    t, d = own[0].shape
    anywhere = pl.BlockSpec(memory_space=pl.ANY)
    return pl.pallas_call(
        place_kernel,
        grid_spec=pltpu.PrefetchScalarGridSpec(
            num_scalar_prefetch=1, grid=(1,), in_specs=[anywhere] * 7, out_specs=anywhere,
            scratch_shapes=[pltpu.SemaphoreType.DMA((4,))]),
        out_shape=sds((4, t, d), bf), name="place",
        cost_estimate=pl.CostEstimate(flops=3_000_000_000, bytes_accessed=0, transcendentals=0),
    )(ids, *own, *others)


def z_shift(values, by):
    half = lax.axis_size("dp") // 2
    pairs = [(z * 2 + y, ((z + by) % half) * 2 + y) for z in range(half) for y in range(2)]
    return lax.ppermute(values, "dp", pairs)


def swapped(values, axis, bit):
    return lax.ppermute(values, axis, [(i, i ^ bit) for i in range(lax.axis_size(axis))])


def after(values, *others):
    return lax.optimization_barrier((values,) + others)[0]


def added(*terms):
    total = terms[0].astype(f32)
    for term in terms[1:]:
        total = total + term.astype(f32)
    return total.astype(bf)


def gather_part(piece, place_ids):
    z = place_ids[0]
    got = [piece] + [z_shift(piece, by) for by in range(1, 4)]
    column = jnp.stack([lax.select_n((z - at) % 4, *got) for at in range(4)])
    other = swapped(column, "dp", 1)
    return (column, other, swapped(column, "section", 1), swapped(other, "section", 1)), got[-1]


def reduce_part(keep, give):
    got = swapped(give, "section", 1)
    sent = swapped(added(keep[1], got[1]), "dp", 1)
    terms = [added(keep[0, by], got[0, by], sent[by]) for by in range(4)]
    mine = added(terms[0], *[z_shift(terms[by], by) for by in range(1, 4)])
    return (mine,) + tuple(swapped(mine, "section", bit) for bit in (1, 2, 3)), (got, sent)


def to_packed(q, k, v, o, gate, up, down):
    o_part = o.reshape(8, 3, 16, 2, 2, 128).transpose(0, 3, 4, 2, 1, 5).reshape(512, 384)
    d_part = down.reshape(16, 2, 32, 512).transpose(0, 2, 1, 3).reshape(512, 1024)
    return jnp.concatenate([q, k, v, o_part], axis=1), jnp.concatenate([gate, up, d_part], axis=1)


def from_packed(attn, ffn):
    q, k, v = (attn[:, at * 384:at * 384 + 384] for at in range(3))
    o = attn[:, 1152:1536].reshape(8, 2, 2, 16, 3, 128).transpose(0, 4, 3, 1, 2, 5).reshape(384, 512)
    down = ffn[:, 2048:].reshape(16, 32, 2, 512).transpose(0, 2, 1, 3).reshape(1024, 512)
    return q, k, v, o, ffn[:, :1024], ffn[:, 1024:2048], down


def parts_of(whole):
    split = whole.reshape(4, 2, 2, 32, whole.shape[1])
    return tuple(split[:, y, core] for core in range(2) for y in range(2))


def whole_of(keep, give):
    split = jnp.stack([keep, give]).transpose(2, 1, 0, 3, 4)
    return split.reshape(512, keep.shape[3])


def gather_small(gains):
    z = lax.axis_index("dp") // 2
    y = lax.axis_index("dp") % 2
    got = [gains] + [z_shift(gains, by) for by in range(1, 4)]
    column = jnp.stack([lax.select_n((z - at) % 4, *got) for at in range(4)])
    other = swapped(column, "dp", 1)
    pair = jnp.stack([jnp.where(y == 0, column, other), jnp.where(y == 0, other, column)], axis=1)
    return pair.transpose(2, 3, 0, 1, 4).reshape(gains.shape[0], gains.shape[1], -1).astype(f32)


def body(inputs, cotangent, segments, observed, q_weight, k_weight, v_weight, o_weight,
         gate_weight, up_weight, down_weight, gains, position_table):
    section = lax.axis_index("section")
    dp = lax.axis_index("dp")
    micro_count, row_count, seq_count, width = inputs.shape
    layers = q_weight.shape[0]
    heads = position_table.shape[1]
    tokens = row_count * seq_count
    shards = (q_weight, k_weight, v_weight, o_weight, gate_weight, up_weight, down_weight)
    eight = lax.axis_size("dp") == 8
    own_ids = jnp.stack([dp // 2, dp % 2, section % 2, section]).astype(jnp.int32)
    ids = own_ids if eight else jnp.stack([0 * dp, 0 * dp, 0 * dp, section]).astype(jnp.int32)

    weights = []
    if eight:
        pieces = pack_weights(own_ids, *shards)
        previous = None
        for piece in pieces:
            if previous is not None:
                piece = after(piece, previous)
            parts, previous = gather_part(piece, (dp // 2,))
            weights.append(parts)
        gains_all = gather_small(gains)
    else:
        whole = [lax.all_gather(w, "dp", axis=1, tiled=True) for w in shards]
        for layer in range(layers):
            weights.extend(parts_of(w) for w in to_packed(*(w[layer] for w in whole)))
        gains_all = lax.all_gather(gains, "dp", axis=2, tiled=True).astype(f32)

    x = lax.dynamic_index_in_dim(inputs, section, 0, keepdims=False).reshape(tokens, width)
    grad = lax.dynamic_index_in_dim(cotangent, section, 0, keepdims=False).reshape(tokens, width)
    seg = lax.dynamic_index_in_dim(segments, section, 0, keepdims=False)
    obs = lax.dynamic_index_in_dim(observed, section, 0, keepdims=False)
    allowed = (seg[:, :, None] == seg[:, None, :]) & (obs[:, :, None] == 1)
    mask = jnp.where(allowed, 0.0, masked).astype(f32)
    mask = jnp.concatenate([mask, mask], axis=2)
    position = jnp.arange(seq_count, dtype=jnp.int32)
    bucket = bucket_of(position[:, None], position[None, :])
    onehot = (bucket[:, :, None] == jnp.arange(position_table.shape[0])[None, None, :]).astype(f32)
    bias = jnp.einsum("jib,bh->jhi", onehot, position_table.astype(f32), precision=lax.Precision.HIGHEST)
    bias = bias.reshape(seq_count, heads * seq_count)

    states, kept = [x], []
    for s in range(4):
        gain = gains_all[s // 2, s % 2][None]
        if s % 2 == 0:
            out, *saved = attn_fwd(ids, states[-1], mask, bias, gain, weights[s])
        else:
            out, *saved = ffn_fwd(ids, states[-1], gain, weights[s])
        states.append(out)
        kept.append(saved)
    outs = states[1:]

    grads, reduced, gain_terms = [None] * 4, [None] * 4, [None] * 4
    packed, steps = [None] * 4, [None] * 4
    bias_sum = jnp.zeros((seq_count, heads * seq_count), f32)
    for s in (3, 2, 1, 0):
        gain = gains_all[s // 2, s % 2][None]
        if eight and s == 1:
            grad = after(grad, steps[3][0])
        if eight and s == 0:
            grad = after(grad, steps[3][1], steps[2][0])
        if s % 2 == 1:
            grad, keep, give, gain_terms[s] = ffn_bwd(
                ids, states[s], *kept[s], grad, gain, weights[s])
        else:
            earlier = jnp.concatenate(gain_terms[1:]) if s == 0 else jnp.zeros((3, width), f32)
            grad, keep, give, gain_terms[s], bias_sum = attn_bwd(
                ids, states[s], *kept[s], grad, gain, weights[s], earlier, bias_sum, eight and s == 0)
        grads[s] = grad
        if eight:
            reduced[s], steps[s] = reduce_part(keep, give)
        else:
            packed[s] = whole_of(keep, give)

    def sent(values, s):
        return [lax.ppermute(values[s], "section", [(s ^ bit, s)]) for bit in (1, 2, 3)]

    def placed(values):
        arrived = [sent(values, s) for s in range(4)]
        others = [lax.select_n(section, *[arrived[s][at] for s in range(4)]) for at in range(3)]
        full_set = place(ids, values, others)
        return full_set.reshape(1, micro_count, row_count, seq_count, width)

    section_outputs = placed(outs)
    section_grads = placed(grads)

    if eight:
        shapes = [w.shape for w in shards] + [gains.shape, position_table.shape]
        final = unpack_grads(ids, reduced, shapes)
        return (section_outputs, section_grads) + tuple(final)

    dense = [from_packed(packed[2 * layer], packed[2 * layer + 1]) for layer in range(layers)]
    final = []
    for at in range(7):
        both = jnp.stack([d[at] for d in dense])
        part = lax.psum_scatter(both, "dp", scatter_dimension=1, tiled=True)
        final.append(lax.psum(part, "section").astype(f32))
    bias_sum = bias_sum.reshape(seq_count, heads, seq_count)
    table = jnp.einsum("jib,jhi->bh", onehot, bias_sum, precision=lax.Precision.HIGHEST)
    gain_sum = jnp.concatenate(gain_terms).reshape(layers, 2, width)
    table, gain_sum = lax.psum((table, gain_sum), ("section", "dp"))
    shard = gains.shape[2]
    gain_sum = lax.dynamic_slice_in_dim(gain_sum, dp * shard, shard, 2)
    return (section_outputs, section_grads) + tuple(final) + (gain_sum, table)


def solution(mesh):
    rows4 = P(None, "dp", None, None)
    rows3 = P(None, "dp", None)
    staged = P("section", None, "dp", None, None)
    return jax.shard_map(
        body,
        mesh=mesh,
        in_specs=(rows4, rows4) + (rows3,) * 9 + (P(None, None, "dp"), P()),
        out_specs=(staged, staged) + (rows3,) * 7 + (P(None, None, "dp"), P()),
        check_vma=False,
    )
```

time: 589 us -> 646 us (1.097)
  Pallas kernels: 92 us -> 353 us
  local copies, waits for them, and re-layouts: 152 us -> 12.6 us
  waiting for transfers between devices: 158 us -> 107 us
  starting transfers between devices: 88.1 us -> 133 us
  blocking collectives: 31.1 us -> 0 us
  other arithmetic: 58.9 us -> 30.2 us
    pallas_call x6 -> x10, Pallas kernels: 78.4 us -> 338 us  [the longest x2 258 us: place(): pl.pallas_call(place_kernel, grid_spec=pltpu.PrefetchScalarGridSpec(num_s...]
    reshape x62 -> x0, local copies, waits for them, and re-layouts: 83 us -> none  [the longest x24 31.1 us: open_rows(): split = packed.reshape(half, 2, 2, unit, n // width, width)]
    ppermute x8 -> x24, starting transfers between devices: 16.4 us -> 77.1 us  [sent(): lax.ppermute(values[s], 'section', [(s ^ bit, s)])]
    ppermute x8 -> x24, waiting for transfers between devices: 74.3 us -> 18.8 us  [sent(): lax.ppermute(values[s], 'section', [(s ^ bit, s)])]
    another operation x47 -> x12, other arithmetic: 40.3 us -> 2.17 us  [the longest x8 1.51 us: gather_part(): column = jnp.stack([lax.select_n((z - at) % 4, *got) for at in range(4)])]
    all_gather x1 -> x0, blocking collectives: 31.1 us -> none  [body(): gains_all = lax.all_gather(gains, 'dp', axis=2, tiled=True).astype(f32)]
    convert_element_type x30 -> x2, local copies, waits for them, and re-layouts: 19.5 us -> 0.1 us  [gather_small(): pair.transpose(2, 3, 0, 1, 4).reshape(gains.shape[0], gains.shape[1], -1)]
    ppermute x31 -> x33, starting transfers between devices: 30.8 us -> 13.1 us  [swapped(): lax.ppermute(values, axis, [(i, i ^ bit) for i in range(lax.axis_size(axi...]
  transfers between devices with their start and end apart: 63 -> 84, of which waited for: 25 -> 16; matrix products, arithmetic and copies ran while one was open for 33% -> 6% of each run, Pallas kernels for 16% -> 54%
where the time goes in v2:
time: 646 us; the launch traced here: 638 us
  Pallas kernels  353 us (55%)
  starting transfers between devices  133 us (21%)
  waiting for transfers between devices  107 us (17%)
  other arithmetic  30.2 us (5%)
  local copies, waits for them, and re-layouts  12.6 us (2%)
    pallas_call x2, Pallas kernels, place(): pl.pallas_call(place_kernel, grid_spec=pltpu.PrefetchScalarGridSpec(num_s...  258 us
    ppermute x24, starting transfers between devices, sent(): lax.ppermute(values[s], 'section', [(s ^ bit, s)])  77.1 us
    ppermute x33, waiting for transfers between devices, swapped(): lax.ppermute(values, axis, [(i, i ^ bit) for i in range(lax.axis_size(axi...  48.6 us
    ppermute x27, starting transfers between devices, z_shift(): return lax.ppermute(values, 'dp', pairs)  42.6 us
    ppermute x27, waiting for transfers between devices, z_shift(): return lax.ppermute(values, 'dp', pairs)  39.6 us
    pallas_call x2, Pallas kernels, ffn_bwd(): call(ffn_bwd_kernel, t // block, [tok(block, d), tok(block, 1024), tok(bl...  32 us
    pallas_call x2, Pallas kernels, attn_bwd(): call(attn_bwd_kernel, t // block, [tok(block, d)] + [tok(block, 384)] * 5...  25.8 us
    ppermute x24, waiting for transfers between devices, sent(): lax.ppermute(values[s], 'section', [(s ^ bit, s)])  18.8 us
  transfers between devices with their start and end apart: 84, of which 16 were waited for; matrix products, arithmetic and copies ran while one was open for 6% of the time, Pallas kernels for 54%

profile of v2, /device:TPU:0, one launch (start us, length us, event | category | flops | bytes accessed | tf_op | source)
XLA Modules:
  0.0 638.4 jit_solution(12274318932028453821)
XLA Ops:
  1.3 2.9 pack_weights.1
  4.2 5.0 collective-permute-start.6
  9.3 4.4 collective-permute-start.1
  14.5 2.3 constant_dynamic-slice_fusion.1
  16.8 2.3 constant_dynamic-slice_fusion
  25.8 2.9 collective-permute-start.12
  31.1 4.6 collective-permute-done.12
  35.8 2.7 collective-permute-start.18
  38.7 5.0 collective-permute-start.16
  43.7 10.9 %collective-permute-done.11 = bf16[32,3072]{1,0:T(8,128)(2,1)S(1)} collective-permute-done((bf16[32,3072]{1,0:T(8,128)(2,1)S(1)}, bf16[32,3072]{1,0:T(8,128)(2,1)S(1)}, u32[]{:S(2)}, u32[]{:S(2)}) %collective-permute-start.11) | collective-permute-done | bytes 196640 | tf_op jit(solution)/shard_map/ppermute | solution.py:492
  54.9 2.4 collective-permute-start.22
  57.9 7.3 %collective-permute-done.17 = bf16[32,1536]{1,0:T(8,128)(2,1)S(1)} collective-permute-done((bf16[32,1536]{1,0:T(8,128)(2,1)S(1)}, bf16[32,1536]{1,0:T(8,128)(2,1)S(1)}, u32[]{:S(2)}, u32[]{:S(2)}) %collective-permute-start.17) | collective-permute-done | bytes 98336 | tf_op jit(solution)/shard_map/ppermute | solution.py:492
  65.5 1.9 collective-permute-done.23
  67.3 3.6 collective-permute-done.24
  72.0 11.0 %collective-permute-done.13.w1 = bf16[4,32,3072]{2,1,0:T(8,128)(2,1)} collective-permute-done((bf16[4,32,3072]{2,1,0:T(8,128)(2,1)S(1)}, bf16[4,32,3072]{2,1,0:T(8,128)(2,1)}, u32[]{:S(2)}, u32[]{:S(2)}) %collective-permute-start.13) | collective-permute-done | bytes 786464 | tf_op jit(solution)/shard_map/ppermute | solution.py:496
  84.6 7.7 %attn_fwd.2 = (bf16[1024,512]{1,0:T(8,128)(2,1)}, bf16[1024,384]{1,0:T(8,128)(2,1)}, bf16[1024,384]{1,0:T(8,128)(2,1)}, bf16[1024,384]{1,0:T(8,128)(2,1)}, bf16[...) custom-call(s32[4]{0:T(128)} %pad_add_fusion.ids, bf16[1024,512]{1,0:T(8,128)(2,1)} %bitcast.201, ...), custom_call_target="tpu_custom_call" | custom-call | flops 7699999744 | tf_op jit(solution)/shard_map/attn_fwd/pallas_call | solution.py:340
  92.4 10.3 %collective-permute-done.19.w1 = bf16[4,32,1536]{2,1,0:T(8,128)(2,1)S(1)} collective-permute-done((bf16[4,32,1536]{2,1,0:T(8,128)(2,1)S(1)}, bf16[4,32,1536]{2,1,0:T(8,128)(2,1)S(1)}, u32[]{:S(2)}, u32[]{:S(2)}) %collective-permute-start.19) | collective-permute-done | bytes 393248 | tf_op jit(solution)/shard_map/ppermute | solution.py:496
  105.9 7.8 %ffn_fwd.2 = (bf16[1024,512]{1,0:T(8,128)(2,1)}, bf16[1024,1024]{1,0:T(8,128)(2,1)}, bf16[1024,1024]{1,0:T(8,128)(2,1)}) custom-call(s32[4]{0:T(128)} %pad_add_fusion.ids, bf16[1024,512]{1,0:T(8,128)(2,1)} %get-tuple-element.64.x_ref.own0, f32[1,512]{1,0:T(1,128)} %get-tuple-element.167.gain_ref, bf16[4,32,3072]{2,1,0:T(8,128)(2,1)} %copy-done.15, ...), custom_call_target="tpu_custom_call" | custom-call | flops 7699999744 | tf_op jit(solution)/shard_map/ffn_fwd/pallas_call | solution.py:370
  116.7 7.8 %attn_fwd.3 = (bf16[1024,512]{1,0:T(8,128)(2,1)}, bf16[1024,384]{1,0:T(8,128)(2,1)}, bf16[1024,384]{1,0:T(8,128)(2,1)}, bf16[1024,384]{1,0:T(8,128)(2,1)}, bf16[...) custom-call(s32[4]{0:T(128)} %pad_add_fusion.ids, bf16[1024,512]{1,0:T(8,128)(2,1)} %get-tuple-element.67.x_ref.own1, ...), custom_call_target="tpu_custom_call" | custom-call | flops 7699999744 | tf_op jit(solution)/shard_map/attn_fwd/pallas_call | solution.py:340
  126.1 7.0 %collective-permute-start.34 = (bf16[1024,512]{1,0:T(8,128)(2,1)}, bf16[1024,512]{1,0:T(8,128)(2,1)}, u32[]{:S(2)}, u32[]{:S(2)}) collective-permute-start(bf16[1024,512]{1,0:T(8,128)(2,1)} %get-tuple-element.70.x_ref.own2), channel_id=1, source_target_pairs={{0,16},{1,17},{2,18},{3,19},{4,20},{5,21},{6,22},{7,23}} | collective-permute-start | bytes 3145736 | tf_op jit(solution)/shard_map/ppermute | solution.py:635
  133.2 7.6 %ffn_fwd.3 = (bf16[1024,512]{1,0:T(8,128)(2,1)}, bf16[1024,1024]{1,0:T(8,128)(2,1)}, bf16[1024,1024]{1,0:T(8,128)(2,1)}) custom-call(s32[4]{0:T(128)} %pad_add_fusion.ids, bf16[1024,512]{1,0:T(8,128)(2,1)} %get-tuple-element.70.x_ref.own2, f32[1,512]{1,0:T(1,128)} %get-tuple-element.165.gain_ref, bf16[4,32,3072]{2,1,0:T(8,128)(2,1)} %pad_maximum_fusion.1.w0, ...), custom_call_target="tpu_custom_call" | custom-call | flops 7699999744 | tf_op jit(solution)/shard_map/ffn_fwd/pallas_call | solution.py:370
  140.8 16.0 %ffn_bwd.2 = (bf16[1024,512]{1,0:T(8,128)(2,1)}, bf16[2,4,32,3072]{3,2,1,0:T(8,128)(2,1)}, bf16[2,4,32,3072]{3,2,1,0:T(8,128)(2,1)}, f32[1,512]{1,0:T(1,128)}) custom-call(s32[4]{0:T(128)} %pad_add_fusion.ids, bf16[1024,512]{1,0:T(8,128)(2,1)} %get-tuple-element.70.x_ref.own2, bf16[1024,1024]{1,0:T(8,128)(2,1)} %get-tuple-element.86.gate_ref, ...), custom_call_target="tpu_custom_call" | custom-call | flops 16499999744 | tf_op jit(solution)/shard_map/ffn_bwd/pallas_call | solution.py:383
  158.5 6.0 collective-permute-start.39
  165.8 12.7 %attn_bwd.2 = (bf16[1024,512]{1,0:T(8,128)(2,1)}, bf16[2,4,32,1536]{3,2,1,0:T(8,128)(2,1)}, bf16[2,4,32,1536]{3,2,1,0:T(8,128)(2,1)}, f32[1,512]{1,0:T(1,128)}, f32[64,384]{1,0:T(8,128)}) custom-call(s32[4]{0:T(128)} %pad_add_fusion.ids, bf16[1024,512]{1,0:T(8,128)(2,1)} %get-tuple-element.67.x_ref.own1, bf16[1024,384]{1,0:T(8,128)(2,1)} %get-tuple-element.81.q_ref, ...), custom_call_target="tpu_custom_call" | custom-call | flops 13200000000 | tf_op jit(solution)/shard_map/attn_bwd/pallas_call | solution.py:355
  182.5 3.2 collective-permute-start.29
  187.6 2.5 select_select_fusion.3.cross
  190.1 2.7 select_select_fusion.4.far
  192.9 7.0 %collective-permute-start.54 = (bf16[1024,512]{1,0:T(8,128)(2,1)}, bf16[1024,512]{1,0:T(8,128)(2,1)}, u32[]{:S(2)}, u32[]{:S(2)}) collective-permute-start(bf16[1024,512]{1,0:T(8,128)(2,1)} %get-tuple-element.88.g_ref.own3), channel_id=1, source_target_pairs={{0,24},{1,25},{2,26},{3,27},{4,28},{5,29},{6,30},{7,31}} | collective-permute-start | bytes 3145736 | tf_op jit(solution)/shard_map/ppermute | solution.py:635
  202.5 2.1 collective-permute-start.72
  204.6 2.4 collective-permute-start.74
  207.0 128.9 %place.2 = bf16[4,1024,512]{2,1,0:T(8,128)(2,1)} custom-call(s32[4]{0:T(128)} %pad_add_fusion.ids, bf16[1024,512]{1,0:T(8,128)(2,1)} %get-tuple-element.64.x_ref.own0, bf16[1024,512]{1,0:T(8,128)(2,1)} %get-tuple-element.67.x_ref.own1, bf16[1024,512]{1,0:T(8,128)(2,1)} %get-tuple-element.70.x_ref.own2, bf16[1024,512]{1,0:T(8,128)(2,1)} %get-tuple-element.73.own3, ...), custom_call_target="tpu_custom_call" | custom-call | flops 3000000000 | tf_op jit(solution)/shard_map/place/pallas_call | solution.py:479
  338.9 10.1 %collective-permute-start.50 = (bf16[1024,512]{1,0:T(8,128)(2,1)}, bf16[1024,512]{1,0:T(8,128)(2,1)}, u32[]{:S(2)}, u32[]{:S(2)}) collective-permute-start(bf16[1024,512]{1,0:T(8,128)(2,1)} %get-tuple-element.88.g_ref.own3), channel_id=1, source_target_pairs={{8,24},{9,25},{10,26},{11,27},{12,28},{13,29},{14,30},{15,31}} | collective-permute-start | bytes 3145736 | tf_op jit(solution)/shard_map/ppermute | solution.py:635
  351.5 1.8 collective-permute-start.41
  353.3 15.9 %ffn_bwd.3 = (bf16[1024,512]{1,0:T(8,128)(2,1)}, bf16[2,4,32,3072]{3,2,1,0:T(8,128)(2,1)}, bf16[2,4,32,3072]{3,2,1,0:T(8,128)(2,1)}, f32[1,512]{1,0:T(1,128)}) custom-call(s32[4]{0:T(128)} %pad_add_fusion.ids, bf16[1024,512]{1,0:T(8,128)(2,1)} %get-tuple-element.64.x_ref.own0, bf16[1024,1024]{1,0:T(8,128)(2,1)} %get-tuple-element.79.gate_ref, ...), custom_call_target="tpu_custom_call" | custom-call | flops 16499999744 | tf_op jit(solution)/shard_map/ffn_bwd/pallas_call | solution.py:383
  373.7 2.2 collective-permute-start.79
  377.7 13.1 %attn_bwd.3 = (bf16[1024,512]{1,0:T(8,128)(2,1)}, bf16[2,4,32,1664]{3,2,1,0:T(8,128)(2,1)}, bf16[2,4,32,1664]{3,2,1,0:T(8,128)(2,1)}, f32[1,512]{1,0:T(1,128)}, f32[64,384]{1,0:T(8,128)}) custom-call(s32[4]{0:T(128)} %pad_add_fusion.ids, bf16[1024,512]{1,0:T(8,128)(2,1)} %bitcast.202, bf16[1024,384]{1,0:T(8,128)(2,1)} %get-tuple-element.74.q_ref, ...), custom_call_target="tpu_custom_call" | custom-call | flops 13200000000 | tf_op jit(solution)/shard_map/attn_bwd/pallas_call | solution.py:355
  400.6 21.5 %collective-permute-start.44 = (bf16[1024,512]{1,0:T(8,128)(2,1)S(1)}, bf16[1024,512]{1,0:T(8,128)(2,1)S(1)}, u32[]{:S(2)}, u32[]{:S(2)}) collective-permute-start(bf16[1024,512]{1,0:T(8,128)(2,1)S(1)} %copy-done.5), channel_id=1, source_target_pairs={{0,8},{1,9},{2,10},{3,11},{4,12},{5,13},{6,14},{7,15}} | collective-permute-start | bytes 3145736 | tf_op jit(solution)/shard_map/ppermute | solution.py:635
  422.1 18.7 %collective-permute-done.51 = bf16[1024,512]{1,0:T(8,128)(2,1)S(1)} collective-permute-done((bf16[1024,512]{1,0:T(8,128)(2,1)}, bf16[1024,512]{1,0:T(8,128)(2,1)S(1)}, u32[]{:S(2)}, u32[]{:S(2)}) %collective-permute-start.51) | collective-permute-done | bytes 1048608 | tf_op jit(solution)/shard_map/ppermute | solution.py:635
  443.3 2.7 select_select_fusion.cross
  451.5 7.0 %collective-permute-done.56 = bf16[4,32,1664]{2,1,0:T(8,128)(2,1)S(1)} collective-permute-done((bf16[4,32,1664]{2,1,0:T(8,128)(2,1)S(1)}, bf16[4,32,1664]{2,1,0:T(8,128)(2,1)S(1)}, u32[]{:S(2)}, u32[]{:S(2)}) %collective-permute-start.56) | collective-permute-done | bytes 426016 | tf_op jit(solution)/shard_map/ppermute | solution.py:496
  460.4 14.9 %collective-permute-done.64 = bf16[4,32,3072]{2,1,0:T(8,128)(2,1)S(1)} collective-permute-done((bf16[4,32,3072]{2,1,0:T(8,128)(2,1)S(1)}, bf16[4,32,3072]{2,1,0:T(8,128)(2,1)S(1)}, u32[]{:S(2)}, u32[]{:S(2)}) %collective-permute-start.64) | collective-permute-done | bytes 786464 | tf_op jit(solution)/shard_map/ppermute | solution.py:496
  480.4 3.2 collective-permute-start.67
  483.9 3.7 collective-permute-done.65
  487.6 7.4 %collective-permute-done.66 = bf16[32,3072]{1,0:T(8,128)(2,1)S(1)} collective-permute-done((bf16[32,3072]{1,0:T(8,128)(2,1)S(1)}, bf16[32,3072]{1,0:T(8,128)(2,1)S(1)}, u32[]{:S(2)}, u32[]{:S(2)}) %collective-permute-start.66) | collective-permute-done | bytes 196640 | tf_op jit(solution)/shard_map/ppermute | solution.py:492
  496.1 2.1 collective-permute-start.61
  498.5 3.6 collective-permute-done.83.refs_15_
  502.3 128.9 %place.3 = bf16[4,1024,512]{2,1,0:T(8,128)(2,1)} custom-call(s32[4]{0:T(128)} %pad_add_fusion.ids, bf16[1024,512]{1,0:T(8,128)(2,1)} %get-tuple-element.100.own0, bf16[1024,512]{1,0:T(8,128)(2,1)} %get-tuple-element.95.g_ref.own1, bf16[1024,512]{1,0:T(8,128)(2,1)} %get-tuple-element.91.g_ref.own2, bf16[1024,512]{1,0:T(8,128)(2,1)} %get-tuple-element.88.g_ref.own3, ...), custom_call_target="tpu_custom_call" | custom-call | flops 3000000000 | tf_op jit(solution)/shard_map/place/pallas_call | solution.py:479
  632.7 4.0 unpack_grads.1
  (279 shorter events, 74.6 us)
Async XLA Ops:
  4.2 21.6 %collective-permute-start.6 = (bf16[32,1536]{1,0:T(8,128)(2,1)}, bf16[32,1536]{1,0:T(8,128)(2,1)S(1)}, u32[]{:S(2)}, u32[]{:S(2)}) collective-permute-start(bf16[32,1536]{1,0:T(8,128)(2,1)} %get-tuple-element.63), channel_id=1, source_target_pairs={{0,6},{1,7},{2,0},{3,1},{4,2},{5,3},{6,4},{7,5},{8,14},{9,15},{10,... | collective-permute-start | bytes 294920 | tf_op jit(solution)/shard_map/ppermute | solution.py:492
  9.3 20.1 %collective-permute-start.4 = (bf16[32,1536]{1,0:T(8,128)(2,1)}, bf16[32,1536]{1,0:T(8,128)(2,1)S(1)}, u32[]{:S(2)}, u32[]{:S(2)}) collective-permute-start(bf16[32,1536]{1,0:T(8,128)(2,1)} %get-tuple-element.63), channel_id=1, source_target_pairs={{0,2},{1,3},{2,4},{3,5},{4,6},{5,7},{6,0},{7,1},{8,10},{9,11},{10,... | collective-permute-start | bytes 294920 | tf_op jit(solution)/shard_map/ppermute | solution.py:492
  28.8 25.9 %collective-permute-start.11 = (bf16[32,3072]{1,0:T(8,128)(2,1)S(1)}, bf16[32,3072]{1,0:T(8,128)(2,1)S(1)}, u32[]{:S(2)}, u32[]{:S(2)}) collective-permute-start(bf16[32,3072]{1,0:T(8,128)(2,1)S(1)} %copy-done.20), channel_id=1, source_target_pairs={{0,4},{1,5},{2,6},{3,7},{4,0},{5,1},{6,2},{7,3},{8,12},{9,13},{10,... | collective-permute-start | bytes 589832 | tf_op jit(solution)/shard_map/ppermute | solution.py:492
  29.5 35.8 %collective-permute-start.7 = (bf16[4,32,1536]{2,1,0:T(8,128)(2,1)S(1)}, bf16[4,32,1536]{2,1,0:T(8,128)(2,1)S(1)}, u32[]{:S(2)}, u32[]{:S(2)}) collective-permute-start(bf16[4,32,1536]{2,1,0:T(8,128)(2,1)S(1)} %pad_maximum_fusion.3.w0), channel_id=1, source_target_pairs={{0,1},{1,0},{2,3},{3,2},{4,5},{5,4},{6,7},{7,6},{8,9},{9,8},{10,11... | collective-permute-start | bytes 1179656 | tf_op jit(solution)/shard_map/ppermute | solution.py:496
  31.1 52.0 %collective-permute-start.8 = (bf16[4,32,1536]{2,1,0:T(8,128)(2,1)S(1)}, bf16[4,32,1536]{2,1,0:T(8,128)(2,1)S(1)}, u32[]{:S(2)}, u32[]{:S(2)}) collective-permute-start(bf16[4,32,1536]{2,1,0:T(8,128)(2,1)S(1)} %pad_maximum_fusion.3.w0), channel_id=1, source_target_pairs={{0,8},{8,0},{16,24},{24,16},{1,9},{9,1},{17,25},{25,17},{2,10},{10... | collective-permute-start | bytes 1179656 | tf_op jit(solution)/shard_map/ppermute | solution.py:496
  35.8 19.1 %collective-permute-start.18 = (bf16[32,1536]{1,0:T(8,128)(2,1)S(1)}, bf16[32,1536]{1,0:T(8,128)(2,1)S(1)}, u32[]{:S(2)}, u32[]{:S(2)}) collective-permute-start(bf16[32,1536]{1,0:T(8,128)(2,1)S(1)} %copy-done.24), channel_id=1, source_target_pairs={{0,6},{1,7},{2,0},{3,1},{4,2},{5,3},{6,4},{7,5},{8,14},{9,15},{10,... | collective-permute-start | bytes 294920 | tf_op jit(solution)/shard_map/ppermute | solution.py:492
  38.7 18.6 %collective-permute-start.16 = (bf16[32,1536]{1,0:T(8,128)(2,1)S(1)}, bf16[32,1536]{1,0:T(8,128)(2,1)S(1)}, u32[]{:S(2)}, u32[]{:S(2)}) collective-permute-start(bf16[32,1536]{1,0:T(8,128)(2,1)S(1)} %copy-done.24), channel_id=1, source_target_pairs={{0,2},{1,3},{2,4},{3,5},{4,6},{5,7},{6,0},{7,1},{8,10},{9,11},{10,... | collective-permute-start | bytes 294920 | tf_op jit(solution)/shard_map/ppermute | solution.py:492
  65.4 37.3 %collective-permute-start.14 = (bf16[4,32,3072]{2,1,0:T(8,128)(2,1)S(1)}, bf16[4,32,3072]{2,1,0:T(8,128)(2,1)S(1)}, u32[]{:S(2)}, u32[]{:S(2)}) collective-permute-start(bf16[4,32,3072]{2,1,0:T(8,128)(2,1)S(1)} %pad_maximum_fusion.w0), channel_id=1, source_target_pairs={{0,8},{8,0},{16,24},{24,16},{1,9},{9,1},{17,25},{25,17},{2,10},{10... | collective-permute-start | bytes 2359304 | tf_op jit(solution)/shard_map/ppermute | solution.py:496
  72.0 31.2 %collective-permute-start.25 = (bf16[4,32,3072]{2,1,0:T(8,128)(2,1)}, bf16[4,32,3072]{2,1,0:T(8,128)(2,1)}, u32[]{:S(2)}, u32[]{:S(2)}) collective-permute-start(bf16[4,32,3072]{2,1,0:T(8,128)(2,1)} %pad_maximum_fusion.1.w0), channel_id=1, source_target_pairs={{0,1},{1,0},{2,3},{3,2},{4,5},{5,4},{6,7},{7,6},{8,9},{9,8},{10,11... | collective-permute-start | bytes 2359304 | tf_op jit(solution)/shard_map/ppermute | solution.py:496
  83.0 21.9 %collective-permute-start.15 = (bf16[4,32,3072]{2,1,0:T(8,128)(2,1)}, bf16[4,32,3072]{2,1,0:T(8,128)(2,1)S(1)}, u32[]{:S(2)}, u32[]{:S(2)}) collective-permute-start(bf16[4,32,3072]{2,1,0:T(8,128)(2,1)} %collective-permute-done.13.w1), channel_id=1, source_target_pairs={{0,8},{8,0},{16,24},{24,16},{1,9},{9,1},{17,25},{25,17},{2,10},{10... | collective-permute-start | bytes 2359304 | tf_op jit(solution)/shard_map/ppermute | solution.py:496
  83.1 19.6 %collective-permute-start.19 = (bf16[4,32,1536]{2,1,0:T(8,128)(2,1)S(1)}, bf16[4,32,1536]{2,1,0:T(8,128)(2,1)S(1)}, u32[]{:S(2)}, u32[]{:S(2)}) collective-permute-start(bf16[4,32,1536]{2,1,0:T(8,128)(2,1)S(1)} %pad_maximum_fusion.4.w0), channel_id=1, source_target_pairs={{0,1},{1,0},{2,3},{3,2},{4,5},{5,4},{6,7},{7,6},{8,9},{9,8},{10,11... | collective-permute-start | bytes 1179656 | tf_op jit(solution)/shard_map/ppermute | solution.py:496
  83.9 29.7 %collective-permute-start.20 = (bf16[4,32,1536]{2,1,0:T(8,128)(2,1)S(1)}, bf16[4,32,1536]{2,1,0:T(8,128)(2,1)}, u32[]{:S(2)}, u32[]{:S(2)}) collective-permute-start(bf16[4,32,1536]{2,1,0:T(8,128)(2,1)S(1)} %pad_maximum_fusion.4.w0), channel_id=1, source_target_pairs={{0,8},{8,0},{16,24},{24,16},{1,9},{9,1},{17,25},{25,17},{2,10},{10... | collective-permute-start | bytes 1179656 | tf_op jit(solution)/shard_map/ppermute | solution.py:496
  102.7 21.8 %collective-permute-start.26 = (bf16[4,32,3072]{2,1,0:T(8,128)(2,1)}, bf16[4,32,3072]{2,1,0:T(8,128)(2,1)}, u32[]{:S(2)}, u32[]{:S(2)}) collective-permute-start(bf16[4,32,3072]{2,1,0:T(8,128)(2,1)} %pad_maximum_fusion.1.w0), channel_id=1, source_target_pairs={{0,8},{8,0},{16,24},{24,16},{1,9},{9,1},{17,25},{25,17},{2,10},{10... | collective-permute-start | bytes 2359304 | tf_op jit(solution)/shard_map/ppermute | solution.py:496
  103.7 53.2 %collective-permute-start.36 = (bf16[1024,512]{1,0:T(8,128)(2,1)}, bf16[1024,512]{1,0:T(8,128)(2,1)S(1)}, u32[]{:S(2)}, u32[]{:S(2)}) collective-permute-start(bf16[1024,512]{1,0:T(8,128)(2,1)} %get-tuple-element.64.x_ref.own0), channel_id=1, source_target_pairs={{24,0},{25,1},{26,2},{27,3},{28,4},{29,5},{30,6},{31,7}} | collective-permute-start | bytes 3145736 | tf_op jit(solution)/shard_map/ppermute | solution.py:635
  105.0 21.2 %collective-permute-start.27 = (bf16[4,32,3072]{2,1,0:T(8,128)(2,1)}, bf16[4,32,3072]{2,1,0:T(8,128)(2,1)S(1)}, u32[]{:S(2)}, u32[]{:S(2)}) collective-permute-start(bf16[4,32,3072]{2,1,0:T(8,128)(2,1)} %collective-permute-done.25.w1), channel_id=1, source_target_pairs={{0,8},{8,0},{16,24},{24,16},{1,9},{9,1},{17,25},{25,17},{2,10},{10... | collective-permute-start | bytes 2359304 | tf_op jit(solution)/shard_map/ppermute | solution.py:496
  113.7 44.9 %collective-permute-start.32 = (bf16[1024,512]{1,0:T(8,128)(2,1)S(1)}, bf16[1024,512]{1,0:T(8,128)(2,1)}, u32[]{:S(2)}, u32[]{:S(2)}) collective-permute-start(bf16[1024,512]{1,0:T(8,128)(2,1)S(1)} %copy-done.6), channel_id=1, source_target_pairs={{16,0},{17,1},{18,2},{19,3},{20,4},{21,5},{22,6},{23,7}} | collective-permute-start | bytes 3145736 | tf_op jit(solution)/shard_map/ppermute | solution.py:635
  115.0 63.6 %collective-permute-start.37 = (bf16[1024,512]{1,0:T(8,128)(2,1)}, bf16[1024,512]{1,0:T(8,128)(2,1)}, u32[]{:S(2)}, u32[]{:S(2)}) collective-permute-start(bf16[1024,512]{1,0:T(8,128)(2,1)} %get-tuple-element.67.x_ref.own1), channel_id=1, source_target_pairs={{16,8},{17,9},{18,10},{19,11},{20,12},{21,13},{22,14},{23,15}} | collective-permute-start | bytes 3145736 | tf_op jit(solution)/shard_map/ppermute | solution.py:635
  124.4 54.1 %collective-permute-start.38 = (bf16[1024,512]{1,0:T(8,128)(2,1)}, bf16[1024,512]{1,0:T(8,128)(2,1)}, u32[]{:S(2)}, u32[]{:S(2)}) collective-permute-start(bf16[1024,512]{1,0:T(8,128)(2,1)} %get-tuple-element.70.x_ref.own2), channel_id=1, source_target_pairs={{8,16},{9,17},{10,18},{11,19},{12,20},{13,21},{14,22},{15,23}} | collective-permute-start | bytes 3145736 | tf_op jit(solution)/shard_map/ppermute | solution.py:635
  126.1 54.1 %collective-permute-start.34 = (bf16[1024,512]{1,0:T(8,128)(2,1)}, bf16[1024,512]{1,0:T(8,128)(2,1)}, u32[]{:S(2)}, u32[]{:S(2)}) collective-permute-start(bf16[1024,512]{1,0:T(8,128)(2,1)} %get-tuple-element.70.x_ref.own2), channel_id=1, source_target_pairs={{0,16},{1,17},{2,18},{3,19},{4,20},{5,21},{6,22},{7,23}} | collective-permute-start | bytes 3145736 | tf_op jit(solution)/shard_map/ppermute | solution.py:635
  156.9 24.8 %collective-permute-start.33 = (bf16[1024,512]{1,0:T(8,128)(2,1)}, bf16[1024,512]{1,0:T(8,128)(2,1)}, u32[]{:S(2)}, u32[]{:S(2)}) collective-permute-start(bf16[1024,512]{1,0:T(8,128)(2,1)} %get-tuple-element.67.x_ref.own1), channel_id=1, source_target_pairs={{24,8},{25,9},{26,10},{27,11},{28,12},{29,13},{30,14},{31,15}} | collective-permute-start | bytes 3145736 | tf_op jit(solution)/shard_map/ppermute | solution.py:635
  158.5 27.1 %collective-permute-start.39 = (bf16[1024,512]{1,0:T(8,128)(2,1)S(1)}, bf16[1024,512]{1,0:T(8,128)(2,1)}, u32[]{:S(2)}, u32[]{:S(2)}) collective-permute-start(bf16[1024,512]{1,0:T(8,128)(2,1)S(1)} %copy-done.9), channel_id=1, source_target_pairs={{0,24},{1,25},{2,26},{3,27},{4,28},{5,29},{6,30},{7,31}} | collective-permute-start | bytes 3145736 | tf_op jit(solution)/shard_map/ppermute | solution.py:635
  181.7 18.2 %collective-permute-start.30 = (bf16[1024,512]{1,0:T(8,128)(2,1)S(1)}, bf16[1024,512]{1,0:T(8,128)(2,1)S(1)}, u32[]{:S(2)}, u32[]{:S(2)}) collective-permute-start(bf16[1024,512]{1,0:T(8,128)(2,1)S(1)} %copy-done.8), channel_id=1, source_target_pairs={{24,16},{25,17},{26,18},{27,19},{28,20},{29,21},{30,22},{31,23}} | collective-permute-start | bytes 3145736 | tf_op jit(solution)/shard_map/ppermute | solution.py:635
  192.9 180.9 %collective-permute-start.54 = (bf16[1024,512]{1,0:T(8,128)(2,1)}, bf16[1024,512]{1,0:T(8,128)(2,1)}, u32[]{:S(2)}, u32[]{:S(2)}) collective-permute-start(bf16[1024,512]{1,0:T(8,128)(2,1)} %get-tuple-element.88.g_ref.own3), channel_id=1, source_target_pairs={{0,24},{1,25},{2,26},{3,27},{4,28},{5,29},{6,30},{7,31}} | collective-permute-start | bytes 3145736 | tf_op jit(solution)/shard_map/ppermute | solution.py:635
  199.9 150.3 %collective-permute-start.40 = (bf16[2,4,32,3072]{3,2,1,0:T(8,128)(2,1)}, bf16[2,4,32,3072]{3,2,1,0:T(8,128)(2,1)}, u32[]{:S(2)}, u32[]{:S(2)}) collective-permute-start(bf16[2,4,32,3072]{3,2,1,0:T(8,128)(2,1)} %get-tuple-element.90), channel_id=1, source_target_pairs={{0,8},{8,0},{16,24},{24,16},{1,9},{9,1},{17,25},{25,17},{2,10},{10... | collective-permute-start | bytes 4718600 | tf_op jit(solution)/shard_map/ppermute | solution.py:496
  202.5 133.4 %collective-permute-start.72 = (bf16[32,1536]{1,0:T(8,128)(2,1)S(1)}, bf16[32,1536]{1,0:T(8,128)(2,1)S(1)}, u32[]{:S(2)}, u32[]{:S(2)}) collective-permute-start(bf16[32,1536]{1,0:T(8,128)(2,1)S(1)} %get-tuple-element.146), channel_id=1, source_target_pairs={{0,2},{1,3},{2,4},{3,5},{4,6},{5,7},{6,0},{7,1},{8,10},{9,11},{10,... | collective-permute-start | bytes 294920 | tf_op jit(solution)/shard_map/ppermute | solution.py:492
  204.6 133.0 %collective-permute-start.73 = (bf16[32,1536]{1,0:T(8,128)(2,1)S(1)}, bf16[32,1536]{1,0:T(8,128)(2,1)S(1)}, u32[]{:S(2)}, u32[]{:S(2)}) collective-permute-start(bf16[32,1536]{1,0:T(8,128)(2,1)S(1)} %get-tuple-element.148), channel_id=1, source_target_pairs={{0,4},{1,5},{2,6},{3,7},{4,0},{5,1},{6,2},{7,3},{8,12},{9,13},{10,... | collective-permute-start | bytes 294920 | tf_op jit(solution)/shard_map/ppermute | solution.py:492
  204.6 134.3 %collective-permute-start.74 = (bf16[32,1536]{1,0:T(8,128)(2,1)S(1)}, bf16[32,1536]{1,0:T(8,128)(2,1)S(1)}, u32[]{:S(2)}, u32[]{:S(2)}) collective-permute-start(bf16[32,1536]{1,0:T(8,128)(2,1)S(1)} %get-tuple-element.147), channel_id=1, source_target_pairs={{0,6},{1,7},{2,0},{3,1},{4,2},{5,3},{6,4},{7,5},{8,14},{9,15},{10,... | collective-permute-start | bytes 294920 | tf_op jit(solution)/shard_map/ppermute | solution.py:492
  335.9 37.8 %collective-permute-start.53 = (bf16[1024,512]{1,0:T(8,128)(2,1)}, bf16[1024,512]{1,0:T(8,128)(2,1)}, u32[]{:S(2)}, u32[]{:S(2)}) collective-permute-start(bf16[1024,512]{1,0:T(8,128)(2,1)} %get-tuple-element.91.g_ref.own2), channel_id=1, source_target_pairs={{8,16},{9,17},{10,18},{11,19},{12,20},{13,21},{14,22},{15,23}} | collective-permute-start | bytes 3145736 | tf_op jit(solution)/shard_map/ppermute | solution.py:635
  337.6 38.3 %collective-permute-start.49 = (bf16[1024,512]{1,0:T(8,128)(2,1)}, bf16[1024,512]{1,0:T(8,128)(2,1)S(1)}, u32[]{:S(2)}, u32[]{:S(2)}) collective-permute-start(bf16[1024,512]{1,0:T(8,128)(2,1)} %get-tuple-element.91.g_ref.own2), channel_id=1, source_target_pairs={{0,16},{1,17},{2,18},{3,19},{4,20},{5,21},{6,22},{7,23}} | collective-permute-start | bytes 3145736 | tf_op jit(solution)/shard_map/ppermute | solution.py:635
  338.9 51.8 %collective-permute-start.50 = (bf16[1024,512]{1,0:T(8,128)(2,1)}, bf16[1024,512]{1,0:T(8,128)(2,1)}, u32[]{:S(2)}, u32[]{:S(2)}) collective-permute-start(bf16[1024,512]{1,0:T(8,128)(2,1)} %get-tuple-element.88.g_ref.own3), channel_id=1, source_target_pairs={{8,24},{9,25},{10,26},{11,27},{12,28},{13,29},{14,30},{15,31}} | collective-permute-start | bytes 3145736 | tf_op jit(solution)/shard_map/ppermute | solution.py:635
  351.5 20.5 %collective-permute-start.41 = (bf16[4,32,3072]{2,1,0:T(8,128)(2,1)S(1)}, bf16[4,32,3072]{2,1,0:T(8,128)(2,1)}, u32[]{:S(2)}, u32[]{:S(2)}) collective-permute-start(bf16[4,32,3072]{2,1,0:T(8,128)(2,1)S(1)} %fusion), channel_id=1, source_target_pairs={{0,1},{1,0},{2,3},{3,2},{4,5},{5,4},{6,7},{7,6},{8,9},{9,8},{10,11... | collective-permute-start | bytes 2359304 | tf_op jit(solution)/shard_map/ppermute | solution.py:496
  372.0 24.4 %collective-permute-start.63 = (bf16[2,4,32,3072]{3,2,1,0:T(8,128)(2,1)}, bf16[2,4,32,3072]{3,2,1,0:T(8,128)(2,1)}, u32[]{:S(2)}, u32[]{:S(2)}) collective-permute-start(bf16[2,4,32,3072]{3,2,1,0:T(8,128)(2,1)} %get-tuple-element.104), channel_id=1, source_target_pairs={{0,8},{8,0},{16,24},{24,16},{1,9},{9,1},{17,25},{25,17},{2,10},{10... | collective-permute-start | bytes 4718600 | tf_op jit(solution)/shard_map/ppermute | solution.py:496
  373.7 18.7 %collective-permute-start.79 = (bf16[32,3072]{1,0:T(8,128)(2,1)S(1)}, bf16[32,3072]{1,0:T(8,128)(2,1)}, u32[]{:S(2)}, u32[]{:S(2)}) collective-permute-start(bf16[32,3072]{1,0:T(8,128)(2,1)S(1)} %get-tuple-element.139), channel_id=1, source_target_pairs={{0,4},{1,5},{2,6},{3,7},{4,0},{5,1},{6,2},{7,3},{8,12},{9,13},{10,... | collective-permute-start | bytes 589832 | tf_op jit(solution)/shard_map/ppermute | solution.py:492
  393.5 47.3 %collective-permute-start.51 = (bf16[1024,512]{1,0:T(8,128)(2,1)}, bf16[1024,512]{1,0:T(8,128)(2,1)S(1)}, u32[]{:S(2)}, u32[]{:S(2)}) collective-permute-start(bf16[1024,512]{1,0:T(8,128)(2,1)} %get-tuple-element.100.own0), channel_id=1, source_target_pairs={{24,0},{25,1},{26,2},{27,3},{28,4},{29,5},{30,6},{31,7}} | collective-permute-start | bytes 3145736 | tf_op jit(solution)/shard_map/ppermute | solution.py:635
  396.5 49.5 %collective-permute-start.47 = (bf16[1024,512]{1,0:T(8,128)(2,1)}, bf16[1024,512]{1,0:T(8,128)(2,1)S(1)}, u32[]{:S(2)}, u32[]{:S(2)}) collective-permute-start(bf16[1024,512]{1,0:T(8,128)(2,1)} %get-tuple-element.100.own0), channel_id=1, source_target_pairs={{16,0},{17,1},{18,2},{19,3},{20,4},{21,5},{22,6},{23,7}} | collective-permute-start | bytes 3145736 | tf_op jit(solution)/shard_map/ppermute | solution.py:635
  399.1 49.5 %collective-permute-start.45 = (bf16[1024,512]{1,0:T(8,128)(2,1)S(1)}, bf16[1024,512]{1,0:T(8,128)(2,1)S(1)}, u32[]{:S(2)}, u32[]{:S(2)}) collective-permute-start(bf16[1024,512]{1,0:T(8,128)(2,1)S(1)} %copy-done.4), channel_id=1, source_target_pairs={{24,16},{25,17},{26,18},{27,19},{28,20},{29,21},{30,22},{31,23}} | collective-permute-start | bytes 3145736 | tf_op jit(solution)/shard_map/ppermute | solution.py:635
  399.9 49.7 %collective-permute-start.46 = (bf16[1024,512]{1,0:T(8,128)(2,1)}, bf16[1024,512]{1,0:T(8,128)(2,1)S(1)}, u32[]{:S(2)}, u32[]{:S(2)}) collective-permute-start(bf16[1024,512]{1,0:T(8,128)(2,1)} %get-tuple-element.88.g_ref.own3), channel_id=1, source_target_pairs={{16,24},{17,25},{18,26},{19,27},{20,28},{21,29},{22,30},{23,31}} | collective-permute-start | bytes 3145736 | tf_op jit(solution)/shard_map/ppermute | solution.py:635
  400.6 48.9 %collective-permute-start.44 = (bf16[1024,512]{1,0:T(8,128)(2,1)S(1)}, bf16[1024,512]{1,0:T(8,128)(2,1)S(1)}, u32[]{:S(2)}, u32[]{:S(2)}) collective-permute-start(bf16[1024,512]{1,0:T(8,128)(2,1)S(1)} %copy-done.5), channel_id=1, source_target_pairs={{0,8},{1,9},{2,10},{3,11},{4,12},{5,13},{6,14},{7,15}} | collective-permute-start | bytes 3145736 | tf_op jit(solution)/shard_map/ppermute | solution.py:635
  448.6 35.0 %collective-permute-start.75 = (bf16[32,1536]{1,0:T(8,128)(2,1)S(1)}, bf16[32,1536]{1,0:T(8,128)(2,1)S(1)}, u32[]{:S(2)}, u32[]{:S(2)}) collective-permute-start(bf16[32,1536]{1,0:T(8,128)(2,1)S(1)} %add_convert_fusion.7.refs_8_), channel_id=1, source_target_pairs={{0,8},{8,0},{16,24},{24,16},{1,9},{9,1},{17,25},{25,17},{2,10},{10... | collective-permute-start | bytes 294920 | tf_op jit(solution)/shard_map/ppermute | solution.py:496
  449.5 34.2 %collective-permute-start.76 = (bf16[32,1536]{1,0:T(8,128)(2,1)S(1)}, bf16[32,1536]{1,0:T(8,128)(2,1)S(1)}, u32[]{:S(2)}, u32[]{:S(2)}) collective-permute-start(bf16[32,1536]{1,0:T(8,128)(2,1)S(1)} %add_convert_fusion.7.refs_8_), channel_id=1, source_target_pairs={{0,16},{8,24},{16,0},{24,8},{1,17},{9,25},{17,1},{25,9},{2,18},{10... | collective-permute-start | bytes 294920 | tf_op jit(solution)/shard_map/ppermute | solution.py:496
  449.6 25.7 %collective-permute-start.64 = (bf16[4,32,3072]{2,1,0:T(8,128)(2,1)S(1)}, bf16[4,32,3072]{2,1,0:T(8,128)(2,1)S(1)}, u32[]{:S(2)}, u32[]{:S(2)}) collective-permute-start(bf16[4,32,3072]{2,1,0:T(8,128)(2,1)S(1)} %fusion.1), channel_id=1, source_target_pairs={{0,1},{1,0},{2,3},{3,2},{4,5},{5,4},{6,7},{7,6},{8,9},{9,8},{10,11... | collective-permute-start | bytes 2359304 | tf_op jit(solution)/shard_map/ppermute | solution.py:496
  458.5 19.3 %collective-permute-start.57 = (bf16[32,1664]{1,0:T(8,128)(2,1)S(1)}, bf16[32,1664]{1,0:T(8,128)(2,1)S(1)}, u32[]{:S(2)}, u32[]{:S(2)}) collective-permute-start(bf16[32,1664]{1,0:T(8,128)(2,1)S(1)} %get-tuple-element.143), channel_id=1, source_target_pairs={{0,2},{1,3},{2,4},{3,5},{4,6},{5,7},{6,0},{7,1},{8,10},{9,11},{10,... | collective-permute-start | bytes 319496 | tf_op jit(solution)/shard_map/ppermute | solution.py:492
  460.1 18.6 %collective-permute-start.58 = (bf16[32,1664]{1,0:T(8,128)(2,1)S(1)}, bf16[32,1664]{1,0:T(8,128)(2,1)S(1)}, u32[]{:S(2)}, u32[]{:S(2)}) collective-permute-start(bf16[32,1664]{1,0:T(8,128)(2,1)S(1)} %get-tuple-element.145), channel_id=1, source_target_pairs={{0,4},{1,5},{2,6},{3,7},{4,0},{5,1},{6,2},{7,3},{8,12},{9,13},{10,... | collective-permute-start | bytes 319496 | tf_op jit(solution)/shard_map/ppermute | solution.py:492
  496.1 135.1 %collective-permute-start.61 = (bf16[32,1664]{1,0:T(8,128)(2,1)S(1)}, bf16[32,1664]{1,0:T(8,128)(2,1)S(1)}, u32[]{:S(2)}, u32[]{:S(2)}) collective-permute-start(bf16[32,1664]{1,0:T(8,128)(2,1)S(1)} %add_convert_fusion.6.refs_0_), channel_id=1, source_target_pairs={{0,16},{8,24},{16,0},{24,8},{1,17},{9,25},{17,1},{25,9},{2,18},{10... | collective-permute-start | bytes 319496 | tf_op jit(solution)/shard_map/ppermute | solution.py:496
  498.3 133.0 %collective-permute-start.62 = (bf16[32,1664]{1,0:T(8,128)(2,1)S(1)}, bf16[32,1664]{1,0:T(8,128)(2,1)S(1)}, u32[]{:S(2)}, u32[]{:S(2)}) collective-permute-start(bf16[32,1664]{1,0:T(8,128)(2,1)S(1)} %add_convert_fusion.6.refs_0_), channel_id=1, source_target_pairs={{0,24},{8,16},{16,8},{24,0},{1,25},{9,17},{17,9},{25,1},{2,26},{10... | collective-permute-start | bytes 319496 | tf_op jit(solution)/shard_map/ppermute | solution.py:496
  498.3 133.0 %collective-permute-start.68 = (bf16[32,3072]{1,0:T(8,128)(2,1)S(1)}, bf16[32,3072]{1,0:T(8,128)(2,1)S(1)}, u32[]{:S(2)}, u32[]{:S(2)}) collective-permute-start(bf16[32,3072]{1,0:T(8,128)(2,1)S(1)} %add_convert_fusion.5.refs_4_), channel_id=1, source_target_pairs={{0,8},{8,0},{16,24},{24,16},{1,9},{9,1},{17,25},{25,17},{2,10},{10... | collective-permute-start | bytes 589832 | tf_op jit(solution)/shard_map/ppermute | solution.py:496
  502.1 129.2 %collective-permute-start.69 = (bf16[32,3072]{1,0:T(8,128)(2,1)S(1)}, bf16[32,3072]{1,0:T(8,128)(2,1)S(1)}, u32[]{:S(2)}, u32[]{:S(2)}) collective-permute-start(bf16[32,3072]{1,0:T(8,128)(2,1)S(1)} %add_convert_fusion.5.refs_4_), channel_id=1, source_target_pairs={{0,16},{8,24},{16,0},{24,8},{1,17},{9,25},{17,1},{25,9},{2,18},{10... | collective-permute-start | bytes 589832 | tf_op jit(solution)/shard_map/ppermute | solution.py:496
  502.1 129.2 %collective-permute-start.70 = (bf16[32,3072]{1,0:T(8,128)(2,1)S(1)}, bf16[32,3072]{1,0:T(8,128)(2,1)S(1)}, u32[]{:S(2)}, u32[]{:S(2)}) collective-permute-start(bf16[32,3072]{1,0:T(8,128)(2,1)S(1)} %add_convert_fusion.5.refs_4_), channel_id=1, source_target_pairs={{0,24},{8,16},{16,8},{24,0},{1,25},{9,17},{17,9},{25,1},{2,26},{10... | collective-permute-start | bytes 589832 | tf_op jit(solution)/shard_map/ppermute | solution.py:496
  (86 other events, 2356.2 us)

commit v3 on v2

--- a/solution.py
+++ b/solution.py
@@ -56,7 +56,8 @@
         other_y, other_core = at % 2, at // 2
         for z in range(4):
             place = order_of(ids, z, other_y, other_core)
-            wqkv[pl.ds(pl.multiple_of(place * 32, 32), 32), :] = ref[z, :, :1152]
+            if wqkv is not None:
+                wqkv[pl.ds(pl.multiple_of(place * 32, 32), 32), :] = ref[z, :, :1152]
             shard = z * 2 + (ids[1] ^ other_y)
             core = ids[2] ^ other_core
             for i in range(3):
@@ -71,7 +72,8 @@
         other_y, other_core = at % 2, at // 2
         for z in range(4):
             place = order_of(ids, z, other_y, other_core)
-            wgu[pl.ds(pl.multiple_of(place * 32, 32), 32), :] = ref[z, :, :2048]
+            if wgu is not None:
+                wgu[pl.ds(pl.multiple_of(place * 32, 32), 32), :] = ref[z, :, :2048]
             for i in range(2):
                 wd[pl.ds(pl.multiple_of(place * 64 + i * 32, 32), 32), :] = (
                     ref[z, :, 2048 + i * 512:2560 + i * 512])
@@ -81,7 +83,7 @@
     for other_core, ref in enumerate((keep_ref, give_ref)):
         for other_y in range(2):
             for by in range(4):
-                place = order_of(ids, (ids[0] + by) & 3, other_y, other_core)
+                place = order_of(ids, ids[0] ^ by, other_y, other_core)
                 ref[other_y, by] = packed[pl.ds(pl.multiple_of(place * 32, 32), 32), :]
 
 
@@ -118,15 +120,28 @@
     out_ref[...] = (x + dot_nn(att, wo[...])).astype(bf)
 
 
-def norm_back(x_ref, gain_ref, gx, g_low, a_ref, dgain):
+def normed(x_ref, gain_ref):
+    x = x_ref[...].astype(f32)
+    return (x * row_scale(x) * gain_ref[...]).astype(bf)
+
+
+def input_grad_kernel(ids, x_ref, back_ref, g_ref, gain_ref, w0, w1, w2, w3, gin_ref, w_s):
+    width = back_ref.shape[1]
+
+    @pl.when(pl.program_id(0) == 0)
+    def _():
+        for at, ref in enumerate((w0, w1, w2, w3)):
+            for z in range(4):
+                place = order_of(ids, z, at % 2, at // 2)
+                w_s[pl.ds(pl.multiple_of(place * 32, 32), 32), :] = ref[z, :, :width]
+
+    gx = dot_nt(back_ref[...], w_s[...])
     x = x_ref[...].astype(f32)
     scale = row_scale(x)
     n = x * scale
-    a_ref[...] = (n * gain_ref[...]).astype(bf)
-    dgain[...] += jnp.sum(gx * n, axis=0, keepdims=True)
     e = gx * gain_ref[...]
     dx = scale * (e - n * jnp.mean(e * n, axis=-1, keepdims=True))
-    return (g_low.astype(f32) + dx).astype(bf)
+    gin_ref[...] = (g_ref[...].astype(f32) + dx).astype(bf)
 
 
 def bucket_of(key, query):
@@ -160,17 +175,16 @@
 
 
 def attn_bwd_kernel(ids, x_ref, q_ref, k_ref, v_ref, p_ref, att_ref, g_ref, gain_ref, w0, w1, w2, w3,
-                    gains_in, bias_in, gin_ref, keep_ref, give_ref, dgain_ref, dbias_ref,
-                    wqkv, wo, a_s, dqkv_s, att_s, g_s, dgain_s, dbias_s, packed):
+                    bias_in, back_ref, keep_ref, give_ref, dbias_ref,
+                    wo, a_s, dqkv_s, att_s, g_s, dbias_s, packed):
     step = pl.program_id(0)
     last = pl.num_programs(0) - 1
     block = x_ref.shape[0]
-    with_small = keep_ref.shape[3] > 1536
+    with_table = keep_ref.shape[3] > 1536
 
     @pl.when(step == 0)
     def _():
-        open_attn(ids, (w0, w1, w2, w3), wqkv, wo)
-        dgain_s[...] = jnp.zeros_like(dgain_s)
+        open_attn(ids, (w0, w1, w2, w3), None, wo)
         dbias_s[...] = bias_in[...]
 
     here = pl.ds(pl.multiple_of(step * block, block), block)
@@ -178,6 +192,7 @@
     da = dot_nt(g_low, wo[...]).astype(bf)
     att_s[here, :] = att_ref[...]
     g_s[here, :] = g_low
+    a_s[here, :] = normed(x_ref, gain_ref)
     rows = block // 64
     units = [(r, h) for r in range(rows) for h in range(3)]
     at = lambda arr, r, h: arr[r * 64:r * 64 + 64, h * 128:h * 128 + 128]
@@ -198,10 +213,9 @@
         [jnp.concatenate([u[r, h] for u in (dq_u, dk_u, dv_u) for h in range(3)], axis=1)
          for r in range(rows)], axis=0)
     dqkv_s[here, :] = dqkv
+    back_ref[...] = dqkv
     for h in range(3):
         dbias_s[:, h * 128:h * 128 + 128] += db[h]
-    gx = dot_nt(dqkv, wqkv[...])
-    gin_ref[...] = norm_back(x_ref, gain_ref, gx, g_low, a_s.at[here, :], dgain_s)
 
     @pl.when(step == last)
     def _():
@@ -217,19 +231,11 @@
                                1152 + i * 128:1280 + i * 128] = (
                             dwo[shard * 48 + i * 16:shard * 48 + i * 16 + 16,
                                 core * 256 + j * 128:core * 256 + j * 128 + 128])
-        dgain_ref[...] = dgain_s[...]
         dbias_ref[...] = dbias_s[...]
-        if with_small:
+        if with_table:
             table = table_terms(dbias_s[...]).astype(bf)
-            terms = jnp.concatenate([dgain_s[...], gains_in[...]], axis=0)
-            row = lax.broadcasted_iota(jnp.int32, (32, 128), 0)
-            for shard in range(8):
-                spot = slice(shard * 64, shard * 64 + 64)
-                first = jnp.concatenate([terms[0:1, spot], terms[1:2, spot]], axis=1)
-                second = jnp.concatenate([terms[2:3, spot], terms[3:4, spot]], axis=1)
-                small = jnp.where(row == 0, first, jnp.where(row == 1, second, 0.0)).astype(bf)
-                packed[shard * 64:shard * 64 + 32, 1536:1664] = small
-                packed[shard * 64 + 32:shard * 64 + 64, 1536:1664] = table
+            for at in range(16):
+                packed[at * 32:at * 32 + 32, 1536:1664] = table
         hand_out(ids, packed, keep_ref, give_ref)
 
 
@@ -265,20 +271,19 @@
 
 
 def ffn_bwd_kernel(ids, x_ref, gate_ref, up_ref, g_ref, gain_ref, w0, w1, w2, w3,
-                   gin_ref, keep_ref, give_ref, dgain_ref,
-                   wgu, wd, a_s, gub_s, hid_s, g_s, dgain_s, packed):
+                   back_ref, keep_ref, give_ref, wd, a_s, gub_s, hid_s, g_s, packed):
     step = pl.program_id(0)
     last = pl.num_programs(0) - 1
     block = x_ref.shape[0]
 
     @pl.when(step == 0)
     def _():
-        open_ffn(ids, (w0, w1, w2, w3), wgu, wd)
-        dgain_s[...] = jnp.zeros_like(dgain_s)
+        open_ffn(ids, (w0, w1, w2, w3), None, wd)
 
     here = pl.ds(pl.multiple_of(step * block, block), block)
     g_low = g_ref[...]
     g_s[here, :] = g_low
+    a_s[here, :] = normed(x_ref, gain_ref)
     hg = dot_nt(g_low, wd[...])
     gate = gate_ref[...].astype(f32)
     up = up_ref[...].astype(f32)
@@ -288,8 +293,8 @@
     ub = (hg * act).astype(bf)
     gub_s[here, :1024] = gb
     gub_s[here, 1024:] = ub
-    gx = dot_nt(gb, wgu[:, :1024]) + dot_nt(ub, wgu[:, 1024:])
-    gin_ref[...] = norm_back(x_ref, gain_ref, gx, g_low, a_s.at[here, :], dgain_s)
+    back_ref[:, :1024] = gb
+    back_ref[:, 1024:] = ub
 
     @pl.when(step == last)
     def _():
@@ -302,7 +307,6 @@
                 for i in range(2):
                     packed[(h * 8 + at) * 32:(h * 8 + at) * 32 + 32, 2048 + i * 512:2560 + i * 512] = (
                         dwd[at * 64 + i * 32:at * 64 + i * 32 + 32])
-        dgain_ref[...] = dgain_s[...]
         hand_out(ids, packed, keep_ref, give_ref)
 
 
@@ -344,24 +348,35 @@
         [tok(block, d)] + [tok(block, 384)] * 5,
         [sds((t, d), bf)] + [sds((t, 384), bf)] * 5,
         [pltpu.VMEM((512, 1152), bf), pltpu.VMEM((384, 512), bf)],
-        7, "attn_fwd")(ids, x, mask, bias, gain, *parts)
-
-
-def attn_bwd(ids, x, q, k, v, p, att, g, gain, parts, gains_in, bias_in, with_small):
+        4, "attn_fwd")(ids, x, mask, bias, gain, *parts)
+
+
+def attn_bwd(ids, x, q, k, v, p, att, g, gain, parts, bias_in, with_table):
     t, d = x.shape
     block = token_block
-    n = 1664 if with_small else 1536
+    n = 1664 if with_table else 1536
     packed = (2, 4, 32, n)
     return call(
         attn_bwd_kernel, t // block,
         [tok(block, d)] + [tok(block, 384)] * 5 + [tok(block, d), full((1, d))]
-        + [full(parts[0].shape)] * 4 + [full(gains_in.shape), full(bias_in.shape)],
-        [tok(block, d), full(packed), full(packed), full((1, d)), full((64, 384))],
-        [sds((t, d), bf), sds(packed, bf), sds(packed, bf), sds((1, d), f32), sds((64, 384), f32)],
-        [pltpu.VMEM((512, 1152), bf), pltpu.VMEM((384, 512), bf), pltpu.VMEM((t, d), bf),
+        + [full(parts[0].shape)] * 4 + [full(bias_in.shape)],
+        [tok(block, 1152), full(packed), full(packed), full((64, 384))],
+        [sds((t, 1152), bf), sds(packed, bf), sds(packed, bf), sds((64, 384), f32)],
+        [pltpu.VMEM((384, 512), bf), pltpu.VMEM((t, d), bf),
          pltpu.VMEM((t, 1152), bf), pltpu.VMEM((t, 384), bf), pltpu.VMEM((t, d), bf),
-         pltpu.VMEM((1, d), f32), pltpu.VMEM((64, 384), f32), pltpu.VMEM((512, n), bf)],
-        12, "attn_bwd")(ids, x, q, k, v, p, att, g, gain, *parts, gains_in, bias_in)
+         pltpu.VMEM((64, 384), f32), pltpu.VMEM((512, n), bf)],
+        6, "attn_bwd")(ids, x, q, k, v, p, att, g, gain, *parts, bias_in)
+
+
+def input_grad(ids, x, back, g, gain, parts):
+    t, d = x.shape
+    block = token_block
+    width = back.shape[1]
+    return call(
+        input_grad_kernel, t // block,
+        [tok(block, d), tok(block, width), tok(block, d), full((1, d))] + [full(parts[0].shape)] * 4,
+        [tok(block, d)], [sds((t, d), bf)], [pltpu.VMEM((512, width), bf)],
+        20, "input_grad")(ids, x, back, g, gain, *parts)[0]
 
 
 def ffn_fwd(ids, x, gain, parts):
@@ -373,7 +388,7 @@
         [tok(block, d), tok(block, 1024), tok(block, 1024)],
         [sds((t, d), bf), sds((t, 1024), bf), sds((t, 1024), bf)],
         [pltpu.VMEM((512, 2048), bf), pltpu.VMEM((1024, 512), bf)],
-        7, "ffn_fwd")(ids, x, gain, *parts)
+        4, "ffn_fwd")(ids, x, gain, *parts)
 
 
 def ffn_bwd(ids, x, gate, up, g, gain, parts):
@@ -384,16 +399,19 @@
         ffn_bwd_kernel, t // block,
         [tok(block, d), tok(block, 1024), tok(block, 1024), tok(block, d), full((1, d))]
         + [full(parts[0].shape)] * 4,
-        [tok(block, d), full(packed), full(packed), full((1, d))],
-        [sds((t, d), bf), sds(packed, bf), sds(packed, bf), sds((1, d), f32)],
-        [pltpu.VMEM((512, 2048), bf), pltpu.VMEM((1024, 512), bf), pltpu.VMEM((t, d), bf),
+        [tok(block, 2048), full(packed), full(packed)],
+        [sds((t, 2048), bf), sds(packed, bf), sds(packed, bf)],
+        [pltpu.VMEM((1024, 512), bf), pltpu.VMEM((t, d), bf),
          pltpu.VMEM((t, 2048), bf), pltpu.VMEM((t, 1024), bf), pltpu.VMEM((t, d), bf),
-         pltpu.VMEM((1, d), f32), pltpu.VMEM((512, 3072), bf)],
-        15, "ffn_bwd")(ids, x, gate, up, g, gain, *parts)
-
-
-def pack_kernel(ids, q, k, v, o, gate, up, down, a0, f0, a1, f1):
+         pltpu.VMEM((512, 3072), bf)],
+        6, "ffn_bwd")(ids, x, gate, up, g, gain, *parts)
+
+
+def pack_kernel(ids, q, k, v, o, gate, up, down, gains, a0, f0, a1, f1):
     core = ids[2]
+    row = lax.broadcasted_iota(jnp.int32, (32, 128), 0)
+    pair = [jnp.concatenate([gains[l, 0:1, :], gains[l, 1:2, :]], axis=1) for l in range(2)]
+    a0[:, 1536:] = jnp.where(row == 0, pair[0], jnp.where(row == 1, pair[1], 0.0)).astype(bf)
     rows = pl.ds(pl.multiple_of(core * 32, 32), 32)
     for layer, a_ref, f_ref in ((0, a0, f0), (1, a1, f1)):
         for at, w in enumerate((q, k, v)):
@@ -411,79 +429,124 @@
 
 
 def pack_weights(ids, *weights):
+    shapes = ((32, 1664), (32, 3072), (32, 1536), (32, 3072))
     return call(
-        pack_kernel, 1, [full(w.shape) for w in weights],
-        [full((32, 1536)), full((32, 3072))] * 2,
-        [sds((32, 1536), bf), sds((32, 3072), bf)] * 2, [], 2, "pack_weights")(ids, *weights)
-
-
-def unpack_kernel(ids, *refs):
-    sums, outs = refs[:16], refs[16:]
-    q, k, v, o, gate, up, down, gains, table = outs
+        pack_kernel, 1, [full(w.shape) for w in weights], [full(shape) for shape in shapes],
+        [sds(shape, bf) for shape in shapes], [], 2, "pack_weights")(ids, *weights)
+
+
+def unpack_kernel(ids, own, peer, qw, kw, vw, gw, uw, gain, q, k, v, o, gate, up, down, gains, table):
     first = ids[2] == 0
-    for s in range(4):
-        own, near, far, cross = (ref[...].astype(f32) for ref in sums[s * 4:s * 4 + 4])
-        mine, peer = own + far, near + cross
-        halves = (jnp.where(first, mine, peer), jnp.where(first, peer, mine))
+    base = 0
+
+    def row_sums(*pairs):
+        total = None
+        for weight, grad in pairs:
+            term = weight.astype(f32) * grad
+            total = term if total is None else total + term
+        ones = jnp.ones((8, total.shape[1]), f32)
+        sums = lax.dot_general(ones, total, (((1,), (1,)), ((), ())), preferred_element_type=f32,
+                               precision=lax.Precision.HIGHEST)
+        return sums[0:1, :]
+
+    for s in (3, 2, 1, 0):
         layer = s // 2
         for core in range(2):
-            part = halves[core]
+            def part(start, width, rows=slice(0, 32)):
+                columns = slice(base + start, base + start + width)
+                one, two = own[rows, columns].astype(f32), peer[rows, columns].astype(f32)
+                return jnp.where(first, one, two) if core == 0 else jnp.where(first, two, one)
+
             rows = slice(core * 32, core * 32 + 32)
             if s % 2 == 0:
                 for at, w in enumerate((q, k, v)):
-                    w[layer, rows, :] = part[:, at * 384:at * 384 + 384]
+                    w[layer, rows, :] = part(at * 384, 384)
                 for i in range(3):
                     for j in range(2):
                         o[layer, i * 16:i * 16 + 16, core * 256 + j * 128:core * 256 + j * 128 + 128] = (
-                            part[j * 16:j * 16 + 16, 1152 + i * 128:1280 + i * 128])
+                            part(1152 + i * 128, 128, slice(j * 16, j * 16 + 16)))
             else:
-                gate[layer, rows, :] = part[:, :1024]
-                up[layer, rows, :] = part[:, 1024:2048]
+                gate[layer, rows, :] = part(0, 1024)
+                up[layer, rows, :] = part(1024, 1024)
                 for i in range(2):
-                    down[layer, core * 64 + i * 32:core * 64 + i * 32 + 32, :] = (
-                        part[:, 2048 + i * 512:2560 + i * 512])
-        if s == 0:
-            for l in range(2):
-                for n in range(2):
-                    gains[l, n:n + 1, :] = halves[0][l:l + 1, 1536 + n * 64:1600 + n * 64]
-            table[...] = halves[1][:, 1536:1542]
-
-
-def unpack_grads(ids, sums, shapes):
-    flat = [array for part in sums for array in part]
+                    down[layer, core * 64 + i * 32:core * 64 + i * 32 + 32, :] = part(2048 + i * 512, 512)
+            if s == 0 and core == 1:
+                table[...] = part(1536, 128)[:, :6]
+        if s % 2 == 0:
+            sums = row_sums(*((w[layer], grad[layer]) for w, grad in ((qw, q), (kw, k), (vw, v))))
+        else:
+            sums = row_sums(*((w[layer], grad[layer]) for w, grad in ((gw, gate), (uw, up))))
+        gains[layer, s % 2:s % 2 + 1, :] = sums / gain[layer, s % 2:s % 2 + 1, :]
+        base += 1536 if s % 2 == 0 else 3072
+
+
+def unpack_grads(ids, own, peer, shards, gains, shapes):
+    q, k, v, o, gate, up, down = shards
+    args = (own, peer, q, k, v, gate, up, gains)
     return call(
-        unpack_kernel, 1, [full(array.shape) for array in flat], [full(shape) for shape in shapes],
-        [sds(shape, f32) for shape in shapes], [], 3, "unpack_grads")(ids, *flat)
-
-
-def place_kernel(ids, own0, own1, own2, own3, near, far, cross, out, sems):
+        unpack_kernel, 1, [full(array.shape) for array in args], [full(shape) for shape in shapes],
+        [sds(shape, f32) for shape in shapes], [], 3, "unpack_grads")(ids, *args)
+
+
+def move(sources, scratch, targets, sems):
+    def fetch(ref, at):
+        return pltpu.make_async_copy(ref, scratch.at[at], sems.at[0, at])
+
+    for at, options in enumerate(sources):
+        for condition, ref in options:
+            if condition is None:
+                fetch(ref, at).start()
+            else:
+                @pl.when(condition)
+                def _(ref=ref, at=at):
+                    fetch(ref, at).start()
+    for at, target in enumerate(targets):
+        fetch(sources[at][0][1], at).wait()
+        pltpu.make_async_copy(scratch.at[at], target, sems.at[1, at]).start()
+    for at, target in enumerate(targets):
+        pltpu.make_async_copy(scratch.at[at], target, sems.at[1, at]).wait()
+
+
+def place_kernel(ids, *refs):
+    own, relay, far, cross = refs[:4], refs[4], refs[5:9], refs[9:-3]
+    out, scratch, sems = refs[-3:]
+    cross = cross + (relay.at[1],) * (4 - len(cross))
     section = ids[3]
-    def copy(ref, slot, sem):
-        return pltpu.make_async_copy(ref, out.at[slot], sems.at[sem])
-    for at, ref in enumerate((own0, own1, own2, own3)):
-        @pl.when(section == at)
-        def _(ref=ref):
-            copy(ref, section, 0).start()
-    copy(near, section ^ 1, 1).start()
-    copy(far, section ^ 2, 2).start()
-    copy(cross, section ^ 3, 3).start()
-    copy(near, section, 0).wait()
-    copy(near, section ^ 1, 1).wait()
-    copy(far, section ^ 2, 2).wait()
-    copy(cross, section ^ 3, 3).wait()
-
-
-def place(ids, own, others):
+    pick = lambda group: [(section == at, ref) for at, ref in enumerate(group)]
+    move([pick(own), [(None, relay.at[0])], pick(far), pick(cross)], scratch,
+         [out.at[section ^ bit] for bit in range(4)], sems)
+
+
+def moving(kernel, ids, arrays, out_shape, slots, micros, name):
+    anywhere = pl.BlockSpec(memory_space=pl.ANY)
+    t, d = arrays[0].shape[-2:]
+    return pl.pallas_call(
+        kernel,
+        grid_spec=pltpu.PrefetchScalarGridSpec(
+            num_scalar_prefetch=1, grid=(1,), in_specs=[anywhere] * len(arrays), out_specs=anywhere,
+            scratch_shapes=[pltpu.VMEM((slots, t, d), bf), pltpu.SemaphoreType.DMA((2, slots))]),
+        out_shape=out_shape, name=name,
+        compiler_params=pltpu.CompilerParams(vmem_limit_bytes=vmem_limit),
+        cost_estimate=pl.CostEstimate(flops=int(micros * 1.1e9), bytes_accessed=0, transcendentals=0),
+    )(ids, *arrays)
+
+
+def place(ids, own, relay, far, cross):
+    arrays = (*own, relay, *far, *cross)
+    return moving(place_kernel, ids, arrays, sds((4,) + own[0].shape, bf), 4, 3, "place")
+
+
+def relay_kernel(ids, *refs):
+    own, far = refs[:4], refs[4:8]
+    out, scratch, sems = refs[8:]
+    pick = lambda group: [((ids[3] ^ 1) == at, ref) for at, ref in enumerate(group)]
+    move([pick(own), pick(far)], scratch, [out.at[0], out.at[1]], sems)
+
+
+def relay(ids, own, far):
     t, d = own[0].shape
-    anywhere = pl.BlockSpec(memory_space=pl.ANY)
-    return pl.pallas_call(
-        place_kernel,
-        grid_spec=pltpu.PrefetchScalarGridSpec(
-            num_scalar_prefetch=1, grid=(1,), in_specs=[anywhere] * 7, out_specs=anywhere,
-            scratch_shapes=[pltpu.SemaphoreType.DMA((4,))]),
-        out_shape=sds((4, t, d), bf), name="place",
-        cost_estimate=pl.CostEstimate(flops=3_000_000_000, bytes_accessed=0, transcendentals=0),
-    )(ids, *own, *others)
+    both = moving(relay_kernel, ids, (*own, *far), sds((2, t, d), bf), 2, 2, "relay")
+    return swapped(both, "section", 1)
 
 
 def z_shift(values, by):
@@ -507,20 +570,34 @@
     return total.astype(bf)
 
 
-def gather_part(piece, place_ids):
-    z = place_ids[0]
-    got = [piece] + [z_shift(piece, by) for by in range(1, 4)]
-    column = jnp.stack([lax.select_n((z - at) % 4, *got) for at in range(4)])
-    other = swapped(column, "dp", 1)
-    return (column, other, swapped(column, "section", 1), swapped(other, "section", 1)), got[-1]
-
-
-def reduce_part(keep, give):
+def gather_part(piece, z, previous):
+    if previous is not None:
+        piece = after(piece, *previous)
+    got = [z_shift(piece, by) for by in range(1, 4)]
+    column = jnp.stack([lax.select_n((z - at) % 4, piece, *got) for at in range(4)])
+    return (column, swapped(column, "dp", 1)), got
+
+
+def gather_core(column, other, hold):
+    if hold is not None:
+        column, other = lax.optimization_barrier((column, other, hold))[:2]
+    return column, other, swapped(column, "section", 1), swapped(other, "section", 1)
+
+
+def reduce_first(keep, give):
     got = swapped(give, "section", 1)
     sent = swapped(added(keep[1], got[1]), "dp", 1)
-    terms = [added(keep[0, by], got[0, by], sent[by]) for by in range(4)]
-    mine = added(terms[0], *[z_shift(terms[by], by) for by in range(1, 4)])
-    return (mine,) + tuple(swapped(mine, "section", bit) for bit in (1, 2, 3)), (got, sent)
+    far = swapped(added(keep[0, 2:], got[0, 2:], sent[2:]), "dp", 4)
+    return dict(keep=keep, core=got, y=sent, far=far)
+
+
+def reduce_near(step):
+    terms = (step["keep"][0, 1], step["core"][0, 1], step["y"][1], step["far"][1])
+    return swapped(added(*terms), "dp", 2)
+
+
+def reduce_last(step):
+    return added(step["keep"][0, 0], step["core"][0, 0], step["y"][0], step["far"][0], step["near"])
 
 
 def to_packed(q, k, v, o, gate, up, down):
@@ -546,14 +623,10 @@
     return split.reshape(512, keep.shape[3])
 
 
-def gather_small(gains):
-    z = lax.axis_index("dp") // 2
-    y = lax.axis_index("dp") % 2
-    got = [gains] + [z_shift(gains, by) for by in range(1, 4)]
-    column = jnp.stack([lax.select_n((z - at) % 4, *got) for at in range(4)])
-    other = swapped(column, "dp", 1)
-    pair = jnp.stack([jnp.where(y == 0, column, other), jnp.where(y == 0, other, column)], axis=1)
-    return pair.transpose(2, 3, 0, 1, 4).reshape(gains.shape[0], gains.shape[1], -1).astype(f32)
+def gains_of(column, other, y):
+    small = [part[:, :2, 1536:1664].reshape(4, 2, 2, 64) for part in (column, other)]
+    pair = [jnp.where(y == at, small[0], small[1]) for at in range(2)]
+    return jnp.stack(pair, axis=3).transpose(1, 2, 0, 3, 4).reshape(2, 2, 512).astype(f32)
 
 
 def body(inputs, cotangent, segments, observed, q_weight, k_weight, v_weight, o_weight,
@@ -569,20 +642,14 @@
     own_ids = jnp.stack([dp // 2, dp % 2, section % 2, section]).astype(jnp.int32)
     ids = own_ids if eight else jnp.stack([0 * dp, 0 * dp, 0 * dp, section]).astype(jnp.int32)
 
-    weights = []
+    weights = [None] * 4
     if eight:
-        pieces = pack_weights(own_ids, *shards)
-        previous = None
-        for piece in pieces:
-            if previous is not None:
-                piece = after(piece, previous)
-            parts, previous = gather_part(piece, (dp // 2,))
-            weights.append(parts)
-        gains_all = gather_small(gains)
+        pieces = pack_weights(own_ids, *shards, gains.astype(f32))
     else:
         whole = [lax.all_gather(w, "dp", axis=1, tiled=True) for w in shards]
         for layer in range(layers):
-            weights.extend(parts_of(w) for w in to_packed(*(w[layer] for w in whole)))
+            weights[2 * layer], weights[2 * layer + 1] = (
+                parts_of(w) for w in to_packed(*(w[layer] for w in whole)))
         gains_all = lax.all_gather(gains, "dp", axis=2, tiled=True).astype(f32)
 
     x = lax.dynamic_index_in_dim(inputs, section, 0, keepdims=False).reshape(tokens, width)
@@ -598,54 +665,93 @@
     bias = jnp.einsum("jib,bh->jhi", onehot, position_table.astype(f32), precision=lax.Precision.HIGHEST)
     bias = bias.reshape(seq_count, heads * seq_count)
 
+    chip = section // 2
+
+    def across(value, pairs):
+        return lax.ppermute(value, "section", pairs)
+
+    arrived = [()] * 4
+    if eight:
+        previous = None
+        for s in range(4):
+            weights[s], previous = gather_part(pieces[s], dp // 2, previous)
+            arrived[s] = previous
+        gains_all = gains_of(*weights[0], dp % 2)
+
     states, kept = [x], []
+    out_far = [None] * 4
     for s in range(4):
         gain = gains_all[s // 2, s % 2][None]
+        feed = after(states[s], *arrived[s + 1]) if s < 3 else states[s]
+        if eight:
+            weights[s] = gather_core(*weights[s], states[s] if s > 0 else None)
         if s % 2 == 0:
-            out, *saved = attn_fwd(ids, states[-1], mask, bias, gain, weights[s])
+            out, *saved = attn_fwd(ids, feed, mask, bias, gain, weights[s])
         else:
-            out, *saved = ffn_fwd(ids, states[-1], gain, weights[s])
+            out, *saved = ffn_fwd(ids, feed, gain, weights[s])
         states.append(out)
         kept.append(saved)
+        if s >= 2:
+            out_far[s] = out_far[s - 2] = swapped(jnp.where(chip == 0, out, states[s - 1]), "section", 2)
     outs = states[1:]
 
-    grads, reduced, gain_terms = [None] * 4, [None] * 4, [None] * 4
+    grads, grad_far = [None] * 4, [None] * 4
     packed, steps = [None] * 4, [None] * 4
     bias_sum = jnp.zeros((seq_count, heads * seq_count), f32)
-    for s in (3, 2, 1, 0):
+
+    def wait(value, *names):
+        others = [steps[s][name] for s, name in names] if eight else []
+        return after(value, *others) if others else value
+
+    def back_part(s, grad):
         gain = gains_all[s // 2, s % 2][None]
-        if eight and s == 1:
-            grad = after(grad, steps[3][0])
-        if eight and s == 0:
-            grad = after(grad, steps[3][1], steps[2][0])
         if s % 2 == 1:
-            grad, keep, give, gain_terms[s] = ffn_bwd(
-                ids, states[s], *kept[s], grad, gain, weights[s])
+            back, keep, give = ffn_bwd(ids, states[s], *kept[s], grad, gain, weights[s])
+            total = bias_sum
         else:
-            earlier = jnp.concatenate(gain_terms[1:]) if s == 0 else jnp.zeros((3, width), f32)
-            grad, keep, give, gain_terms[s], bias_sum = attn_bwd(
-                ids, states[s], *kept[s], grad, gain, weights[s], earlier, bias_sum, eight and s == 0)
-        grads[s] = grad
+            back, keep, give, total = attn_bwd(
+                ids, states[s], *kept[s], grad, gain, weights[s], bias_sum, eight and s == 0)
         if eight:
-            reduced[s], steps[s] = reduce_part(keep, give)
+            steps[s] = reduce_first(keep, give)
         else:
             packed[s] = whole_of(keep, give)
-
-    def sent(values, s):
-        return [lax.ppermute(values[s], "section", [(s ^ bit, s)]) for bit in (1, 2, 3)]
-
-    def placed(values):
-        arrived = [sent(values, s) for s in range(4)]
-        others = [lax.select_n(section, *[arrived[s][at] for s in range(4)]) for at in range(3)]
-        full_set = place(ids, values, others)
-        return full_set.reshape(1, micro_count, row_count, seq_count, width)
-
-    section_outputs = placed(outs)
-    section_grads = placed(grads)
-
+        return back, total
+
+    def front_part(s, back, grad):
+        gain = gains_all[s // 2, s % 2][None]
+        grads[s] = input_grad(ids, states[s], back, grad, gain, weights[s])
+        grad_far[s] = across(grads[s], [(0, 2), (1, 3)] if s >= 2 else [(2, 0), (3, 1)])
+        return grads[s]
+
+    back, bias_sum = back_part(3, grad)
+    grad = front_part(3, back, after(grad, out_far[2]))
+    back, bias_sum = back_part(2, wait(grad, (3, "core")))
+    grad = front_part(2, back, after(wait(grad, (3, "y")), out_far[3]))
+    out_relay = relay(ids, outs, out_far[:3] + [after(out_far[3], grad)])
+    back, bias_sum = back_part(1, wait(grad, (2, "core"), (3, "far")))
     if eight:
+        steps[3]["near"] = reduce_near(steps[3])
+    grad = front_part(1, back, after(wait(grad, (2, "y"), (3, "near")), grad_far[3]))
+    back, bias_sum = back_part(0, after(wait(grad, (1, "core")), grad_far[2], out_relay))
+    if eight:
+        steps[2]["far"] = after(steps[2]["far"], steps[0]["keep"])
+        for s in (2, 1, 0):
+            steps[s]["near"] = reduce_near(steps[s])
+    grad = front_part(0, back, wait(grad, (2, "far")))
+
+    shape = (1, micro_count, row_count, seq_count, width)
+    section_outputs = place(ids, outs, out_relay, out_far, []).reshape(shape)
+    grad_relay = relay(ids, grads, grad_far)
+    section_grads = place(ids, grads, grad_relay, grad_far, []).reshape(shape)
+
+    if eight:
+        own = []
+        for pair in ((3, 2), (1, 0)):
+            both = jnp.concatenate([reduce_last(steps[s]) for s in pair], axis=1)
+            own.append(added(both, swapped(both, "section", 2)))
+        own = jnp.concatenate(own, axis=1)
         shapes = [w.shape for w in shards] + [gains.shape, position_table.shape]
-        final = unpack_grads(ids, reduced, shapes)
+        final = unpack_grads(ids, own, swapped(own, "section", 1), shards, gains.astype(f32), shapes)
         return (section_outputs, section_grads) + tuple(final)
 
     dense = [from_packed(packed[2 * layer], packed[2 * layer + 1]) for layer in range(layers)]
@@ -654,13 +760,12 @@
         both = jnp.stack([d[at] for d in dense])
         part = lax.psum_scatter(both, "dp", scatter_dimension=1, tiled=True)
         final.append(lax.psum(part, "section").astype(f32))
+    terms = [w.astype(f32) * final[at] for at, w in enumerate(shards)]
+    gain_sums = [sum(jnp.sum(terms[at], axis=2) for at in group) for group in ((0, 1, 2), (4, 5))]
+    gains_grad = jnp.stack(gain_sums, axis=1) / gains.astype(f32)
     bias_sum = bias_sum.reshape(seq_count, heads, seq_count)
     table = jnp.einsum("jib,jhi->bh", onehot, bias_sum, precision=lax.Precision.HIGHEST)
-    gain_sum = jnp.concatenate(gain_terms).reshape(layers, 2, width)
-    table, gain_sum = lax.psum((table, gain_sum), ("section", "dp"))
-    shard = gains.shape[2]
-    gain_sum = lax.dynamic_slice_in_dim(gain_sum, dp * shard, shard, 2)
-    return (section_outputs, section_grads) + tuple(final) + (gain_sum, table)
+    return (section_outputs, section_grads) + tuple(final) + (gains_grad, lax.psum(table, ("section", "dp")))
 
 
 def solution(mesh):

time: 646 us -> 317 us (0.49)
  Pallas kernels: 353 us -> 133 us
  starting transfers between devices: 133 us -> 60.6 us
  waiting for transfers between devices: 107 us -> 76.7 us
    pallas_call x4 -> x10, Pallas kernels: 265 us -> 50.4 us  [the longest x4 29 us: input_grad(): call(input_grad_kernel, t // block, [tok(block, d), tok(block, width), to...]
    ppermute x24 -> x4, starting transfers between devices: 77.1 us -> 9.07 us  [across(): return lax.ppermute(value, 'section', pairs)]
    ppermute x27 -> x12, waiting for transfers between devices: 39.6 us -> 15.9 us  [z_shift(): return lax.ppermute(values, 'dp', pairs)]
    ppermute x24 -> x4, waiting for transfers between devices: 18.8 us -> 0.01 us  [across(): return lax.ppermute(value, 'section', pairs)]
    ppermute x27 -> x12, starting transfers between devices: 42.6 us -> 24.3 us  [z_shift(): return lax.ppermute(values, 'dp', pairs)]
    ppermute x33 -> x35, starting transfers between devices: 13.1 us -> 27.3 us  [swapped(): lax.ppermute(values, axis, [(i, i ^ bit) for i in range(lax.axis_size(axi...]
    ppermute x33 -> x35, waiting for transfers between devices: 48.6 us -> 60.8 us  [swapped(): lax.ppermute(values, axis, [(i, i ^ bit) for i in range(lax.axis_size(axi...]
    select_n x6 -> x3, other arithmetic: 11.6 us -> 1.46 us  [the longest x2 1.45 us: body(): jnp.where(chip == 0, out, states[s - 1])]
  transfers between devices with their start and end apart: 84 -> 51, of which waited for: 16 -> 16; matrix products, arithmetic and copies ran while one was open for 6% -> 10% of each run, Pallas kernels for 54% -> 40%
where the time goes in v3:
time: 317 us; the launch traced here: 313 us
  Pallas kernels  133 us (42%)
  waiting for transfers between devices  76.7 us (24%)
  starting transfers between devices  60.6 us (19%)
  other arithmetic  25.7 us (8%)
  local copies, waits for them, and re-layouts  15.6 us (5%)
    ppermute x35, waiting for transfers between devices, swapped(): lax.ppermute(values, axis, [(i, i ^ bit) for i in range(lax.axis_size(axi...  60.8 us
    pallas_call x4, Pallas kernels, input_grad(): call(input_grad_kernel, t // block, [tok(block, d), tok(block, width), to...  29 us
    pallas_call x2, Pallas kernels, ffn_bwd(): call(ffn_bwd_kernel, t // block, [tok(block, d), tok(block, 1024), tok(bl...  28.9 us
    ppermute x35, starting transfers between devices, swapped(): lax.ppermute(values, axis, [(i, i ^ bit) for i in range(lax.axis_size(axi...  27.3 us
    ppermute x12, starting transfers between devices, z_shift(): return lax.ppermute(values, 'dp', pairs)  24.3 us
    pallas_call x2, Pallas kernels, attn_bwd(): call(attn_bwd_kernel, t // block, [tok(block, d)] + [tok(block, 384)] * 5...  22.3 us
    convert_element_type x18, other arithmetic, added(): return total.astype(bf)  19.5 us
    ppermute x12, waiting for transfers between devices, z_shift(): return lax.ppermute(values, 'dp', pairs)  15.9 us
  transfers between devices with their start and end apart: 51, of which 16 were waited for; matrix products, arithmetic and copies ran while one was open for 10% of the time, Pallas kernels for 40%

profile of v3, /device:TPU:0, one launch (start us, length us, event | category | flops | bytes accessed | tf_op | source)
XLA Modules:
  0.0 313.2 jit_solution(16858475755848659472)
XLA Ops:
  2.6 2.8 pack_weights.1
  5.4 3.1 collective-permute-start
  8.4 2.6 collective-permute-start.1
  12.4 2.3 constant_dynamic-slice_fusion.1
  18.3 2.8 collective-permute-start.3
  25.2 2.8 collective-permute-done.3
  28.1 7.4 %collective-permute-done.4 = bf16[32,3072]{1,0:T(8,128)(2,1)S(1)} collective-permute-done((bf16[32,3072]{1,0:T(8,128)(2,1)S(1)}, bf16[32,3072]{1,0:T(8,128)(2,1)S(1)}, u32[]{:S(2)}, u32[]{:S(2)}) %collective-permute-start.4) | collective-permute-done | bytes 196640 | tf_op jit(solution)/shard_map/ppermute | solution.py:555
  35.4 3.7 %collective-permute-start.10 = (bf16[32,1536]{1,0:T(8,128)(2,1)S(1)}, bf16[32,1536]{1,0:T(8,128)(2,1)S(1)}, u32[]{:S(2)}, u32[]{:S(2)}) collective-permute-start(bf16[32,1536]{1,0:T(8,128)(2,1)S(1)} %copy-done.27), channel_id=1, source_target_pairs={{0,4},{1,5},{2,6},{3,7},{4,0},{5,1},{6,2},{7,3},{8,12},{9,13},{10,... | collective-permute-start | bytes 294920 | tf_op jit(solution)/shard_map/ppermute | solution.py:555
  39.1 3.4 %collective-permute-start.11 = (bf16[32,1536]{1,0:T(8,128)(2,1)S(1)}, bf16[32,1536]{1,0:T(8,128)(2,1)S(1)}, u32[]{:S(2)}, u32[]{:S(2)}) collective-permute-start(bf16[32,1536]{1,0:T(8,128)(2,1)S(1)} %copy-done.27), channel_id=1, source_target_pairs={{0,6},{1,7},{2,0},{3,1},{4,2},{5,3},{6,4},{7,5},{8,14},{9,15},{10,... | collective-permute-start | bytes 294920 | tf_op jit(solution)/shard_map/ppermute | solution.py:555
  45.6 3.8 %collective-permute-done.9 = bf16[32,1536]{1,0:T(8,128)(2,1)S(1)} collective-permute-done((bf16[32,1536]{1,0:T(8,128)(2,1)S(1)}, bf16[32,1536]{1,0:T(8,128)(2,1)S(1)}, u32[]{:S(2)}, u32[]{:S(2)}) %collective-permute-start.9) | collective-permute-done | bytes 98336 | tf_op jit(solution)/shard_map/ppermute | solution.py:555
  49.4 2.7 collective-permute-start.16
  53.2 2.4 collective-permute-start.17
  56.4 7.9 %attn_fwd.2 = (bf16[1024,512]{1,0:T(8,128)(2,1)}, bf16[1024,384]{1,0:T(8,128)(2,1)}, bf16[1024,384]{1,0:T(8,128)(2,1)}, bf16[1024,384]{1,0:T(8,128)(2,1)}, bf16[...) custom-call(s32[4]{0:T(128)} %pad_add_fusion.ids, bf16[1024,512]{1,0:T(8,128)(2,1)} %bitcast.177, ...), custom_call_target="tpu_custom_call" | custom-call | flops 4400000000 | tf_op jit(solution)/shard_map/attn_fwd/pallas_call | solution.py:344
  68.9 7.6 %ffn_fwd.2 = (bf16[1024,512]{1,0:T(8,128)(2,1)}, bf16[1024,1024]{1,0:T(8,128)(2,1)}, bf16[1024,1024]{1,0:T(8,128)(2,1)}) custom-call(s32[4]{0:T(128)} %pad_add_fusion.ids, bf16[1024,512]{1,0:T(8,128)(2,1)} %get-tuple-element.86.x_ref.refs_0_, f32[1,512]{1,0:T(1,128)} %get-tuple-element.189.gain_ref, bf16[4,32,3072]{2,1,0:T(8,128)(2,1)} %copy-done.16, ...), custom_call_target="tpu_custom_call" | custom-call | flops 4400000000 | tf_op jit(solution)/shard_map/ffn_fwd/pallas_call | solution.py:385
  79.7 7.9 %attn_fwd.3 = (bf16[1024,512]{1,0:T(8,128)(2,1)}, bf16[1024,384]{1,0:T(8,128)(2,1)}, bf16[1024,384]{1,0:T(8,128)(2,1)}, bf16[1024,384]{1,0:T(8,128)(2,1)}, bf16[...) custom-call(s32[4]{0:T(128)} %pad_add_fusion.ids, bf16[1024,512]{1,0:T(8,128)(2,1)} %get-tuple-element.92.x_ref.refs_1_, ...), custom_call_target="tpu_custom_call" | custom-call | flops 4400000000 | tf_op jit(solution)/shard_map/attn_fwd/pallas_call | solution.py:344
  87.6 9.4 %collective-permute-done.21.w1 = bf16[4,32,3072]{2,1,0:T(8,128)(2,1)} collective-permute-done((bf16[4,32,3072]{2,1,0:T(8,128)(2,1)S(1)}, bf16[4,32,3072]{2,1,0:T(8,128)(2,1)}, u32[]{:S(2)}, u32[]{:S(2)}) %collective-permute-start.21) | collective-permute-done | bytes 786464 | tf_op jit(solution)/shard_map/ppermute | solution.py:559
  99.2 2.4 constant_dynamic-slice_fusion
  101.6 7.6 %ffn_fwd.3 = (bf16[1024,512]{1,0:T(8,128)(2,1)}, bf16[1024,1024]{1,0:T(8,128)(2,1)}, bf16[1024,1024]{1,0:T(8,128)(2,1)}) custom-call(s32[4]{0:T(128)} %pad_add_fusion.ids, bf16[1024,512]{1,0:T(8,128)(2,1)} %get-tuple-element.95.x_ref.refs_2_, f32[1,512]{1,0:T(1,128)} %get-tuple-element.187.gain_ref, bf16[4,32,3072]{2,1,0:T(8,128)(2,1)} %copy-done.17, ...), custom_call_target="tpu_custom_call" | custom-call | flops 4400000000 | tf_op jit(solution)/shard_map/ffn_fwd/pallas_call | solution.py:385
  109.2 14.5 %ffn_bwd.2 = (bf16[1024,2048]{1,0:T(8,128)(2,1)}, bf16[2,4,32,3072]{3,2,1,0:T(8,128)(2,1)}, bf16[2,4,32,3072]{3,2,1,0:T(8,128)(2,1)}) custom-call(s32[4]{0:T(128)} %pad_add_fusion.ids, bf16[1024,512]{1,0:T(8,128)(2,1)} %get-tuple-element.95.x_ref.refs_2_, bf16[1024,1024]{1,0:T(8,128)(2,1)} %get-tuple-element.104.gate_ref, ...), custom_call_target="tpu_custom_call" | custom-call | flops 6600000000 | tf_op jit(solution)/shard_map/ffn_bwd/pallas_call | solution.py:398
  124.0 8.2 %input_grad.4.g_ref.refs_3_ = bf16[1024,512]{1,0:T(8,128)(2,1)} custom-call(s32[4]{0:T(128)} %pad_add_fusion.ids, bf16[1024,512]{1,0:T(8,128)(2,1)} %get-tuple-element.95.x_ref.refs_2_, bf16[1024,2048]{1,0:T(8,128)(2,1)} %get-tuple-element.106.back_ref, bf16[1024,512]{1,0:T(8,128)(2,1)} %bitcast.181, f32[1,512]{1,0:T(1,128)} %get-tuple-element.187.gain_ref, ...), custom_call_target="tpu_custom_call" | custom-call | flops 22000001024 | tf_op jit(solution)/shard_map/input_grad/pallas_call | solution.py:375
  132.3 2.2 fusion
  136.6 10.9 %attn_bwd.2 = (bf16[1024,1152]{1,0:T(8,128)(2,1)}, bf16[2,4,32,1536]{3,2,1,0:T(8,128)(2,1)}, bf16[2,4,32,1536]{3,2,1,0:T(8,128)(2,1)}, f32[64,384]{1,0:T(8,128)}) custom-call(s32[4]{0:T(128)} %pad_add_fusion.ids, bf16[1024,512]{1,0:T(8,128)(2,1)} %get-tuple-element.92.x_ref.refs_1_, bf16[1024,384]{1,0:T(8,128)(2,1)} %get-tuple-element.99.q_ref, ...), custom_call_target="tpu_custom_call" | custom-call | flops 6600000000 | tf_op jit(solution)/shard_map/attn_bwd/pallas_call | solution.py:359
  147.8 1.8 collective-permute-start.25
  149.6 2.3 collective-permute-start.33
  151.8 2.7 collective-permute-done.27
  154.5 2.1 fusion.3
  156.7 1.8 collective-permute-start.30
  160.9 12.4 %collective-permute-done.25.refs_5_.refs_7_.refs_6_.refs_8_ = bf16[1024,512]{1,0:T(8,128)(2,1)S(1)} collective-permute-done((bf16[1024,512]{1,0:T(8,128)(2,1)S(1)}, bf16[1024,512]{1,0:T(8,128)(2,1)S(1)}, u32[]{:S(2)}, u32[]{:S(2)}) %collective-permute-start.25) | collective-permute-done | bytes 1048608 | tf_op jit(solution)/shard_map/ppermute | solution.py:559
  173.4 6.4 %input_grad.5.g_ref.refs_2_ = bf16[1024,512]{1,0:T(8,128)(2,1)} custom-call(s32[4]{0:T(128)} %pad_add_fusion.ids, bf16[1024,512]{1,0:T(8,128)(2,1)} %get-tuple-element.92.x_ref.refs_1_, bf16[1024,1152]{1,0:T(8,128)(2,1)} %get-tuple-element.110.back_ref, bf16[1024,512]{1,0:T(8,128)(2,1)} %input_grad.4.g_ref.refs_3_, f32[1,512]{1,0:T(1,128)} %get-tuple-element.188.gain_ref, ...), custom_call_target="tpu_custom_call" | custom-call | flops 22000001024 | tf_op jit(solution)/shard_map/input_grad/pallas_call | solution.py:375
  179.8 4.1 %collective-permute-start.35 = (bf16[1024,512]{1,0:T(8,128)(2,1)}, bf16[1024,512]{1,0:T(8,128)(2,1)S(1)}, u32[]{:S(2)}, u32[]{:S(2)}) collective-permute-start(bf16[1024,512]{1,0:T(8,128)(2,1)} %input_grad.5.g_ref.refs_2_), channel_id=1, source_target_pairs={{0,16},{8,24},{1,17},{9,25},{2,18},{10,26},{3,19},{11,27},{4,20},{... | collective-permute-start | bytes 3145736 | tf_op jit(solution)/shard_map/ppermute | solution.py:671
  183.9 3.2 %relay.2 = bf16[2,1024,512]{2,1,0:T(8,128)(2,1)} custom-call(s32[4]{0:T(128)} %pad_add_fusion.ids, bf16[1024,512]{1,0:T(8,128)(2,1)} %get-tuple-element.86.x_ref.refs_0_, bf16[1024,512]{1,0:T(8,128)(2,1)} %get-tuple-element.92.x_ref.refs_1_, bf16[1024,512]{1,0:T(8,128)(2,1)} %get-tuple-element.95.x_ref.refs_2_, bf16[1024,512]{1,0:T(8,128)(2,1)} %get-tuple-element.98.refs_3_, ...), custom_call_target="tpu_custom_call" | custom-call | flops 2200000000 | tf_op jit(solution)/shard_map/relay/pallas_call | solution.py:523
  188.6 2.9 collective-permute-start.32
  193.2 3.3 %collective-permute-start.36 = (bf16[2,32,1536]{2,1,0:T(8,128)(2,1)}, bf16[2,32,1536]{2,1,0:T(8,128)(2,1)}, u32[]{:S(2)}, u32[]{:S(2)}) collective-permute-start(bf16[2,32,1536]{2,1,0:T(8,128)(2,1)} %fusion.14), channel_id=1, source_target_pairs={{0,4},{1,5},{2,6},{3,7},{4,0},{5,1},{6,2},{7,3},{8,12},{9,13},{10,... | collective-permute-start | bytes 589832 | tf_op jit(solution)/shard_map/ppermute | solution.py:559
  196.5 14.4 %ffn_bwd.3 = (bf16[1024,2048]{1,0:T(8,128)(2,1)}, bf16[2,4,32,3072]{3,2,1,0:T(8,128)(2,1)}, bf16[2,4,32,3072]{3,2,1,0:T(8,128)(2,1)}) custom-call(s32[4]{0:T(128)} %pad_add_fusion.ids, bf16[1024,512]{1,0:T(8,128)(2,1)} %get-tuple-element.86.x_ref.refs_0_, bf16[1024,1024]{1,0:T(8,128)(2,1)} %get-tuple-element.120.gate_ref, ...), custom_call_target="tpu_custom_call" | custom-call | flops 6600000000 | tf_op jit(solution)/shard_map/ffn_bwd/pallas_call | solution.py:398
  211.5 8.0 %input_grad.6.g_ref.refs_1_ = bf16[1024,512]{1,0:T(8,128)(2,1)} custom-call(s32[4]{0:T(128)} %pad_add_fusion.ids, bf16[1024,512]{1,0:T(8,128)(2,1)} %get-tuple-element.86.x_ref.refs_0_, bf16[1024,2048]{1,0:T(8,128)(2,1)} %get-tuple-element.124.back_ref, bf16[1024,512]{1,0:T(8,128)(2,1)} %input_grad.5.g_ref.refs_2_, f32[1,512]{1,0:T(1,128)} %get-tuple-element.189.gain_ref, ...), custom_call_target="tpu_custom_call" | custom-call | flops 22000001024 | tf_op jit(solution)/shard_map/input_grad/pallas_call | solution.py:375
  222.3 2.5 fusion.1
  225.3 11.4 %attn_bwd.3 = (bf16[1024,1152]{1,0:T(8,128)(2,1)}, bf16[2,4,32,1664]{3,2,1,0:T(8,128)(2,1)}, bf16[2,4,32,1664]{3,2,1,0:T(8,128)(2,1)}, f32[64,384]{1,0:T(8,128)}) custom-call(s32[4]{0:T(128)} %pad_add_fusion.ids, bf16[1024,512]{1,0:T(8,128)(2,1)} %bitcast.178, bf16[1024,384]{1,0:T(8,128)(2,1)} %get-tuple-element.115.q_ref, ...), custom_call_target="tpu_custom_call" | custom-call | flops 6600000000 | tf_op jit(solution)/shard_map/attn_bwd/pallas_call | solution.py:359
  238.0 6.4 %input_grad.7.refs_0_ = bf16[1024,512]{1,0:T(8,128)(2,1)} custom-call(s32[4]{0:T(128)} %pad_add_fusion.ids, bf16[1024,512]{1,0:T(8,128)(2,1)} %bitcast.179, bf16[1024,1152]{1,0:T(8,128)(2,1)} %get-tuple-element.132.back_ref, bf16[1024,512]{1,0:T(8,128)(2,1)} %input_grad.6.g_ref.refs_1_, f32[1,512]{1,0:T(1,128)} %get-tuple-element.190.gain_ref, ...), custom_call_target="tpu_custom_call" | custom-call | flops 22000001024 | tf_op jit(solution)/shard_map/input_grad/pallas_call | solution.py:375
  246.9 2.8 collective-permute-start.41
  252.8 9.1 %collective-permute-done.46 = bf16[4,32,1664]{2,1,0:T(8,128)(2,1)S(1)} collective-permute-done((bf16[4,32,1664]{2,1,0:T(8,128)(2,1)S(1)}, bf16[4,32,1664]{2,1,0:T(8,128)(2,1)S(1)}, u32[]{:S(2)}, u32[]{:S(2)}) %collective-permute-start.46) | collective-permute-done | bytes 426016 | tf_op jit(solution)/shard_map/ppermute | solution.py:559
  262.0 16.6 %collective-permute-done.43 = bf16[2,32,3072]{2,1,0:T(8,128)(2,1)S(1)} collective-permute-done((bf16[2,32,3072]{2,1,0:T(8,128)(2,1)S(1)}, bf16[2,32,3072]{2,1,0:T(8,128)(2,1)S(1)}, u32[]{:S(2)}, u32[]{:S(2)}) %collective-permute-start.43) | collective-permute-done | bytes 393248 | tf_op jit(solution)/shard_map/ppermute | solution.py:559
  279.9 2.4 collective-permute-done.47
  282.4 5.1 %collective-permute-done.44 = bf16[32,3072]{1,0:T(8,128)(2,1)S(1)} collective-permute-done((bf16[32,3072]{1,0:T(8,128)(2,1)S(1)}, bf16[32,3072]{1,0:T(8,128)(2,1)S(1)}, u32[]{:S(2)}, u32[]{:S(2)}) %collective-permute-start.44) | collective-permute-done | bytes 196640 | tf_op jit(solution)/shard_map/ppermute | solution.py:559
  292.1 3.2 %relay.3 = bf16[2,1024,512]{2,1,0:T(8,128)(2,1)} custom-call(s32[4]{0:T(128)} %pad_add_fusion.ids, bf16[1024,512]{1,0:T(8,128)(2,1)} %input_grad.7.refs_0_, bf16[1024,512]{1,0:T(8,128)(2,1)} %input_grad.6.g_ref.refs_1_, bf16[1024,512]{1,0:T(8,128)(2,1)} %input_grad.5.g_ref.refs_2_, bf16[1024,512]{1,0:T(8,128)(2,1)} %input_grad.4.g_ref.refs_3_, ...), custom_call_target="tpu_custom_call" | custom-call | flops 2200000000 | tf_op jit(solution)/shard_map/relay/pallas_call | solution.py:523
  295.5 2.2 collective-permute-done.49
  297.9 4.0 %place.2 = bf16[4,1024,512]{2,1,0:T(8,128)(2,1)} custom-call(s32[4]{0:T(128)} %pad_add_fusion.ids, bf16[1024,512]{1,0:T(8,128)(2,1)} %get-tuple-element.86.x_ref.refs_0_, bf16[1024,512]{1,0:T(8,128)(2,1)} %get-tuple-element.92.x_ref.refs_1_, bf16[1024,512]{1,0:T(8,128)(2,1)} %get-tuple-element.95.x_ref.refs_2_, bf16[1024,512]{1,0:T(8,128)(2,1)} %get-tuple-element.98.refs_3_, ...), custom_call_target="tpu_custom_call" | custom-call | flops 3300000000 | tf_op jit(solution)/shard_map/place/pallas_call | solution.py:523
  301.9 4.1 %unpack_grads.1 = (f32[2,64,384]{2,1,0:T(8,128)}, f32[2,64,384]{2,1,0:T(8,128)}, f32[2,64,384]{2,1,0:T(8,128)}, f32[2,48,512]{2,1,0:T(8,128)}, f32[2,64,1024]{2,...) custom-call(s32[4]{0:T(128)} %pad_add_fusion.ids, ...), custom_call_target="tpu_custom_call" | custom-call | flops 3300000000 | tf_op jit(solution)/shard_map/unpack_grads/pallas_call | solution.py:486
  308.8 4.1 %place.3 = bf16[4,1024,512]{2,1,0:T(8,128)(2,1)} custom-call(s32[4]{0:T(128)} %pad_add_fusion.ids, bf16[1024,512]{1,0:T(8,128)(2,1)} %input_grad.7.refs_0_, bf16[1024,512]{1,0:T(8,128)(2,1)} %input_grad.6.g_ref.refs_1_, bf16[1024,512]{1,0:T(8,128)(2,1)} %input_grad.5.g_ref.refs_2_, bf16[1024,512]{1,0:T(8,128)(2,1)} %input_grad.4.g_ref.refs_3_, ...), custom_call_target="tpu_custom_call" | custom-call | flops 3300000000 | tf_op jit(solution)/shard_map/place/pallas_call | solution.py:523
  (196 shorter events, 53.8 us)
Async XLA Ops:
  5.4 12.5 %collective-permute-start = (bf16[32,1664]{1,0:T(8,128)(2,1)}, bf16[32,1664]{1,0:T(8,128)(2,1)S(1)}, u32[]{:S(2)}, u32[]{:S(2)}) collective-permute-start(bf16[32,1664]{1,0:T(8,128)(2,1)} %get-tuple-element.80), channel_id=1, source_target_pairs={{0,2},{1,3},{2,4},{3,5},{4,6},{5,7},{6,0},{7,1},{8,10},{9,11},{10,... | collective-permute-start | bytes 319496 | tf_op jit(solution)/shard_map/ppermute | solution.py:555
  8.4 9.9 %collective-permute-start.1 = (bf16[32,1664]{1,0:T(8,128)(2,1)}, bf16[32,1664]{1,0:T(8,128)(2,1)S(1)}, u32[]{:S(2)}, u32[]{:S(2)}) collective-permute-start(bf16[32,1664]{1,0:T(8,128)(2,1)} %get-tuple-element.80), channel_id=1, source_target_pairs={{0,4},{1,5},{2,6},{3,7},{4,0},{5,1},{6,2},{7,3},{8,12},{9,13},{10,... | collective-permute-start | bytes 319496 | tf_op jit(solution)/shard_map/ppermute | solution.py:555
  11.0 7.3 %collective-permute-start.2 = (bf16[32,1664]{1,0:T(8,128)(2,1)}, bf16[32,1664]{1,0:T(8,128)(2,1)S(1)}, u32[]{:S(2)}, u32[]{:S(2)}) collective-permute-start(bf16[32,1664]{1,0:T(8,128)(2,1)} %get-tuple-element.80), channel_id=1, source_target_pairs={{0,6},{1,7},{2,0},{3,1},{4,2},{5,3},{6,4},{7,5},{8,14},{9,15},{10,... | collective-permute-start | bytes 319496 | tf_op jit(solution)/shard_map/ppermute | solution.py:555
  18.3 9.7 %collective-permute-start.3 = (bf16[32,3072]{1,0:T(8,128)(2,1)S(1)}, bf16[32,3072]{1,0:T(8,128)(2,1)S(1)}, u32[]{:S(2)}, u32[]{:S(2)}) collective-permute-start(bf16[32,3072]{1,0:T(8,128)(2,1)S(1)} %copy-done.24), channel_id=1, source_target_pairs={{0,2},{1,3},{2,4},{3,5},{4,6},{5,7},{6,0},{7,1},{8,10},{9,11},{10,... | collective-permute-start | bytes 589832 | tf_op jit(solution)/shard_map/ppermute | solution.py:555
  21.1 14.3 %collective-permute-start.4 = (bf16[32,3072]{1,0:T(8,128)(2,1)S(1)}, bf16[32,3072]{1,0:T(8,128)(2,1)S(1)}, u32[]{:S(2)}, u32[]{:S(2)}) collective-permute-start(bf16[32,3072]{1,0:T(8,128)(2,1)S(1)} %copy-done.24), channel_id=1, source_target_pairs={{0,4},{1,5},{2,6},{3,7},{4,0},{5,1},{6,2},{7,3},{8,12},{9,13},{10,... | collective-permute-start | bytes 589832 | tf_op jit(solution)/shard_map/ppermute | solution.py:555
  22.7 12.8 %collective-permute-start.5 = (bf16[32,3072]{1,0:T(8,128)(2,1)S(1)}, bf16[32,3072]{1,0:T(8,128)(2,1)S(1)}, u32[]{:S(2)}, u32[]{:S(2)}) collective-permute-start(bf16[32,3072]{1,0:T(8,128)(2,1)S(1)} %copy-done.24), channel_id=1, source_target_pairs={{0,6},{1,7},{2,0},{3,1},{4,2},{5,3},{6,4},{7,5},{8,14},{9,15},{10,... | collective-permute-start | bytes 589832 | tf_op jit(solution)/shard_map/ppermute | solution.py:555
  23.6 28.6 %collective-permute-start.6 = (bf16[4,32,1664]{2,1,0:T(8,128)(2,1)S(1)}, bf16[4,32,1664]{2,1,0:T(8,128)(2,1)S(1)}, u32[]{:S(2)}, u32[]{:S(2)}) collective-permute-start(bf16[4,32,1664]{2,1,0:T(8,128)(2,1)S(1)} %pad_maximum_fusion.4.w0), channel_id=1, source_target_pairs={{0,1},{1,0},{2,3},{3,2},{4,5},{5,4},{6,7},{7,6},{8,9},{9,8},{10,11... | collective-permute-start | bytes 1277960 | tf_op jit(solution)/shard_map/ppermute | solution.py:559
  25.2 28.0 %collective-permute-start.7 = (bf16[4,32,1664]{2,1,0:T(8,128)(2,1)S(1)}, bf16[4,32,1664]{2,1,0:T(8,128)(2,1)}, u32[]{:S(2)}, u32[]{:S(2)}) collective-permute-start(bf16[4,32,1664]{2,1,0:T(8,128)(2,1)S(1)} %pad_maximum_fusion.4.w0), channel_id=1, source_target_pairs={{0,8},{8,0},{16,24},{24,16},{1,9},{9,1},{17,25},{25,17},{2,10},{10... | collective-permute-start | bytes 1277960 | tf_op jit(solution)/shard_map/ppermute | solution.py:559
  35.4 7.3 %collective-permute-start.10 = (bf16[32,1536]{1,0:T(8,128)(2,1)S(1)}, bf16[32,1536]{1,0:T(8,128)(2,1)S(1)}, u32[]{:S(2)}, u32[]{:S(2)}) collective-permute-start(bf16[32,1536]{1,0:T(8,128)(2,1)S(1)} %copy-done.27), channel_id=1, source_target_pairs={{0,4},{1,5},{2,6},{3,7},{4,0},{5,1},{6,2},{7,3},{8,12},{9,13},{10,... | collective-permute-start | bytes 294920 | tf_op jit(solution)/shard_map/ppermute | solution.py:555
  39.1 6.5 %collective-permute-start.11 = (bf16[32,1536]{1,0:T(8,128)(2,1)S(1)}, bf16[32,1536]{1,0:T(8,128)(2,1)S(1)}, u32[]{:S(2)}, u32[]{:S(2)}) collective-permute-start(bf16[32,1536]{1,0:T(8,128)(2,1)S(1)} %copy-done.27), channel_id=1, source_target_pairs={{0,6},{1,7},{2,0},{3,1},{4,2},{5,3},{6,4},{7,5},{8,14},{9,15},{10,... | collective-permute-start | bytes 294920 | tf_op jit(solution)/shard_map/ppermute | solution.py:555
  42.5 6.9 %collective-permute-start.9 = (bf16[32,1536]{1,0:T(8,128)(2,1)S(1)}, bf16[32,1536]{1,0:T(8,128)(2,1)S(1)}, u32[]{:S(2)}, u32[]{:S(2)}) collective-permute-start(bf16[32,1536]{1,0:T(8,128)(2,1)S(1)} %copy-done.27), channel_id=1, source_target_pairs={{0,2},{1,3},{2,4},{3,5},{4,6},{5,7},{6,0},{7,1},{8,10},{9,11},{10,... | collective-permute-start | bytes 294920 | tf_op jit(solution)/shard_map/ppermute | solution.py:555
  42.7 21.5 %collective-permute-start.12 = (bf16[4,32,3072]{2,1,0:T(8,128)(2,1)S(1)}, bf16[4,32,3072]{2,1,0:T(8,128)(2,1)}, u32[]{:S(2)}, u32[]{:S(2)}) collective-permute-start(bf16[4,32,3072]{2,1,0:T(8,128)(2,1)S(1)} %pad_maximum_fusion.w0), channel_id=1, source_target_pairs={{0,1},{1,0},{2,3},{3,2},{4,5},{5,4},{6,7},{7,6},{8,9},{9,8},{10,11... | collective-permute-start | bytes 2359304 | tf_op jit(solution)/shard_map/ppermute | solution.py:559
  49.4 15.5 %collective-permute-start.15 = (bf16[32,3072]{1,0:T(8,128)(2,1)S(1)}, bf16[32,3072]{1,0:T(8,128)(2,1)S(1)}, u32[]{:S(2)}, u32[]{:S(2)}) collective-permute-start(bf16[32,3072]{1,0:T(8,128)(2,1)S(1)} %copy-done.23), channel_id=1, source_target_pairs={{0,2},{1,3},{2,4},{3,5},{4,6},{5,7},{6,0},{7,1},{8,10},{9,11},{10,... | collective-permute-start | bytes 589832 | tf_op jit(solution)/shard_map/ppermute | solution.py:555
  49.4 17.1 %collective-permute-start.16 = (bf16[32,3072]{1,0:T(8,128)(2,1)S(1)}, bf16[32,3072]{1,0:T(8,128)(2,1)S(1)}, u32[]{:S(2)}, u32[]{:S(2)}) collective-permute-start(bf16[32,3072]{1,0:T(8,128)(2,1)S(1)} %copy-done.23), channel_id=1, source_target_pairs={{0,4},{1,5},{2,6},{3,7},{4,0},{5,1},{6,2},{7,3},{8,12},{9,13},{10,... | collective-permute-start | bytes 589832 | tf_op jit(solution)/shard_map/ppermute | solution.py:555
  52.2 3.4 %collective-permute-start.8 = (bf16[4,32,1664]{2,1,0:T(8,128)(2,1)S(1)}, bf16[4,32,1664]{2,1,0:T(8,128)(2,1)S(1)}, u32[]{:S(2)}, u32[]{:S(2)}) collective-permute-start(bf16[4,32,1664]{2,1,0:T(8,128)(2,1)S(1)} %collective-permute-done.6.w1), channel_id=1, source_target_pairs={{0,8},{8,0},{16,24},{24,16},{1,9},{9,1},{17,25},{25,17},{2,10},{10... | collective-permute-start | bytes 1277960 | tf_op jit(solution)/shard_map/ppermute | solution.py:559
  53.2 13.3 %collective-permute-start.17 = (bf16[32,3072]{1,0:T(8,128)(2,1)S(1)}, bf16[32,3072]{1,0:T(8,128)(2,1)S(1)}, u32[]{:S(2)}, u32[]{:S(2)}) collective-permute-start(bf16[32,3072]{1,0:T(8,128)(2,1)S(1)} %copy-done.23), channel_id=1, source_target_pairs={{0,6},{1,7},{2,0},{3,1},{4,2},{5,3},{6,4},{7,5},{8,14},{9,15},{10,... | collective-permute-start | bytes 589832 | tf_op jit(solution)/shard_map/ppermute | solution.py:555
  64.5 3.4 %collective-permute-start.14 = (bf16[4,32,3072]{2,1,0:T(8,128)(2,1)}, bf16[4,32,3072]{2,1,0:T(8,128)(2,1)S(1)}, u32[]{:S(2)}, u32[]{:S(2)}) collective-permute-start(bf16[4,32,3072]{2,1,0:T(8,128)(2,1)} %collective-permute-done.12.w1), channel_id=1, source_target_pairs={{0,8},{8,0},{16,24},{24,16},{1,9},{9,1},{17,25},{25,17},{2,10},{10... | collective-permute-start | bytes 2359304 | tf_op jit(solution)/shard_map/ppermute | solution.py:559
  64.9 11.6 %collective-permute-start.18 = (bf16[4,32,1536]{2,1,0:T(8,128)(2,1)S(1)}, bf16[4,32,1536]{2,1,0:T(8,128)(2,1)S(1)}, u32[]{:S(2)}, u32[]{:S(2)}) collective-permute-start(bf16[4,32,1536]{2,1,0:T(8,128)(2,1)S(1)} %pad_maximum_fusion.5.w0), channel_id=1, source_target_pairs={{0,1},{1,0},{2,3},{3,2},{4,5},{5,4},{6,7},{7,6},{8,9},{9,8},{10,11... | collective-permute-start | bytes 1179656 | tf_op jit(solution)/shard_map/ppermute | solution.py:559
  77.2 19.8 %collective-permute-start.21 = (bf16[4,32,3072]{2,1,0:T(8,128)(2,1)S(1)}, bf16[4,32,3072]{2,1,0:T(8,128)(2,1)}, u32[]{:S(2)}, u32[]{:S(2)}) collective-permute-start(bf16[4,32,3072]{2,1,0:T(8,128)(2,1)S(1)} %pad_maximum_fusion.1.w0), channel_id=1, source_target_pairs={{0,1},{1,0},{2,3},{3,2},{4,5},{5,4},{6,7},{7,6},{8,9},{9,8},{10,11... | collective-permute-start | bytes 2359304 | tf_op jit(solution)/shard_map/ppermute | solution.py:559
  97.0 4.5 %collective-permute-start.22 = (bf16[4,32,3072]{2,1,0:T(8,128)(2,1)S(1)}, bf16[4,32,3072]{2,1,0:T(8,128)(2,1)}, u32[]{:S(2)}, u32[]{:S(2)}) collective-permute-start(bf16[4,32,3072]{2,1,0:T(8,128)(2,1)S(1)} %pad_maximum_fusion.1.w0), channel_id=1, source_target_pairs={{0,8},{8,0},{16,24},{24,16},{1,9},{9,1},{17,25},{25,17},{2,10},{10... | collective-permute-start | bytes 2359304 | tf_op jit(solution)/shard_map/ppermute | solution.py:559
  97.0 4.5 %collective-permute-start.23 = (bf16[4,32,3072]{2,1,0:T(8,128)(2,1)}, bf16[4,32,3072]{2,1,0:T(8,128)(2,1)}, u32[]{:S(2)}, u32[]{:S(2)}) collective-permute-start(bf16[4,32,3072]{2,1,0:T(8,128)(2,1)} %collective-permute-done.21.w1), channel_id=1, source_target_pairs={{0,8},{8,0},{16,24},{24,16},{1,9},{9,1},{17,25},{25,17},{2,10},{10... | collective-permute-start | bytes 2359304 | tf_op jit(solution)/shard_map/ppermute | solution.py:559
  98.9 25.1 %collective-permute-start.24 = (bf16[1024,512]{1,0:T(8,128)(2,1)S(1)}, bf16[1024,512]{1,0:T(8,128)(2,1)S(1)}, u32[]{:S(2)}, u32[]{:S(2)}) collective-permute-start(bf16[1024,512]{1,0:T(8,128)(2,1)S(1)} %broadcast_select_fusion.1), channel_id=1, source_target_pairs={{0,16},{8,24},{16,0},{24,8},{1,17},{9,25},{17,1},{25,9},{2,18},{10... | collective-permute-start | bytes 3145736 | tf_op jit(solution)/shard_map/ppermute | solution.py:559
  123.7 8.5 %collective-permute-start.26 = (bf16[2,4,32,3072]{3,2,1,0:T(8,128)(2,1)}, bf16[2,4,32,3072]{3,2,1,0:T(8,128)(2,1)}, u32[]{:S(2)}, u32[]{:S(2)}) collective-permute-start(bf16[2,4,32,3072]{3,2,1,0:T(8,128)(2,1)} %get-tuple-element.108), channel_id=1, source_target_pairs={{0,8},{8,0},{16,24},{24,16},{1,9},{9,1},{17,25},{25,17},{2,10},{10... | collective-permute-start | bytes 4718600 | tf_op jit(solution)/shard_map/ppermute | solution.py:559
  134.5 20.1 %collective-permute-start.27 = (bf16[4,32,3072]{2,1,0:T(8,128)(2,1)}, bf16[4,32,3072]{2,1,0:T(8,128)(2,1)}, u32[]{:S(2)}, u32[]{:S(2)}) collective-permute-start(bf16[4,32,3072]{2,1,0:T(8,128)(2,1)} %fusion), channel_id=1, source_target_pairs={{0,1},{1,0},{2,3},{3,2},{4,5},{5,4},{6,7},{7,6},{8,9},{9,8},{10,11... | collective-permute-start | bytes 2359304 | tf_op jit(solution)/shard_map/ppermute | solution.py:559
  147.5 10.9 %collective-permute-start.29 = (bf16[2,4,32,1536]{3,2,1,0:T(8,128)(2,1)}, bf16[2,4,32,1536]{3,2,1,0:T(8,128)(2,1)S(1)}, u32[]{:S(2)}, u32[]{:S(2)}) collective-permute-start(bf16[2,4,32,1536]{3,2,1,0:T(8,128)(2,1)} %get-tuple-element.122), channel_id=1, source_target_pairs={{0,8},{8,0},{16,24},{24,16},{1,9},{9,1},{17,25},{25,17},{2,10},{10... | collective-permute-start | bytes 2359304 | tf_op jit(solution)/shard_map/ppermute | solution.py:559
  147.8 25.6 %collective-permute-start.25 = (bf16[1024,512]{1,0:T(8,128)(2,1)S(1)}, bf16[1024,512]{1,0:T(8,128)(2,1)S(1)}, u32[]{:S(2)}, u32[]{:S(2)}) collective-permute-start(bf16[1024,512]{1,0:T(8,128)(2,1)S(1)} %broadcast_select_fusion), channel_id=1, source_target_pairs={{0,16},{8,24},{16,0},{24,8},{1,17},{9,25},{17,1},{25,9},{2,18},{10... | collective-permute-start | bytes 3145736 | tf_op jit(solution)/shard_map/ppermute | solution.py:559
  149.6 61.4 %collective-permute-start.33 = (bf16[1024,512]{1,0:T(8,128)(2,1)}, bf16[1024,512]{1,0:T(8,128)(2,1)S(1)}, u32[]{:S(2)}, u32[]{:S(2)}) collective-permute-start(bf16[1024,512]{1,0:T(8,128)(2,1)} %input_grad.4.g_ref.refs_3_), channel_id=1, source_target_pairs={{0,16},{8,24},{1,17},{9,25},{2,18},{10,26},{3,19},{11,27},{4,20},{... | collective-permute-start | bytes 3145736 | tf_op jit(solution)/shard_map/ppermute | solution.py:671
  156.7 30.6 %collective-permute-start.30 = (bf16[2,32,3072]{2,1,0:T(8,128)(2,1)}, bf16[2,32,3072]{2,1,0:T(8,128)(2,1)}, u32[]{:S(2)}, u32[]{:S(2)}) collective-permute-start(bf16[2,32,3072]{2,1,0:T(8,128)(2,1)} %fusion.3), channel_id=1, source_target_pairs={{0,4},{1,5},{2,6},{3,7},{4,0},{5,1},{6,2},{7,3},{8,12},{9,13},{10,... | collective-permute-start | bytes 1179656 | tf_op jit(solution)/shard_map/ppermute | solution.py:559
  159.4 32.0 %collective-permute-start.31 = (bf16[4,32,1536]{2,1,0:T(8,128)(2,1)}, bf16[4,32,1536]{2,1,0:T(8,128)(2,1)}, u32[]{:S(2)}, u32[]{:S(2)}) collective-permute-start(bf16[4,32,1536]{2,1,0:T(8,128)(2,1)} %fusion.7), channel_id=1, source_target_pairs={{0,1},{1,0},{2,3},{3,2},{4,5},{5,4},{6,7},{7,6},{8,9},{9,8},{10,11... | collective-permute-start | bytes 1179656 | tf_op jit(solution)/shard_map/ppermute | solution.py:559
  179.8 45.5 %collective-permute-start.35 = (bf16[1024,512]{1,0:T(8,128)(2,1)}, bf16[1024,512]{1,0:T(8,128)(2,1)S(1)}, u32[]{:S(2)}, u32[]{:S(2)}) collective-permute-start(bf16[1024,512]{1,0:T(8,128)(2,1)} %input_grad.5.g_ref.refs_2_), channel_id=1, source_target_pairs={{0,16},{8,24},{1,17},{9,25},{2,18},{10,26},{3,19},{11,27},{4,20},{... | collective-permute-start | bytes 3145736 | tf_op jit(solution)/shard_map/ppermute | solution.py:671
  187.1 38.2 %collective-permute-start.28 = (bf16[2,1024,512]{2,1,0:T(8,128)(2,1)}, bf16[2,1024,512]{2,1,0:T(8,128)(2,1)}, u32[]{:S(2)}, u32[]{:S(2)}) collective-permute-start(bf16[2,1024,512]{2,1,0:T(8,128)(2,1)} %relay.2), channel_id=1, source_target_pairs={{0,8},{8,0},{16,24},{24,16},{1,9},{9,1},{17,25},{25,17},{2,10},{10... | collective-permute-start | bytes 6291464 | tf_op jit(solution)/shard_map/ppermute | solution.py:559
  188.6 22.3 %collective-permute-start.32 = (bf16[32,3072]{1,0:T(8,128)(2,1)S(1)}, bf16[32,3072]{1,0:T(8,128)(2,1)S(1)}, u32[]{:S(2)}, u32[]{:S(2)}) collective-permute-start(bf16[32,3072]{1,0:T(8,128)(2,1)S(1)} %fusion.13), channel_id=1, source_target_pairs={{0,2},{1,3},{2,0},{3,1},{4,6},{5,7},{6,4},{7,5},{8,10},{9,11},{10,... | collective-permute-start | bytes 589832 | tf_op jit(solution)/shard_map/ppermute | solution.py:559
  193.2 43.5 %collective-permute-start.36 = (bf16[2,32,1536]{2,1,0:T(8,128)(2,1)}, bf16[2,32,1536]{2,1,0:T(8,128)(2,1)}, u32[]{:S(2)}, u32[]{:S(2)}) collective-permute-start(bf16[2,32,1536]{2,1,0:T(8,128)(2,1)} %fusion.14), channel_id=1, source_target_pairs={{0,4},{1,5},{2,6},{3,7},{4,0},{5,1},{6,2},{7,3},{8,12},{9,13},{10,... | collective-permute-start | bytes 589832 | tf_op jit(solution)/shard_map/ppermute | solution.py:559
  210.9 11.4 %collective-permute-start.34 = (bf16[2,4,32,3072]{3,2,1,0:T(8,128)(2,1)}, bf16[2,4,32,3072]{3,2,1,0:T(8,128)(2,1)}, u32[]{:S(2)}, u32[]{:S(2)}) collective-permute-start(bf16[2,4,32,3072]{3,2,1,0:T(8,128)(2,1)} %get-tuple-element.128), channel_id=1, source_target_pairs={{0,8},{8,0},{16,24},{24,16},{1,9},{9,1},{17,25},{25,17},{2,10},{10... | collective-permute-start | bytes 4718600 | tf_op jit(solution)/shard_map/ppermute | solution.py:559
  219.5 70.7 %collective-permute-start.38 = (bf16[1024,512]{1,0:T(8,128)(2,1)}, bf16[1024,512]{1,0:T(8,128)(2,1)S(1)}, u32[]{:S(2)}, u32[]{:S(2)}) collective-permute-start(bf16[1024,512]{1,0:T(8,128)(2,1)} %input_grad.6.g_ref.refs_1_), channel_id=1, source_target_pairs={{16,0},{24,8},{17,1},{25,9},{18,2},{26,10},{19,3},{27,11},{20,4},{... | collective-permute-start | bytes 3145736 | tf_op jit(solution)/shard_map/ppermute | solution.py:671
  224.8 26.7 %collective-permute-start.42 = (bf16[4,32,3072]{2,1,0:T(8,128)(2,1)}, bf16[4,32,3072]{2,1,0:T(8,128)(2,1)}, u32[]{:S(2)}, u32[]{:S(2)}) collective-permute-start(bf16[4,32,3072]{2,1,0:T(8,128)(2,1)} %fusion.1), channel_id=1, source_target_pairs={{0,1},{1,0},{2,3},{3,2},{4,5},{5,4},{6,7},{7,6},{8,9},{9,8},{10,11... | collective-permute-start | bytes 2359304 | tf_op jit(solution)/shard_map/ppermute | solution.py:559
  237.8 7.9 %collective-permute-start.40 = (bf16[32,1536]{1,0:T(8,128)(2,1)S(1)}, bf16[32,1536]{1,0:T(8,128)(2,1)}, u32[]{:S(2)}, u32[]{:S(2)}) collective-permute-start(bf16[32,1536]{1,0:T(8,128)(2,1)S(1)} %fusion.18), channel_id=1, source_target_pairs={{0,2},{1,3},{2,0},{3,1},{4,6},{5,7},{6,4},{7,5},{8,10},{9,11},{10,... | collective-permute-start | bytes 294920 | tf_op jit(solution)/shard_map/ppermute | solution.py:559
  237.9 11.9 %collective-permute-start.45 = (bf16[2,4,32,1664]{3,2,1,0:T(8,128)(2,1)}, bf16[2,4,32,1664]{3,2,1,0:T(8,128)(2,1)S(1)}, u32[]{:S(2)}, u32[]{:S(2)}) collective-permute-start(bf16[2,4,32,1664]{3,2,1,0:T(8,128)(2,1)} %get-tuple-element.137), channel_id=1, source_target_pairs={{0,8},{8,0},{16,24},{24,16},{1,9},{9,1},{17,25},{25,17},{2,10},{10... | collective-permute-start | bytes 2555912 | tf_op jit(solution)/shard_map/ppermute | solution.py:559
  244.3 45.9 %collective-permute-start.37 = (bf16[1024,512]{1,0:T(8,128)(2,1)}, bf16[1024,512]{1,0:T(8,128)(2,1)S(1)}, u32[]{:S(2)}, u32[]{:S(2)}) collective-permute-start(bf16[1024,512]{1,0:T(8,128)(2,1)} %input_grad.7.refs_0_), channel_id=1, source_target_pairs={{16,0},{24,8},{17,1},{25,9},{18,2},{26,10},{19,3},{27,11},{20,4},{... | collective-permute-start | bytes 3145736 | tf_op jit(solution)/shard_map/ppermute | solution.py:671
  246.9 43.2 %collective-permute-start.41 = (bf16[32,4608]{1,0:T(8,128)(2,1)S(1)}, bf16[32,4608]{1,0:T(8,128)(2,1)S(1)}, u32[]{:S(2)}, u32[]{:S(2)}) collective-permute-start(bf16[32,4608]{1,0:T(8,128)(2,1)S(1)} %pad_maximum_fusion.7), channel_id=1, source_target_pairs={{0,16},{8,24},{16,0},{24,8},{1,17},{9,25},{17,1},{25,9},{2,18},{10... | collective-permute-start | bytes 884744 | tf_op jit(solution)/shard_map/ppermute | solution.py:559
  249.9 12.0 %collective-permute-start.46 = (bf16[4,32,1664]{2,1,0:T(8,128)(2,1)S(1)}, bf16[4,32,1664]{2,1,0:T(8,128)(2,1)S(1)}, u32[]{:S(2)}, u32[]{:S(2)}) collective-permute-start(bf16[4,32,1664]{2,1,0:T(8,128)(2,1)S(1)} %fusion.5), channel_id=1, source_target_pairs={{0,1},{1,0},{2,3},{3,2},{4,5},{5,4},{6,7},{7,6},{8,9},{9,8},{10,11... | collective-permute-start | bytes 1277960 | tf_op jit(solution)/shard_map/ppermute | solution.py:559
  252.7 25.9 %collective-permute-start.43 = (bf16[2,32,3072]{2,1,0:T(8,128)(2,1)S(1)}, bf16[2,32,3072]{2,1,0:T(8,128)(2,1)S(1)}, u32[]{:S(2)}, u32[]{:S(2)}) collective-permute-start(bf16[2,32,3072]{2,1,0:T(8,128)(2,1)S(1)} %fusion.2), channel_id=1, source_target_pairs={{0,4},{1,5},{2,6},{3,7},{4,0},{5,1},{6,2},{7,3},{8,12},{9,13},{10,... | collective-permute-start | bytes 1179656 | tf_op jit(solution)/shard_map/ppermute | solution.py:559
  262.0 20.3 %collective-permute-start.47 = (bf16[2,32,1664]{2,1,0:T(8,128)(2,1)S(1)}, bf16[2,32,1664]{2,1,0:T(8,128)(2,1)S(1)}, u32[]{:S(2)}, u32[]{:S(2)}) collective-permute-start(bf16[2,32,1664]{2,1,0:T(8,128)(2,1)S(1)} %fusion.6), channel_id=1, source_target_pairs={{0,4},{1,5},{2,6},{3,7},{4,0},{5,1},{6,2},{7,3},{8,12},{9,13},{10,... | collective-permute-start | bytes 638984 | tf_op jit(solution)/shard_map/ppermute | solution.py:559
  279.8 7.7 %collective-permute-start.44 = (bf16[32,3072]{1,0:T(8,128)(2,1)S(1)}, bf16[32,3072]{1,0:T(8,128)(2,1)S(1)}, u32[]{:S(2)}, u32[]{:S(2)}) collective-permute-start(bf16[32,3072]{1,0:T(8,128)(2,1)S(1)} %fusion.8), channel_id=1, source_target_pairs={{0,2},{1,3},{2,0},{3,1},{4,6},{5,7},{6,4},{7,5},{8,10},{9,11},{10,... | collective-permute-start | bytes 589832 | tf_op jit(solution)/shard_map/ppermute | solution.py:559
  282.4 6.3 %collective-permute-start.48 = (bf16[32,1664]{1,0:T(8,128)(2,1)S(1)}, bf16[32,1664]{1,0:T(8,128)(2,1)S(1)}, u32[]{:S(2)}, u32[]{:S(2)}) collective-permute-start(bf16[32,1664]{1,0:T(8,128)(2,1)S(1)} %fusion.15), channel_id=1, source_target_pairs={{0,2},{1,3},{2,0},{3,1},{4,6},{5,7},{6,4},{7,5},{8,10},{9,11},{10,... | collective-permute-start | bytes 319496 | tf_op jit(solution)/shard_map/ppermute | solution.py:559
  289.8 7.9 %collective-permute-start.49 = (bf16[32,4736]{1,0:T(8,128)(2,1)S(1)}, bf16[32,4736]{1,0:T(8,128)(2,1)S(1)}, u32[]{:S(2)}, u32[]{:S(2)}) collective-permute-start(bf16[32,4736]{1,0:T(8,128)(2,1)S(1)} %pad_maximum_fusion.6), channel_id=1, source_target_pairs={{0,16},{8,24},{16,0},{24,8},{1,17},{9,25},{17,1},{25,9},{2,18},{10... | collective-permute-start | bytes 909320 | tf_op jit(solution)/shard_map/ppermute | solution.py:559
  295.4 12.1 %collective-permute-start.39 = (bf16[2,1024,512]{2,1,0:T(8,128)(2,1)}, bf16[2,1024,512]{2,1,0:T(8,128)(2,1)S(1)}, u32[]{:S(2)}, u32[]{:S(2)}) collective-permute-start(bf16[2,1024,512]{2,1,0:T(8,128)(2,1)} %relay.3), channel_id=1, source_target_pairs={{0,8},{8,0},{16,24},{24,16},{1,9},{9,1},{17,25},{25,17},{2,10},{10... | collective-permute-start | bytes 6291464 | tf_op jit(solution)/shard_map/ppermute | solution.py:559
  297.8 4.1 %collective-permute-start.50 = (bf16[32,9344]{1,0:T(8,128)(2,1)S(1)}, bf16[32,9344]{1,0:T(8,128)(2,1)}, u32[]{:S(2)}, u32[]{:S(2)}) collective-permute-start(bf16[32,9344]{1,0:T(8,128)(2,1)S(1)} %pad_maximum_fusion.2.own), channel_id=1, source_target_pairs={{0,8},{8,0},{16,24},{24,16},{1,9},{9,1},{17,25},{25,17},{2,10},{10... | collective-permute-start | bytes 1794056 | tf_op jit(solution)/shard_map/ppermute | solution.py:559
  (39 other events, 339.8 us)
